TPU v7x, 32 devices: a whole 2x2x4 slice. The times are simulated.
32 devices in a mesh: ka: 8 (over z, x), ba: 4 (over y, core).
Axes of the slice: x: 2, y: 2, z: 4, core: 2. Of those that a mesh axis runs over, the one named last changes fastest.
Arguments:
- density: float32 [2, 2048, 4096], P(None, 'ka', 'ba'), may hold values from -6 to 6
- h_bands: float32 [2, 2048, 4096], P(None, ('ka', 'ba')), may hold values from -0.75 to 0.75
- coupling: bfloat16 [16, 4, 128, 128], P('ka'), may hold values from -0.03125 to 0.03125
- donors: int32 [16, 4], P('ka'), may hold values from 0 to 15, as said below
- counts: int32 [16], P('ka'), may hold values from 2 to 4, as said below
Outputs:
- evolved: float32 [2, 2048, 4096], P(None, 'ka', 'ba')
Inputs may be any that keep to these rules, and one draw needn't show every extreme that they name: donors[t] holds 4 different tiles, each within 2 tiles of t in the cyclic order of the 16 tiles; donors[t, 0] = t. `counts`: some tile uses all 4 slots.
All inputs are finite; a program needn't handle non-finite values.
Results may differ from a plain program's by a relative error of at most 0.0013.
Values may be sent and summed in bfloat16 or wider, within the bound.
No kernel may reach another device: no remote copies, remote signals or barrier semaphores. Data moves between devices by JAX's collectives and lax.ppermute only.
A program may use at most 64 MiB of HBM per device.

v0:
```python
import functools

import jax
import jax.numpy as jnp
from jax import lax
from jax.experimental import pallas as pl
from jax.experimental.pallas import tpu as pltpu
from jax.sharding import PartitionSpec as P

NB = 64
TILE = 128
ND = 4
REACH = 2
LANE = 2 * NB
SPAN = (2 * REACH + 1) * TILE

step_size = 0.25
f32, bf16, i16, i32 = jnp.float32, jnp.bfloat16, jnp.int16, jnp.int32
SMEM = pl.BlockSpec(memory_space=pltpu.SMEM)
VMEM = pl.BlockSpec(memory_space=pltpu.VMEM)


def call(kernel, out, scratch=(), specs=None, n_in=0, flops=0, moved=0):
    return pl.pallas_call(
        kernel,
        out_shape=out,
        in_specs=specs if specs is not None else [SMEM] + [VMEM] * n_in,
        scratch_shapes=scratch,
        compiler_params=pltpu.CompilerParams(vmem_limit_bytes=48 * 2**20),
        cost_estimate=pl.CostEstimate(flops=flops, bytes_accessed=moved, transcendentals=0),
    )


def half_lanes(shape):
    return lax.broadcasted_iota(i32, shape, 1) < NB


def rows_of(real, imag):
    low = half_lanes(real.shape)
    even = jnp.where(low, real, pltpu.roll(imag, NB, 1))
    odd = jnp.where(low, pltpu.roll(real, NB, 1), imag)
    return even, odd


def parts_of(even, odd):
    low = half_lanes(even.shape)
    real = jnp.where(low, even, pltpu.roll(odd, NB, 1))
    imag = jnp.where(low, pltpu.roll(even, NB, 1), odd)
    return real, imag


def encode(values, peak):
    power = jnp.ceil(jnp.log2(jnp.maximum(peak, 1e-30)))
    scale = jnp.exp2(15.0 - power)
    codes = [jnp.clip(jnp.round(v * scale), -32767.0, 32767.0).astype(i32).astype(i16) for v in values]
    return codes, power


def decode_scale(power):
    return jnp.exp2(power.astype(i32).astype(f32) - 15.0)


def round_kernel(place, density, mine, other):
    x = place[0]
    width = density.shape[2] // 2
    for out, half in ((mine, x), (other, 1 - x)):
        for t in range(width // LANE):
            cols = pl.ds(pl.multiple_of(half * width + t * LANE, LANE), LANE)
            even, odd = rows_of(density[0, :, cols], density[1, :, cols])
            out[:, 2 * t * LANE : (2 * t + 1) * LANE] = even.astype(bf16)
            out[:, (2 * t + 1) * LANE : (2 * t + 2) * LANE] = odd.astype(bf16)


def split_kernel(place, density, *outs):
    j = place[1]
    rows = outs[0].shape[0]
    for k, out in enumerate(outs):
        at = pl.ds(pl.multiple_of((j ^ k) * rows, rows), rows)
        for t in range(density.shape[2] // LANE):
            cols = slice(t * LANE, (t + 1) * LANE)
            even, odd = rows_of(density[0, at, cols], density[1, at, cols])
            out[:, 2 * t * LANE : (2 * t + 1) * LANE] = even
            out[:, (2 * t + 1) * LANE : (2 * t + 2) * LANE] = odd


def matrices_from_rows(rows, out):
    count = out.shape[0]

    def body(m, carry):
        out[m] = rows[pl.ds(m, NB, stride=count), :]
        return carry

    lax.fori_loop(0, count, body, 0, unroll=4)


def hamilton_kernel(h, out, rows):
    count = out.shape[0]
    for t in range(h.shape[2] // LANE):
        cols = slice(t * LANE, (t + 1) * LANE)
        even, odd = rows_of(h[0, :, cols], h[1, :, cols])
        rows[2 * t * count : (2 * t + 1) * count, :] = even
        rows[(2 * t + 1) * count : (2 * t + 2) * count, :] = odd
    matrices_from_rows(rows, out)


def state_kernel(place, *refs):
    pieces, out, rows = refs[:-2], refs[-2], refs[-1]
    j = place[1]
    count = out.shape[0]
    own = pieces[0].shape[1] // LANE
    for k, piece in enumerate(pieces):
        for a in range(own):
            at = pl.multiple_of(((j ^ k) * own + a) * count, count)
            rows[pl.ds(at, count), :] = piece[:, a * LANE : (a + 1) * LANE]
    matrices_from_rows(rows, out)


def coupling_kernel(total, place, donors, counts, coupling, out):
    for t in range(coupling.shape[0]):
        for o in range(2 * REACH + 1):
            block = jnp.zeros((TILE, TILE), f32)
            for s in range(ND):
                shift = lax.rem(donors[t, s] - (place[2] + t) + REACH + total, total)
                used = jnp.logical_and(shift == o, s < counts[t])
                block = block - coupling[t, s].astype(f32) * jnp.where(used, 1.0, 0.0)
            out[t, :, o * TILE : (o + 1) * TILE] = block.astype(bf16)


def field(place, window, dense, dense_other, codes, outs, chunks):
    x, j = place[0], place[1]
    tiles = dense.shape[0]
    width = window.shape[1]
    ways = len(outs) // chunks
    g = x * (ways // 2) + j
    for t in range(2 * tiles):
        own = (t // tiles) == x
        weights = jnp.where(own, dense[t % tiles], dense_other[t % tiles])
        sigma = jnp.dot(weights, window[t * TILE : t * TILE + SPAN, :], preferred_element_type=f32)
        peak = jnp.max(jnp.abs(sigma), axis=1, keepdims=True)
        (code,), power = encode([sigma], peak)
        at = slice(t * TILE, (t + 1) * TILE)
        codes[at, :width] = code
        codes[at, width:] = jnp.broadcast_to(power, (TILE, LANE)).astype(i32).astype(i16)
    count = outs[0].shape[0]
    for c in range(chunks):
        for k in range(ways):
            at = pl.multiple_of(((g ^ k) * chunks + c) * count, count)
            outs[c * ways + k][...] = codes[pl.ds(at, count), :]


def field_one_kernel(chunks, place, mine, swap, straight, diag, dense, dense_other, *refs):
    outs, window, codes = refs[:-2], refs[-2], refs[-1]
    x = place[0]
    size = mine.shape[0]
    for ref, spot in ((mine, 1 + x), (swap, 2 - x), (straight, 3 - 3 * x), (diag, 3 * x)):
        window[pl.ds(pl.multiple_of(spot * size, size), size), :] = ref[...]
    field(place, window, dense, dense_other, codes, outs, chunks)


def field_two_kernel(chunks, place, dense, dense_other, *refs):
    states, outs, window, codes = refs[: 4 * chunks], refs[4 * chunks : -2], refs[-2], refs[-1]
    x, j = place[0], place[1]
    ways = len(outs) // chunks // 2
    for c in range(chunks):
        own, partner, near, far = states[4 * c : 4 * c + 4]
        count = own.shape[0] // ways
        for ref, spot in ((own, 1 + x), (partner, 2 - x), (near, 3 - 3 * x), (far, 3 * x)):
            for k in range(ways):
                at = ((spot * ways + (j ^ k)) * chunks + c) * count
                window[pl.ds(pl.multiple_of(at, count), count), :] = ref[k * count : (k + 1) * count, :]
    field(place, window, dense, dense_other, codes, outs, chunks)


def turned(rows):
    sign = jnp.where(half_lanes(rows.shape), 1.0, -1.0)
    return pltpu.roll(rows, NB, 1) * sign


def two_parts(values):
    high = values.astype(bf16)
    return high, (values - high.astype(f32)).astype(bf16)


def rate(h, s):
    h_high, h_low = two_parts(h)
    s_high, s_low = two_parts(s)
    ht_high, ht_low = two_parts(turned(h))
    st_high, st_low = two_parts(turned(s))
    left = jnp.concatenate(
        [jnp.concatenate([h_high, -s_high], 1), jnp.concatenate([h_low, -s_low], 1)], 0
    )
    right = jnp.concatenate(
        [
            jnp.concatenate([st_high, st_low], 1),
            jnp.concatenate([s_high, s_low], 1),
            jnp.concatenate([ht_high, ht_low], 1),
            jnp.concatenate([h_high, h_low], 1),
        ],
        0,
    )
    o = jnp.dot(left, right, preferred_element_type=f32)
    return (o[:NB, :LANE] + o[NB:, :LANE]) + (o[:NB, LANE:] + o[NB:, LANE:])


def unpack_field(place, pieces, rows):
    x, j = place[0], place[1]
    ways = len(pieces)
    g = x * (ways // 2) + j
    count = pieces[0].shape[0]
    own = pieces[0].shape[1] // LANE - 1
    for k, piece in enumerate(pieces):
        source = g ^ k
        first = ((source % (ways // 2)) * 2 + source // (ways // 2)) * own
        scale = decode_scale(piece[:, own * LANE :])
        for a in range(own):
            at = pl.multiple_of((first + a) * count, count)
            rows[pl.ds(at, count), :] = piece[:, a * LANE : (a + 1) * LANE].astype(i32).astype(f32) * scale


def first_kernel(place, h, s, *refs):
    ways = (len(refs) - 3) // 2
    pieces, middle, outs, rows, back = refs[:ways], refs[ways], refs[ways + 1 : -2], refs[-2], refs[-1]
    x, j = place[0], place[1]
    g = x * (ways // 2) + j
    count = middle.shape[0]
    unpack_field(place, pieces, rows)

    def body(m, carry):
        state = s[m]
        value = state + 0.5 * step_size * rate(h[m] + rows[pl.ds(m, NB, stride=count), :], state)
        middle[m] = value
        back[pl.ds(m, NB, stride=count), :] = value
        return carry

    lax.fori_loop(0, count, body, 0, unroll=4)
    own = outs[0].shape[1] // LANE
    for k, out in enumerate(outs):
        target = g ^ k
        first = ((target % (ways // 2)) * 2 + target // (ways // 2)) * own
        for a in range(own):
            at = pl.multiple_of((first + a) * count, count)
            out[:, a * LANE : (a + 1) * LANE] = back[pl.ds(at, count), :].astype(bf16)


def second_kernel(place, h, s, *refs):
    outs_n = (len(refs) - 2) // 3
    ways = 2 * outs_n
    pieces, outs, rows, back = refs[:ways], refs[ways:-2], refs[-2], refs[-1]
    j = place[1]
    count = outs[0].shape[0]
    unpack_field(place, pieces, rows)

    def body(m, carry):
        back[pl.ds(m, NB, stride=count), :] = rate(h[m] + rows[pl.ds(m, NB, stride=count), :], s[m])
        return carry

    lax.fori_loop(0, count, body, 0, unroll=4)
    own = outs[0].shape[1] // LANE - 1
    for k, out in enumerate(outs):
        first = (j ^ k) * own
        values = [back[pl.ds(pl.multiple_of((first + a) * count, count), count), :] for a in range(own)]
        peak = functools.reduce(jnp.maximum, [jnp.abs(v) for v in values])
        peak = jnp.max(peak, axis=1, keepdims=True)
        codes, power = encode(values, peak)
        for a in range(own):
            out[:, a * LANE : (a + 1) * LANE] = codes[a]
        out[:, own * LANE :] = jnp.broadcast_to(power, (count, LANE)).astype(i32).astype(i16)


def last_kernel(chunks, place, density, *refs):
    pieces, out = refs[:-1], refs[-1]
    j = place[1]
    ways = len(pieces) // chunks
    count = pieces[0].shape[0]
    own = pieces[0].shape[1] // LANE - 1
    for c in range(chunks):
        for k in range(ways):
            piece = pieces[c * ways + k]
            at = pl.ds(pl.multiple_of(((j ^ k) * chunks + c) * count, count), count)
            scale = decode_scale(piece[:, own * LANE :]) * step_size
            for t in range(own // 2):
                even = piece[:, 2 * t * LANE : (2 * t + 1) * LANE].astype(i32).astype(f32) * scale
                odd = piece[:, (2 * t + 1) * LANE : (2 * t + 2) * LANE].astype(i32).astype(f32) * scale
                real, imag = parts_of(even, odd)
                cols = slice(t * LANE, (t + 1) * LANE)
                out[0, at, cols] = density[0, at, cols] + real
                out[1, at, cols] = density[1, at, cols] + imag


def join_kernel(*refs):
    pieces, out = refs[:-1], refs[-1]
    count = pieces[0].shape[0]
    for k, piece in enumerate(pieces):
        out[k * count : (k + 1) * count, :] = piece[...]


def local(density, h_bands, coupling, donors, counts):
    nka, nb = lax.axis_size("ka"), lax.axis_size("ba")
    ways = 2 * nb
    i, j = lax.axis_index("ka"), lax.axis_index("ba")
    tiles, mom, pairs = coupling.shape[0], density.shape[1], density.shape[2]
    assert mom == tiles * TILE == REACH * TILE and nka % 2 == 0
    own = pairs // NB
    half = own // 2
    band = mom // nb
    chunks = 2 if band % 32 == 0 else 1
    count = band // chunks
    place = jnp.stack([i % 2, j, i * tiles]).astype(i32)

    def move(value, target):
        pairs_of = []
        for a in range(nka):
            for b in range(nb):
                ta, tb = target(a, b)
                pairs_of.append((a * nb + b, (ta % nka) * nb + tb))
        return lax.ppermute(value, ("ka", "ba"), pairs_of)

    def in_group(value, k):
        def target(a, b):
            t = ((a % 2) * nb + b) ^ k
            return a - a % 2 + t // nb, t % nb
        return value if k == 0 else move(value, target)

    def across(value):
        return move(value, lambda a, b: (a ^ 1, b))

    def along(value, odd, even):
        return move(value, lambda a, b: (a + (odd if a % 2 else even), b))

    shape = jax.ShapeDtypeStruct
    mine, other = call(round_kernel, [shape((mom, half * LANE), bf16)] * 2, n_in=1)(place, density)
    straight = along(mine, 2, -2)
    diag = along(other, 1, -1)
    swap = across(other)
    dense = call(
        functools.partial(coupling_kernel, nka * tiles),
        shape((tiles, TILE, SPAN), bf16),
        specs=[SMEM, SMEM, SMEM, VMEM],
    )(place, donors, counts, coupling)
    dense_other = across(dense)
    sent = call(split_kernel, [shape((band, own * LANE), f32)] * nb, n_in=1)(place, density)
    states = [in_group(v, k) for k, v in enumerate(sent)]
    matrices = shape((band, NB, LANE), f32)
    rows = pltpu.VMEM((band * NB, LANE), f32)
    state = call(state_kernel, matrices, [rows], n_in=nb)(place, *states)
    hamilton = call(hamilton_kernel, matrices, [rows], specs=[VMEM])(h_bands)

    window = pltpu.VMEM((4 * mom, half * LANE), bf16)
    codes = pltpu.VMEM((2 * mom, half * LANE + LANE), i16)
    pieces = [shape((count, half * LANE + LANE), i16)] * (ways * chunks)
    chunk_rows = pltpu.VMEM((count * NB, LANE), f32)
    chunk_shape = shape((count, NB, LANE), f32)

    fields = call(
        functools.partial(field_one_kernel, chunks), pieces, [window, codes], n_in=6
    )(place, mine, swap, straight, diag, dense, dense_other)

    middles, parts = [], []
    for c in range(chunks):
        got = [in_group(fields[c * ways + k], k) for k in range(ways)]
        at = slice(c * count, (c + 1) * count)
        middle, *outs = call(
            first_kernel,
            [chunk_shape] + [shape((count, half * LANE), bf16)] * ways,
            [chunk_rows, chunk_rows],
            n_in=2 + ways,
        )(place, hamilton[at], state[at], *got)
        middles.append(middle)
        back = [in_group(v, k) for k, v in enumerate(outs)]
        joined = shape((nb * count, half * LANE), bf16)
        own_part = call(join_kernel, joined, specs=[VMEM] * nb)(*back[:nb])
        partner = call(join_kernel, joined, specs=[VMEM] * nb)(*back[nb:])
        parts += [own_part, partner, along(own_part, 2, -2), along(partner, -2, 2)]

    fields = call(
        functools.partial(field_two_kernel, chunks), pieces, [window, codes], n_in=2 + 4 * chunks
    )(place, dense, dense_other, *parts)

    rates = []
    for c in range(chunks):
        got = [in_group(fields[c * ways + k], k) for k in range(ways)]
        outs = call(
            second_kernel,
            [shape((count, own * LANE + LANE), i16)] * nb,
            [chunk_rows, chunk_rows],
            n_in=2 + ways,
        )(place, hamilton[c * count : (c + 1) * count], middles[c], *got)
        rates += [in_group(v, k) for k, v in enumerate(outs)]
    return call(
        functools.partial(last_kernel, chunks), shape(density.shape, f32), n_in=1 + nb * chunks
    )(place, density, *rates)


def solution(mesh):
    placed = (
        P(None, "ka", "ba"),
        P(None, ("ka", "ba"), None),
        P("ka", None, None, None),
        P("ka", None),
        P("ka"),
    )
    return jax.shard_map(
        local, mesh=mesh, in_specs=placed, out_specs=P(None, "ka", "ba"), check_vma=False
    )
```

profile of v0, /device:TPU:0, one launch (start us, length us, event | category | flops | bytes accessed | tf_op | source)
XLA Modules:
  0.0 156.2 jit_solution(5144913624933890644)
XLA Ops:
  0.1 1.6 %copy-done = f32[2,256,1024]{2,1,0:T(8,128)S(1)} copy-done((f32[2,256,1024]{2,1,0:T(8,128)S(1)}, f32[2,256,1024]{2,1,0:T(8,128)}, u32[]{:S(2)}) %copy-start) | copy-done | bytes 2097176
  1.7 1.1 shard_map.58
  2.8 5.1 %collective-permute-start.4 = (bf16[256,1024]{1,0:T(8,128)(2,1)S(1)}, bf16[256,1024]{1,0:T(8,128)(2,1)S(1)}, u32[]{:S(2)}, u32[]{:S(2)}) collective-permute-start(bf16[256,1024]{1,0:T(8,128)(2,1)S(1)} %get-tuple-element.73.mine), channel_id=1, source_target_pairs={{0,24},{1,25},{2,26},{3,27},{4,12},{5,13},{6,14},{7,15},{8,0},{9,1... | collective-permute-start | bytes 1572872 | tf_op jit(solution)/shard_map/ppermute | solution.py:316
  9.8 1.9 %collective-permute-start.5 = (bf16[256,1024]{1,0:T(8,128)(2,1)S(1)}, bf16[256,1024]{1,0:T(8,128)(2,1)S(1)}, u32[]{:S(2)}, u32[]{:S(2)}) collective-permute-start(bf16[256,1024]{1,0:T(8,128)(2,1)S(1)} %get-tuple-element.74), channel_id=1, source_target_pairs={{0,28},{1,29},{2,30},{3,31},{4,8},{5,9},{6,10},{7,11},{8,4},{9,5},... | collective-permute-start | bytes 1572872 | tf_op jit(solution)/shard_map/ppermute | solution.py:316
  12.3 1.2 shard_map.56
  13.5 15.6 %collective-permute-done.6.dense_other = bf16[2,128,640]{2,1,0:T(8,128)(2,1)S(1)} collective-permute-done((bf16[2,128,640]{2,1,0:T(8,128)(2,1)S(1)}, bf16[2,128,640]{2,1,0:T(8,128)(2,1)S(1)}, u32[]{:S(2)}, u32[]{:S(2)}) %collective-permute-start.6) | collective-permute-done | bytes 327712 | tf_op jit(solution)/shard_map/ppermute | solution.py:316
  29.1 1.5 collective-permute-start.1
  30.6 1.4 collective-permute-done.5.diag
  32.1 9.3 %collective-permute-done.3.swap = bf16[256,1024]{1,0:T(8,128)(2,1)S(1)} collective-permute-done((bf16[256,1024]{1,0:T(8,128)(2,1)S(1)}, bf16[256,1024]{1,0:T(8,128)(2,1)S(1)}, u32[]{:S(2)}, u32[]{:S(2)}) %collective-permute-start.3) | collective-permute-done | bytes 524320 | tf_op jit(solution)/shard_map/ppermute | solution.py:316
  41.4 2.0 %shard_map.60 = (s16[32,1152]{1,0:T(8,128)(2,1)S(1)}, s16[32,1152]{1,0:T(8,128)(2,1)S(1)}, s16[32,1152]{1,0:T(8,128)(2,1)S(1)}, s16[32,1152]{1,0:T(8,128)(2,1)S(...) custom-call(s32[3]{0:T(128)S(1)} %pad_add_fusion.place, ...), custom_call_target="tpu_custom_call" | custom-call | tf_op jit(solution)/shard_map/pallas_call | solution.py:354
  43.5 1.6 %collective-permute-start.8 = (s16[32,1152]{1,0:T(8,128)(2,1)S(1)}, s16[32,1152]{1,0:T(8,128)(2,1)S(1)}, u32[]{:S(2)}, u32[]{:S(2)}) collective-permute-start(s16[32,1152]{1,0:T(8,128)(2,1)S(1)} %get-tuple-element.77), channel_id=1, source_target_pairs={{0,2},{1,3},{2,0},{3,1},{4,6},{5,7},{6,4},{7,5},{8,10},{9,11},{10,... | collective-permute-start | bytes 221192 | tf_op jit(solution)/shard_map/ppermute | solution.py:316
  45.8 2.1 %shard_map.55 = f32[64,64,128]{2,1,0:T(8,128)S(1)} custom-call(f32[2,64,4096]{2,1,0:T(8,128)S(1)} %copy-done.2), custom_call_target="tpu_custom_call" | custom-call | tf_op jit(solution)/shard_map/pallas_call | solution.py:346
  47.8 2.2 %collective-permute-done.2.refs_3_ = f32[64,2048]{1,0:T(8,128)S(1)} collective-permute-done((f32[64,2048]{1,0:T(8,128)S(1)}, f32[64,2048]{1,0:T(8,128)S(1)}, u32[]{:S(2)}, u32[]{:S(2)}) %collective-permute-start.2) | collective-permute-done | bytes 524320 | tf_op jit(solution)/shard_map/ppermute | solution.py:316
  50.1 1.9 %collective-permute-start.25 = (s16[32,1152]{1,0:T(8,128)(2,1)S(1)}, s16[32,1152]{1,0:T(8,128)(2,1)S(1)}, u32[]{:S(2)}, u32[]{:S(2)}) collective-permute-start(s16[32,1152]{1,0:T(8,128)(2,1)S(1)} %get-tuple-element.95), channel_id=1, source_target_pairs={{0,3},{1,2},{2,1},{3,0},{4,7},{5,6},{6,5},{7,4},{8,11},{9,10},{10,... | collective-permute-start | bytes 221192 | tf_op jit(solution)/shard_map/ppermute | solution.py:316
  52.0 2.5 %collective-permute-start.26 = (s16[32,1152]{1,0:T(8,128)(2,1)S(1)}, s16[32,1152]{1,0:T(8,128)(2,1)S(1)}, u32[]{:S(2)}, u32[]{:S(2)}) collective-permute-start(s16[32,1152]{1,0:T(8,128)(2,1)S(1)} %get-tuple-element.96), channel_id=1, source_target_pairs={{0,4},{1,5},{2,6},{3,7},{4,0},{5,1},{6,2},{7,3},{8,12},{9,13},{10,... | collective-permute-start | bytes 221192 | tf_op jit(solution)/shard_map/ppermute | solution.py:316
  54.5 1.2 collective-permute-start.28
  55.7 1.2 collective-permute-start.29
  57.2 2.2 %shard_map.57 = f32[64,64,128]{2,1,0:T(8,128)S(1)} custom-call(s32[3]{0:T(128)S(1)} %pad_add_fusion.place, f32[64,2048]{1,0:T(8,128)S(1)} %get-tuple-element.69.refs_0_, f32[64,2048]{1,0:T(8,128)S(1)} %collective-permute-done.refs_1_, f32[64,2048]{1,0:T(8,128)S(1)} %collective-permute-done.1.refs_2_, f32[64,2048]{1,0:T(8,128)S(1)} %collective-permute-done.2.refs_3_), custom_call_target="tpu_custom_call" | custom-call | tf_op jit(solution)/shard_map/pallas_call | solution.py:345
  60.2 1.2 collective-permute-start.10
  62.2 2.1 %collective-permute-start.12 = (s16[32,1152]{1,0:T(8,128)(2,1)S(1)}, s16[32,1152]{1,0:T(8,128)(2,1)S(1)}, u32[]{:S(2)}, u32[]{:S(2)}) collective-permute-start(s16[32,1152]{1,0:T(8,128)(2,1)S(1)} %get-tuple-element.81), channel_id=1, source_target_pairs={{0,6},{1,7},{2,4},{3,5},{4,2},{5,3},{6,0},{7,1},{8,14},{9,15},{10,... | collective-permute-start | bytes 221192 | tf_op jit(solution)/shard_map/ppermute | solution.py:316
  64.8 3.9 %shard_map.64 = (f32[32,64,128]{2,1,0:T(8,128)S(1)}, bf16[32,1024]{1,0:T(8,128)(2,1)S(1)}, bf16[32,1024]{1,0:T(8,128)(2,1)S(1)}, bf16[32,1024]{1,0:T(8,128)(2,1)...) custom-call(s32[3]{0:T(128)S(1)} %pad_add_fusion.place, ...), custom_call_target="tpu_custom_call" | custom-call | tf_op jit(solution)/shard_map/pallas_call | solution.py:362
  68.7 1.3 collective-permute-start.33
  70.7 3.9 %shard_map.61 = (f32[32,64,128]{2,1,0:T(8,128)S(1)}, bf16[32,1024]{1,0:T(8,128)(2,1)S(1)}, bf16[32,1024]{1,0:T(8,128)(2,1)S(1)}, bf16[32,1024]{1,0:T(8,128)(2,1)...) custom-call(s32[3]{0:T(128)S(1)} %pad_add_fusion.place, ...), custom_call_target="tpu_custom_call" | custom-call | tf_op jit(solution)/shard_map/pallas_call | solution.py:362
  74.9 1.5 collective-permute-start.15
  76.6 1.2 collective-permute-start.17
  78.4 2.0 %collective-permute-start.19 = (bf16[32,1024]{1,0:T(8,128)(2,1)S(1)}, bf16[32,1024]{1,0:T(8,128)(2,1)S(1)}, u32[]{:S(2)}, u32[]{:S(2)}) collective-permute-start(bf16[32,1024]{1,0:T(8,128)(2,1)S(1)} %get-tuple-element.90), channel_id=1, source_target_pairs={{0,6},{1,7},{2,4},{3,5},{4,2},{5,3},{6,0},{7,1},{8,14},{9,15},{10,... | collective-permute-start | bytes 196616 | tf_op jit(solution)/shard_map/ppermute | solution.py:316
  81.9 1.7 %collective-permute-start.35 = (bf16[32,1024]{1,0:T(8,128)(2,1)S(1)}, bf16[32,1024]{1,0:T(8,128)(2,1)S(1)}, u32[]{:S(2)}, u32[]{:S(2)}) collective-permute-start(bf16[32,1024]{1,0:T(8,128)(2,1)S(1)} %get-tuple-element.106), channel_id=1, source_target_pairs={{0,6},{1,7},{2,4},{3,5},{4,2},{5,3},{6,0},{7,1},{8,14},{9,15},{10,... | collective-permute-start | bytes 196616 | tf_op jit(solution)/shard_map/ppermute | solution.py:316
  83.6 1.1 collective-permute-start.36
  86.4 1.3 collective-permute-done.35.refs_2_
  89.1 2.4 %collective-permute-start.21 = (bf16[128,1024]{1,0:T(8,128)(2,1)S(1)}, bf16[128,1024]{1,0:T(8,128)(2,1)S(1)}, u32[]{:S(2)}, u32[]{:S(2)}) collective-permute-start(bf16[128,1024]{1,0:T(8,128)(2,1)S(1)} %shard_map.62.refs_0_), channel_id=1, source_target_pairs={{0,24},{1,25},{2,26},{3,27},{4,12},{5,13},{6,14},{7,15},{8,0},{9,1... | collective-permute-start | bytes 786440 | tf_op jit(solution)/shard_map/ppermute | solution.py:316
  91.8 3.9 %collective-permute-start.37 = (bf16[128,1024]{1,0:T(8,128)(2,1)S(1)}, bf16[128,1024]{1,0:T(8,128)(2,1)S(1)}, u32[]{:S(2)}, u32[]{:S(2)}) collective-permute-start(bf16[128,1024]{1,0:T(8,128)(2,1)S(1)} %shard_map.65.refs_4_), channel_id=1, source_target_pairs={{0,24},{1,25},{2,26},{3,27},{4,12},{5,13},{6,14},{7,15},{8,0},{9,1... | collective-permute-start | bytes 786440 | tf_op jit(solution)/shard_map/ppermute | solution.py:316
  95.7 3.0 %collective-permute-done.22.refs_3_ = bf16[128,1024]{1,0:T(8,128)(2,1)S(1)} collective-permute-done((bf16[128,1024]{1,0:T(8,128)(2,1)S(1)}, bf16[128,1024]{1,0:T(8,128)(2,1)S(1)}, u32[]{:S(2)}, u32[]{:S(2)}) %collective-permute-start.22) | collective-permute-done | bytes 262176 | tf_op jit(solution)/shard_map/ppermute | solution.py:316
  98.7 5.7 %collective-permute-done.21.refs_2_ = bf16[128,1024]{1,0:T(8,128)(2,1)S(1)} collective-permute-done((bf16[128,1024]{1,0:T(8,128)(2,1)S(1)}, bf16[128,1024]{1,0:T(8,128)(2,1)S(1)}, u32[]{:S(2)}, u32[]{:S(2)}) %collective-permute-start.21) | collective-permute-done | bytes 262176 | tf_op jit(solution)/shard_map/ppermute | solution.py:316
  104.4 5.6 %collective-permute-done.38.refs_7_ = bf16[128,1024]{1,0:T(8,128)(2,1)S(1)} collective-permute-done((bf16[128,1024]{1,0:T(8,128)(2,1)S(1)}, bf16[128,1024]{1,0:T(8,128)(2,1)S(1)}, u32[]{:S(2)}, u32[]{:S(2)}) %collective-permute-start.38) | collective-permute-done | bytes 262176 | tf_op jit(solution)/shard_map/ppermute | solution.py:316
  110.0 4.2 %collective-permute-done.37.refs_6_ = bf16[128,1024]{1,0:T(8,128)(2,1)S(1)} collective-permute-done((bf16[128,1024]{1,0:T(8,128)(2,1)S(1)}, bf16[128,1024]{1,0:T(8,128)(2,1)S(1)}, u32[]{:S(2)}, u32[]{:S(2)}) %collective-permute-start.37) | collective-permute-done | bytes 262176 | tf_op jit(solution)/shard_map/ppermute | solution.py:316
  114.2 2.0 %shard_map.67 = (s16[32,1152]{1,0:T(8,128)(2,1)S(1)}, s16[32,1152]{1,0:T(8,128)(2,1)S(1)}, s16[32,1152]{1,0:T(8,128)(2,1)S(1)}, s16[32,1152]{1,0:T(8,128)(2,1)S(...) custom-call(s32[3]{0:T(128)S(1)} %pad_add_fusion.place, ...), custom_call_target="tpu_custom_call" | custom-call | tf_op jit(solution)/shard_map/pallas_call | solution.py:375
  117.0 1.1 collective-permute-start.51
  121.4 1.1 collective-permute-start.55
  124.8 1.7 %collective-permute-done.54.refs_6_ = s16[32,1152]{1,0:T(8,128)(2,1)S(1)} collective-permute-done((s16[32,1152]{1,0:T(8,128)(2,1)S(1)}, s16[32,1152]{1,0:T(8,128)(2,1)S(1)}, u32[]{:S(2)}, u32[]{:S(2)}) %collective-permute-start.54) | collective-permute-done | bytes 73760 | tf_op jit(solution)/shard_map/ppermute | solution.py:316
  127.1 4.0 %shard_map.69 = (s16[32,2176]{1,0:T(8,128)(2,1)S(1)}, s16[32,2176]{1,0:T(8,128)(2,1)S(1)}, s16[32,2176]{1,0:T(8,128)(2,1)S(1)}, s16[32,2176]{1,0:T(8,128)(2,1)S(1)}) custom-call(s32[3]{0:T(128)S(1)} %pad_add_fusion.place, f32[32,64,128]{2,1,0:T(8,128)S(1)} %get-tuple-element.135.h, f32[32,64,128]{2,1,0:T(8,128)S(1)} %get-tuple-element.120.s, ...), custom_call_target="tpu_custom_call" | custom-call | tf_op jit(solution)/shard_map/pallas_call | solution.py:382
  133.1 1.8 %collective-permute-start.44 = (s16[32,1152]{1,0:T(8,128)(2,1)S(1)}, s16[32,1152]{1,0:T(8,128)(2,1)S(1)}, u32[]{:S(2)}, u32[]{:S(2)}) collective-permute-start(s16[32,1152]{1,0:T(8,128)(2,1)S(1)} %get-tuple-element.114), channel_id=1, source_target_pairs={{0,6},{1,7},{2,4},{3,5},{4,2},{5,3},{6,0},{7,1},{8,14},{9,15},{10,... | collective-permute-start | bytes 221192 | tf_op jit(solution)/shard_map/ppermute | solution.py:316
  136.4 1.3 collective-permute-start.57
  137.7 1.3 collective-permute-start.58
  139.0 1.4 collective-permute-done.44.refs_6_
  141.2 4.0 %shard_map.68 = (s16[32,2176]{1,0:T(8,128)(2,1)S(1)}, s16[32,2176]{1,0:T(8,128)(2,1)S(1)}, s16[32,2176]{1,0:T(8,128)(2,1)S(1)}, s16[32,2176]{1,0:T(8,128)(2,1)S(1)}) custom-call(s32[3]{0:T(128)S(1)} %pad_add_fusion.place, f32[32,64,128]{2,1,0:T(8,128)S(1)} %get-tuple-element.136.h, f32[32,64,128]{2,1,0:T(8,128)S(1)} %get-tuple-element.83.s, ...), custom_call_target="tpu_custom_call" | custom-call | tf_op jit(solution)/shard_map/pallas_call | solution.py:382
  147.3 4.7 %collective-permute-done.47.refs_2_ = s16[32,2176]{1,0:T(8,128)(2,1)S(1)} collective-permute-done((s16[32,2176]{1,0:T(8,128)(2,1)S(1)}, s16[32,2176]{1,0:T(8,128)(2,1)S(1)}, u32[]{:S(2)}, u32[]{:S(2)}) %collective-permute-start.47) | collective-permute-done | bytes 139296 | tf_op jit(solution)/shard_map/ppermute | solution.py:316
  152.0 1.7 %collective-permute-done.48.refs_3_ = s16[32,2176]{1,0:T(8,128)(2,1)S(1)} collective-permute-done((s16[32,2176]{1,0:T(8,128)(2,1)S(1)}, s16[32,2176]{1,0:T(8,128)(2,1)S(1)}, u32[]{:S(2)}, u32[]{:S(2)}) %collective-permute-start.48) | collective-permute-done | bytes 139296 | tf_op jit(solution)/shard_map/ppermute | solution.py:316
  153.7 2.5 %shard_map.70 = f32[2,256,1024]{2,1,0:T(8,128)} custom-call(s32[3]{0:T(128)S(1)} %pad_add_fusion.place, f32[2,256,1024]{2,1,0:T(8,128)S(1)} %copy-done.1, s16[32,2176]{1,0:T(8,128)(2,1)S(1)} %get-tuple-element.116.refs_0_, s16[32,2176]{1,0:T(8,128)(2,1)S(1)} %collective-permute-done.46.refs_1_, s16[32,2176]{1,0:T(8,128)(2,1)S(1)} %collective-permute-done.47.refs_2_, ...), custom_call_target="tpu_custom_call" | custom-call | tf_op jit(solution)/shard_map/pallas_call | solution.py:389
  (101 shorter events, 25.7 us)
Async XLA Ops:
  2.8 27.9 %collective-permute-start.4 = (bf16[256,1024]{1,0:T(8,128)(2,1)S(1)}, bf16[256,1024]{1,0:T(8,128)(2,1)S(1)}, u32[]{:S(2)}, u32[]{:S(2)}) collective-permute-start(bf16[256,1024]{1,0:T(8,128)(2,1)S(1)} %get-tuple-element.73.mine), channel_id=1, source_target_pairs={{0,24},{1,25},{2,26},{3,27},{4,12},{5,13},{6,14},{7,15},{8,0},{9,1... | collective-permute-start | bytes 1572872 | tf_op jit(solution)/shard_map/ppermute | solution.py:316
  9.7 19.4 %collective-permute-start.6 = (bf16[2,128,640]{2,1,0:T(8,128)(2,1)S(1)}, bf16[2,128,640]{2,1,0:T(8,128)(2,1)S(1)}, u32[]{:S(2)}, u32[]{:S(2)}) collective-permute-start(bf16[2,128,640]{2,1,0:T(8,128)(2,1)S(1)} %shard_map.59.dense), channel_id=1, source_target_pairs={{0,4},{1,5},{2,6},{3,7},{4,0},{5,1},{6,2},{7,3},{8,12},{9,13},{10,... | collective-permute-start | bytes 983048 | tf_op jit(solution)/shard_map/ppermute | solution.py:316
  9.8 22.3 %collective-permute-start.5 = (bf16[256,1024]{1,0:T(8,128)(2,1)S(1)}, bf16[256,1024]{1,0:T(8,128)(2,1)S(1)}, u32[]{:S(2)}, u32[]{:S(2)}) collective-permute-start(bf16[256,1024]{1,0:T(8,128)(2,1)S(1)} %get-tuple-element.74), channel_id=1, source_target_pairs={{0,28},{1,29},{2,30},{3,31},{4,8},{5,9},{6,10},{7,11},{8,4},{9,5},... | collective-permute-start | bytes 1572872 | tf_op jit(solution)/shard_map/ppermute | solution.py:316
  11.7 29.7 %collective-permute-start.3 = (bf16[256,1024]{1,0:T(8,128)(2,1)S(1)}, bf16[256,1024]{1,0:T(8,128)(2,1)S(1)}, u32[]{:S(2)}, u32[]{:S(2)}) collective-permute-start(bf16[256,1024]{1,0:T(8,128)(2,1)S(1)} %get-tuple-element.74), channel_id=1, source_target_pairs={{0,4},{1,5},{2,6},{3,7},{4,0},{5,1},{6,2},{7,3},{8,12},{9,13},{10,... | collective-permute-start | bytes 1572872 | tf_op jit(solution)/shard_map/ppermute | solution.py:316
  13.4 31.7 %collective-permute-start = (f32[64,2048]{1,0:T(8,128)S(1)}, f32[64,2048]{1,0:T(8,128)S(1)}, u32[]{:S(2)}, u32[]{:S(2)}) collective-permute-start(f32[64,2048]{1,0:T(8,128)S(1)} %get-tuple-element.70), channel_id=1, source_target_pairs={{0,1},{1,0},{2,3},{3,2},{4,5},{5,4},{6,7},{7,6},{8,9},{9,8},{10,11... | collective-permute-start | bytes 1572872 | tf_op jit(solution)/shard_map/ppermute | solution.py:316
  29.1 16.1 %collective-permute-start.1 = (f32[64,2048]{1,0:T(8,128)S(1)}, f32[64,2048]{1,0:T(8,128)S(1)}, u32[]{:S(2)}, u32[]{:S(2)}) collective-permute-start(f32[64,2048]{1,0:T(8,128)S(1)} %get-tuple-element.71), channel_id=1, source_target_pairs={{0,2},{1,3},{2,0},{3,1},{4,6},{5,7},{6,4},{7,5},{8,10},{9,11},{10,... | collective-permute-start | bytes 1572872 | tf_op jit(solution)/shard_map/ppermute | solution.py:316
  30.6 19.4 %collective-permute-start.2 = (f32[64,2048]{1,0:T(8,128)S(1)}, f32[64,2048]{1,0:T(8,128)S(1)}, u32[]{:S(2)}, u32[]{:S(2)}) collective-permute-start(f32[64,2048]{1,0:T(8,128)S(1)} %get-tuple-element.72), channel_id=1, source_target_pairs={{0,3},{1,2},{2,1},{3,0},{4,7},{5,6},{6,5},{7,4},{8,11},{9,10},{10,... | collective-permute-start | bytes 1572872 | tf_op jit(solution)/shard_map/ppermute | solution.py:316
  43.4 8.6 %collective-permute-start.7 = (s16[32,1152]{1,0:T(8,128)(2,1)S(1)}, s16[32,1152]{1,0:T(8,128)(2,1)S(1)}, u32[]{:S(2)}, u32[]{:S(2)}) collective-permute-start(s16[32,1152]{1,0:T(8,128)(2,1)S(1)} %get-tuple-element.76), channel_id=1, source_target_pairs={{0,1},{1,0},{2,3},{3,2},{4,5},{5,4},{6,7},{7,6},{8,9},{9,8},{10,11... | collective-permute-start | bytes 221192 | tf_op jit(solution)/shard_map/ppermute | solution.py:316
  43.5 11.0 %collective-permute-start.8 = (s16[32,1152]{1,0:T(8,128)(2,1)S(1)}, s16[32,1152]{1,0:T(8,128)(2,1)S(1)}, u32[]{:S(2)}, u32[]{:S(2)}) collective-permute-start(s16[32,1152]{1,0:T(8,128)(2,1)S(1)} %get-tuple-element.77), channel_id=1, source_target_pairs={{0,2},{1,3},{2,0},{3,1},{4,6},{5,7},{6,4},{7,5},{8,10},{9,11},{10,... | collective-permute-start | bytes 221192 | tf_op jit(solution)/shard_map/ppermute | solution.py:316
  45.1 9.4 %collective-permute-start.23 = (s16[32,1152]{1,0:T(8,128)(2,1)S(1)}, s16[32,1152]{1,0:T(8,128)(2,1)S(1)}, u32[]{:S(2)}, u32[]{:S(2)}) collective-permute-start(s16[32,1152]{1,0:T(8,128)(2,1)S(1)} %get-tuple-element.93), channel_id=1, source_target_pairs={{0,1},{1,0},{2,3},{3,2},{4,5},{5,4},{6,7},{7,6},{8,9},{9,8},{10,11... | collective-permute-start | bytes 221192 | tf_op jit(solution)/shard_map/ppermute | solution.py:316
  45.2 10.4 %collective-permute-start.24 = (s16[32,1152]{1,0:T(8,128)(2,1)S(1)}, s16[32,1152]{1,0:T(8,128)(2,1)S(1)}, u32[]{:S(2)}, u32[]{:S(2)}) collective-permute-start(s16[32,1152]{1,0:T(8,128)(2,1)S(1)} %get-tuple-element.94), channel_id=1, source_target_pairs={{0,2},{1,3},{2,0},{3,1},{4,6},{5,7},{6,4},{7,5},{8,10},{9,11},{10,... | collective-permute-start | bytes 221192 | tf_op jit(solution)/shard_map/ppermute | solution.py:316
  50.1 9.2 %collective-permute-start.25 = (s16[32,1152]{1,0:T(8,128)(2,1)S(1)}, s16[32,1152]{1,0:T(8,128)(2,1)S(1)}, u32[]{:S(2)}, u32[]{:S(2)}) collective-permute-start(s16[32,1152]{1,0:T(8,128)(2,1)S(1)} %get-tuple-element.95), channel_id=1, source_target_pairs={{0,3},{1,2},{2,1},{3,0},{4,7},{5,6},{6,5},{7,4},{8,11},{9,10},{10,... | collective-permute-start | bytes 221192 | tf_op jit(solution)/shard_map/ppermute | solution.py:316
  52.0 8.3 %collective-permute-start.26 = (s16[32,1152]{1,0:T(8,128)(2,1)S(1)}, s16[32,1152]{1,0:T(8,128)(2,1)S(1)}, u32[]{:S(2)}, u32[]{:S(2)}) collective-permute-start(s16[32,1152]{1,0:T(8,128)(2,1)S(1)} %get-tuple-element.96), channel_id=1, source_target_pairs={{0,4},{1,5},{2,6},{3,7},{4,0},{5,1},{6,2},{7,3},{8,12},{9,13},{10,... | collective-permute-start | bytes 221192 | tf_op jit(solution)/shard_map/ppermute | solution.py:316
  54.5 7.0 %collective-permute-start.27 = (s16[32,1152]{1,0:T(8,128)(2,1)S(1)}, s16[32,1152]{1,0:T(8,128)(2,1)S(1)}, u32[]{:S(2)}, u32[]{:S(2)}) collective-permute-start(s16[32,1152]{1,0:T(8,128)(2,1)S(1)} %get-tuple-element.97), channel_id=1, source_target_pairs={{0,5},{1,4},{2,7},{3,6},{4,1},{5,0},{6,3},{7,2},{8,13},{9,12},{10,... | collective-permute-start | bytes 221192 | tf_op jit(solution)/shard_map/ppermute | solution.py:316
  54.5 7.7 %collective-permute-start.28 = (s16[32,1152]{1,0:T(8,128)(2,1)S(1)}, s16[32,1152]{1,0:T(8,128)(2,1)S(1)}, u32[]{:S(2)}, u32[]{:S(2)}) collective-permute-start(s16[32,1152]{1,0:T(8,128)(2,1)S(1)} %get-tuple-element.98), channel_id=1, source_target_pairs={{0,6},{1,7},{2,4},{3,5},{4,2},{5,3},{6,0},{7,1},{8,14},{9,15},{10,... | collective-permute-start | bytes 221192 | tf_op jit(solution)/shard_map/ppermute | solution.py:316
  55.7 8.6 %collective-permute-start.29 = (s16[32,1152]{1,0:T(8,128)(2,1)S(1)}, s16[32,1152]{1,0:T(8,128)(2,1)S(1)}, u32[]{:S(2)}, u32[]{:S(2)}) collective-permute-start(s16[32,1152]{1,0:T(8,128)(2,1)S(1)} %get-tuple-element.99), channel_id=1, source_target_pairs={{0,7},{1,6},{2,5},{3,4},{4,3},{5,2},{6,1},{7,0},{8,15},{9,14},{10,... | collective-permute-start | bytes 221192 | tf_op jit(solution)/shard_map/ppermute | solution.py:316
  59.3 9.4 %collective-permute-start.9 = (s16[32,1152]{1,0:T(8,128)(2,1)S(1)}, s16[32,1152]{1,0:T(8,128)(2,1)S(1)}, u32[]{:S(2)}, u32[]{:S(2)}) collective-permute-start(s16[32,1152]{1,0:T(8,128)(2,1)S(1)} %get-tuple-element.78), channel_id=1, source_target_pairs={{0,3},{1,2},{2,1},{3,0},{4,7},{5,6},{6,5},{7,4},{8,11},{9,10},{10,... | collective-permute-start | bytes 221192 | tf_op jit(solution)/shard_map/ppermute | solution.py:316
  60.2 9.8 %collective-permute-start.10 = (s16[32,1152]{1,0:T(8,128)(2,1)S(1)}, s16[32,1152]{1,0:T(8,128)(2,1)S(1)}, u32[]{:S(2)}, u32[]{:S(2)}) collective-permute-start(s16[32,1152]{1,0:T(8,128)(2,1)S(1)} %get-tuple-element.79), channel_id=1, source_target_pairs={{0,4},{1,5},{2,6},{3,7},{4,0},{5,1},{6,2},{7,3},{8,12},{9,13},{10,... | collective-permute-start | bytes 221192 | tf_op jit(solution)/shard_map/ppermute | solution.py:316
  61.4 9.3 %collective-permute-start.11 = (s16[32,1152]{1,0:T(8,128)(2,1)S(1)}, s16[32,1152]{1,0:T(8,128)(2,1)S(1)}, u32[]{:S(2)}, u32[]{:S(2)}) collective-permute-start(s16[32,1152]{1,0:T(8,128)(2,1)S(1)} %get-tuple-element.80), channel_id=1, source_target_pairs={{0,5},{1,4},{2,7},{3,6},{4,1},{5,0},{6,3},{7,2},{8,13},{9,12},{10,... | collective-permute-start | bytes 221192 | tf_op jit(solution)/shard_map/ppermute | solution.py:316
  62.2 8.6 %collective-permute-start.12 = (s16[32,1152]{1,0:T(8,128)(2,1)S(1)}, s16[32,1152]{1,0:T(8,128)(2,1)S(1)}, u32[]{:S(2)}, u32[]{:S(2)}) collective-permute-start(s16[32,1152]{1,0:T(8,128)(2,1)S(1)} %get-tuple-element.81), channel_id=1, source_target_pairs={{0,6},{1,7},{2,4},{3,5},{4,2},{5,3},{6,0},{7,1},{8,14},{9,15},{10,... | collective-permute-start | bytes 221192 | tf_op jit(solution)/shard_map/ppermute | solution.py:316
  64.3 6.4 %collective-permute-start.13 = (s16[32,1152]{1,0:T(8,128)(2,1)S(1)}, s16[32,1152]{1,0:T(8,128)(2,1)S(1)}, u32[]{:S(2)}, u32[]{:S(2)}) collective-permute-start(s16[32,1152]{1,0:T(8,128)(2,1)S(1)} %get-tuple-element.82), channel_id=1, source_target_pairs={{0,7},{1,6},{2,5},{3,4},{4,3},{5,2},{6,1},{7,0},{8,15},{9,14},{10,... | collective-permute-start | bytes 221192 | tf_op jit(solution)/shard_map/ppermute | solution.py:316
  68.7 7.8 %collective-permute-start.33 = (bf16[32,1024]{1,0:T(8,128)(2,1)S(1)}, bf16[32,1024]{1,0:T(8,128)(2,1)S(1)}, u32[]{:S(2)}, u32[]{:S(2)}) collective-permute-start(bf16[32,1024]{1,0:T(8,128)(2,1)S(1)} %get-tuple-element.104), channel_id=1, source_target_pairs={{0,4},{1,5},{2,6},{3,7},{4,0},{5,1},{6,2},{7,3},{8,12},{9,13},{10,... | collective-permute-start | bytes 196616 | tf_op jit(solution)/shard_map/ppermute | solution.py:316
  70.0 7.8 %collective-permute-start.34 = (bf16[32,1024]{1,0:T(8,128)(2,1)S(1)}, bf16[32,1024]{1,0:T(8,128)(2,1)S(1)}, u32[]{:S(2)}, u32[]{:S(2)}) collective-permute-start(bf16[32,1024]{1,0:T(8,128)(2,1)S(1)} %get-tuple-element.105), channel_id=1, source_target_pairs={{0,5},{1,4},{2,7},{3,6},{4,1},{5,0},{6,3},{7,2},{8,13},{9,12},{10,... | collective-permute-start | bytes 196616 | tf_op jit(solution)/shard_map/ppermute | solution.py:316
  74.9 5.5 %collective-permute-start.15 = (bf16[32,1024]{1,0:T(8,128)(2,1)S(1)}, bf16[32,1024]{1,0:T(8,128)(2,1)S(1)}, u32[]{:S(2)}, u32[]{:S(2)}) collective-permute-start(bf16[32,1024]{1,0:T(8,128)(2,1)S(1)} %get-tuple-element.86), channel_id=1, source_target_pairs={{0,2},{1,3},{2,0},{3,1},{4,6},{5,7},{6,4},{7,5},{8,10},{9,11},{10,... | collective-permute-start | bytes 196616 | tf_op jit(solution)/shard_map/ppermute | solution.py:316
  77.8 5.8 %collective-permute-start.18 = (bf16[32,1024]{1,0:T(8,128)(2,1)S(1)}, bf16[32,1024]{1,0:T(8,128)(2,1)S(1)}, u32[]{:S(2)}, u32[]{:S(2)}) collective-permute-start(bf16[32,1024]{1,0:T(8,128)(2,1)S(1)} %get-tuple-element.89), channel_id=1, source_target_pairs={{0,5},{1,4},{2,7},{3,6},{4,1},{5,0},{6,3},{7,2},{8,13},{9,12},{10,... | collective-permute-start | bytes 196616 | tf_op jit(solution)/shard_map/ppermute | solution.py:316
  78.4 6.6 %collective-permute-start.19 = (bf16[32,1024]{1,0:T(8,128)(2,1)S(1)}, bf16[32,1024]{1,0:T(8,128)(2,1)S(1)}, u32[]{:S(2)}, u32[]{:S(2)}) collective-permute-start(bf16[32,1024]{1,0:T(8,128)(2,1)S(1)} %get-tuple-element.90), channel_id=1, source_target_pairs={{0,6},{1,7},{2,4},{3,5},{4,2},{5,3},{6,0},{7,1},{8,14},{9,15},{10,... | collective-permute-start | bytes 196616 | tf_op jit(solution)/shard_map/ppermute | solution.py:316
  80.4 5.5 %collective-permute-start.20 = (bf16[32,1024]{1,0:T(8,128)(2,1)S(1)}, bf16[32,1024]{1,0:T(8,128)(2,1)S(1)}, u32[]{:S(2)}, u32[]{:S(2)}) collective-permute-start(bf16[32,1024]{1,0:T(8,128)(2,1)S(1)} %get-tuple-element.91), channel_id=1, source_target_pairs={{0,7},{1,6},{2,5},{3,4},{4,3},{5,2},{6,1},{7,0},{8,15},{9,14},{10,... | collective-permute-start | bytes 196616 | tf_op jit(solution)/shard_map/ppermute | solution.py:316
  81.0 10.6 %collective-permute-start.30 = (bf16[32,1024]{1,0:T(8,128)(2,1)S(1)}, bf16[32,1024]{1,0:T(8,128)(2,1)S(1)}, u32[]{:S(2)}, u32[]{:S(2)}) collective-permute-start(bf16[32,1024]{1,0:T(8,128)(2,1)S(1)} %get-tuple-element.101), channel_id=1, source_target_pairs={{0,1},{1,0},{2,3},{3,2},{4,5},{5,4},{6,7},{7,6},{8,9},{9,8},{10,11... | collective-permute-start | bytes 196616 | tf_op jit(solution)/shard_map/ppermute | solution.py:316
  81.9 5.7 %collective-permute-start.35 = (bf16[32,1024]{1,0:T(8,128)(2,1)S(1)}, bf16[32,1024]{1,0:T(8,128)(2,1)S(1)}, u32[]{:S(2)}, u32[]{:S(2)}) collective-permute-start(bf16[32,1024]{1,0:T(8,128)(2,1)S(1)} %get-tuple-element.106), channel_id=1, source_target_pairs={{0,6},{1,7},{2,4},{3,5},{4,2},{5,3},{6,0},{7,1},{8,14},{9,15},{10,... | collective-permute-start | bytes 196616 | tf_op jit(solution)/shard_map/ppermute | solution.py:316
  85.1 6.5 %collective-permute-start.31 = (bf16[32,1024]{1,0:T(8,128)(2,1)S(1)}, bf16[32,1024]{1,0:T(8,128)(2,1)S(1)}, u32[]{:S(2)}, u32[]{:S(2)}) collective-permute-start(bf16[32,1024]{1,0:T(8,128)(2,1)S(1)} %get-tuple-element.102), channel_id=1, source_target_pairs={{0,2},{1,3},{2,0},{3,1},{4,6},{5,7},{6,4},{7,5},{8,10},{9,11},{10,... | collective-permute-start | bytes 196616 | tf_op jit(solution)/shard_map/ppermute | solution.py:316
  86.0 5.8 %collective-permute-start.32 = (bf16[32,1024]{1,0:T(8,128)(2,1)S(1)}, bf16[32,1024]{1,0:T(8,128)(2,1)S(1)}, u32[]{:S(2)}, u32[]{:S(2)}) collective-permute-start(bf16[32,1024]{1,0:T(8,128)(2,1)S(1)} %get-tuple-element.103), channel_id=1, source_target_pairs={{0,3},{1,2},{2,1},{3,0},{4,7},{5,6},{6,5},{7,4},{8,11},{9,10},{10,... | collective-permute-start | bytes 196616 | tf_op jit(solution)/shard_map/ppermute | solution.py:316
  87.7 11.0 %collective-permute-start.22 = (bf16[128,1024]{1,0:T(8,128)(2,1)S(1)}, bf16[128,1024]{1,0:T(8,128)(2,1)S(1)}, u32[]{:S(2)}, u32[]{:S(2)}) collective-permute-start(bf16[128,1024]{1,0:T(8,128)(2,1)S(1)} %shard_map.63.refs_1_), channel_id=1, source_target_pairs={{0,8},{1,9},{2,10},{3,11},{4,28},{5,29},{6,30},{7,31},{8,16},{9,17... | collective-permute-start | bytes 786440 | tf_op jit(solution)/shard_map/ppermute | solution.py:316
  89.1 15.3 %collective-permute-start.21 = (bf16[128,1024]{1,0:T(8,128)(2,1)S(1)}, bf16[128,1024]{1,0:T(8,128)(2,1)S(1)}, u32[]{:S(2)}, u32[]{:S(2)}) collective-permute-start(bf16[128,1024]{1,0:T(8,128)(2,1)S(1)} %shard_map.62.refs_0_), channel_id=1, source_target_pairs={{0,24},{1,25},{2,26},{3,27},{4,12},{5,13},{6,14},{7,15},{8,0},{9,1... | collective-permute-start | bytes 786440 | tf_op jit(solution)/shard_map/ppermute | solution.py:316
  91.5 18.5 %collective-permute-start.38 = (bf16[128,1024]{1,0:T(8,128)(2,1)S(1)}, bf16[128,1024]{1,0:T(8,128)(2,1)S(1)}, u32[]{:S(2)}, u32[]{:S(2)}) collective-permute-start(bf16[128,1024]{1,0:T(8,128)(2,1)S(1)} %shard_map.66.refs_5_), channel_id=1, source_target_pairs={{0,8},{1,9},{2,10},{3,11},{4,28},{5,29},{6,30},{7,31},{8,16},{9,17... | collective-permute-start | bytes 786440 | tf_op jit(solution)/shard_map/ppermute | solution.py:316
  91.8 22.4 %collective-permute-start.37 = (bf16[128,1024]{1,0:T(8,128)(2,1)S(1)}, bf16[128,1024]{1,0:T(8,128)(2,1)S(1)}, u32[]{:S(2)}, u32[]{:S(2)}) collective-permute-start(bf16[128,1024]{1,0:T(8,128)(2,1)S(1)} %shard_map.65.refs_4_), channel_id=1, source_target_pairs={{0,24},{1,25},{2,26},{3,27},{4,12},{5,13},{6,14},{7,15},{8,0},{9,1... | collective-permute-start | bytes 786440 | tf_op jit(solution)/shard_map/ppermute | solution.py:316
  117.0 5.5 %collective-permute-start.51 = (s16[32,1152]{1,0:T(8,128)(2,1)S(1)}, s16[32,1152]{1,0:T(8,128)(2,1)S(1)}, u32[]{:S(2)}, u32[]{:S(2)}) collective-permute-start(s16[32,1152]{1,0:T(8,128)(2,1)S(1)} %get-tuple-element.124), channel_id=1, source_target_pairs={{0,3},{1,2},{2,1},{3,0},{4,7},{5,6},{6,5},{7,4},{8,11},{9,10},{10,... | collective-permute-start | bytes 221192 | tf_op jit(solution)/shard_map/ppermute | solution.py:316
  119.8 6.6 %collective-permute-start.54 = (s16[32,1152]{1,0:T(8,128)(2,1)S(1)}, s16[32,1152]{1,0:T(8,128)(2,1)S(1)}, u32[]{:S(2)}, u32[]{:S(2)}) collective-permute-start(s16[32,1152]{1,0:T(8,128)(2,1)S(1)} %get-tuple-element.127), channel_id=1, source_target_pairs={{0,6},{1,7},{2,4},{3,5},{4,2},{5,3},{6,0},{7,1},{8,14},{9,15},{10,... | collective-permute-start | bytes 221192 | tf_op jit(solution)/shard_map/ppermute | solution.py:316
  121.4 5.7 %collective-permute-start.55 = (s16[32,1152]{1,0:T(8,128)(2,1)S(1)}, s16[32,1152]{1,0:T(8,128)(2,1)S(1)}, u32[]{:S(2)}, u32[]{:S(2)}) collective-permute-start(s16[32,1152]{1,0:T(8,128)(2,1)S(1)} %get-tuple-element.128), channel_id=1, source_target_pairs={{0,7},{1,6},{2,5},{3,4},{4,3},{5,2},{6,1},{7,0},{8,15},{9,14},{10,... | collective-permute-start | bytes 221192 | tf_op jit(solution)/shard_map/ppermute | solution.py:316
  122.5 9.9 %collective-permute-start.39 = (s16[32,1152]{1,0:T(8,128)(2,1)S(1)}, s16[32,1152]{1,0:T(8,128)(2,1)S(1)}, u32[]{:S(2)}, u32[]{:S(2)}) collective-permute-start(s16[32,1152]{1,0:T(8,128)(2,1)S(1)} %get-tuple-element.109), channel_id=1, source_target_pairs={{0,1},{1,0},{2,3},{3,2},{4,5},{5,4},{6,7},{7,6},{8,9},{9,8},{10,11... | collective-permute-start | bytes 221192 | tf_op jit(solution)/shard_map/ppermute | solution.py:316
  123.1 10.0 %collective-permute-start.40 = (s16[32,1152]{1,0:T(8,128)(2,1)S(1)}, s16[32,1152]{1,0:T(8,128)(2,1)S(1)}, u32[]{:S(2)}, u32[]{:S(2)}) collective-permute-start(s16[32,1152]{1,0:T(8,128)(2,1)S(1)} %get-tuple-element.110), channel_id=1, source_target_pairs={{0,2},{1,3},{2,0},{3,1},{4,6},{5,7},{6,4},{7,5},{8,10},{9,11},{10,... | collective-permute-start | bytes 221192 | tf_op jit(solution)/shard_map/ppermute | solution.py:316
  124.1 10.8 %collective-permute-start.41 = (s16[32,1152]{1,0:T(8,128)(2,1)S(1)}, s16[32,1152]{1,0:T(8,128)(2,1)S(1)}, u32[]{:S(2)}, u32[]{:S(2)}) collective-permute-start(s16[32,1152]{1,0:T(8,128)(2,1)S(1)} %get-tuple-element.111), channel_id=1, source_target_pairs={{0,3},{1,2},{2,1},{3,0},{4,7},{5,6},{6,5},{7,4},{8,11},{9,10},{10,... | collective-permute-start | bytes 221192 | tf_op jit(solution)/shard_map/ppermute | solution.py:316
  131.1 15.0 %collective-permute-start.56 = (s16[32,2176]{1,0:T(8,128)(2,1)S(1)}, s16[32,2176]{1,0:T(8,128)(2,1)S(1)}, u32[]{:S(2)}, u32[]{:S(2)}) collective-permute-start(s16[32,2176]{1,0:T(8,128)(2,1)S(1)} %get-tuple-element.130), channel_id=1, source_target_pairs={{0,1},{1,0},{2,3},{3,2},{4,5},{5,4},{6,7},{7,6},{8,9},{9,8},{10,11... | collective-permute-start | bytes 417800 | tf_op jit(solution)/shard_map/ppermute | solution.py:316
  133.1 7.3 %collective-permute-start.44 = (s16[32,1152]{1,0:T(8,128)(2,1)S(1)}, s16[32,1152]{1,0:T(8,128)(2,1)S(1)}, u32[]{:S(2)}, u32[]{:S(2)}) collective-permute-start(s16[32,1152]{1,0:T(8,128)(2,1)S(1)} %get-tuple-element.114), channel_id=1, source_target_pairs={{0,6},{1,7},{2,4},{3,5},{4,2},{5,3},{6,0},{7,1},{8,14},{9,15},{10,... | collective-permute-start | bytes 221192 | tf_op jit(solution)/shard_map/ppermute | solution.py:316
  134.9 6.3 %collective-permute-start.45 = (s16[32,1152]{1,0:T(8,128)(2,1)S(1)}, s16[32,1152]{1,0:T(8,128)(2,1)S(1)}, u32[]{:S(2)}, u32[]{:S(2)}) collective-permute-start(s16[32,1152]{1,0:T(8,128)(2,1)S(1)} %get-tuple-element.115), channel_id=1, source_target_pairs={{0,7},{1,6},{2,5},{3,4},{4,3},{5,2},{6,1},{7,0},{8,15},{9,14},{10,... | collective-permute-start | bytes 221192 | tf_op jit(solution)/shard_map/ppermute | solution.py:316
  136.4 10.7 %collective-permute-start.57 = (s16[32,2176]{1,0:T(8,128)(2,1)S(1)}, s16[32,2176]{1,0:T(8,128)(2,1)S(1)}, u32[]{:S(2)}, u32[]{:S(2)}) collective-permute-start(s16[32,2176]{1,0:T(8,128)(2,1)S(1)} %get-tuple-element.131), channel_id=1, source_target_pairs={{0,2},{1,3},{2,0},{3,1},{4,6},{5,7},{6,4},{7,5},{8,10},{9,11},{10,... | collective-permute-start | bytes 417800 | tf_op jit(solution)/shard_map/ppermute | solution.py:316
  137.7 9.6 %collective-permute-start.58 = (s16[32,2176]{1,0:T(8,128)(2,1)S(1)}, s16[32,2176]{1,0:T(8,128)(2,1)S(1)}, u32[]{:S(2)}, u32[]{:S(2)}) collective-permute-start(s16[32,2176]{1,0:T(8,128)(2,1)S(1)} %get-tuple-element.132), channel_id=1, source_target_pairs={{0,3},{1,2},{2,1},{3,0},{4,7},{5,6},{6,5},{7,4},{8,11},{9,10},{10,... | collective-permute-start | bytes 417800 | tf_op jit(solution)/shard_map/ppermute | solution.py:316
  145.5 6.5 %collective-permute-start.47 = (s16[32,2176]{1,0:T(8,128)(2,1)S(1)}, s16[32,2176]{1,0:T(8,128)(2,1)S(1)}, u32[]{:S(2)}, u32[]{:S(2)}) collective-permute-start(s16[32,2176]{1,0:T(8,128)(2,1)S(1)} %get-tuple-element.118), channel_id=1, source_target_pairs={{0,2},{1,3},{2,0},{3,1},{4,6},{5,7},{6,4},{7,5},{8,10},{9,11},{10,... | collective-permute-start | bytes 417800 | tf_op jit(solution)/shard_map/ppermute | solution.py:316
  146.1 7.6 %collective-permute-start.48 = (s16[32,2176]{1,0:T(8,128)(2,1)S(1)}, s16[32,2176]{1,0:T(8,128)(2,1)S(1)}, u32[]{:S(2)}, u32[]{:S(2)}) collective-permute-start(s16[32,2176]{1,0:T(8,128)(2,1)S(1)} %get-tuple-element.119), channel_id=1, source_target_pairs={{0,3},{1,2},{2,1},{3,0},{4,7},{5,6},{6,5},{7,4},{8,11},{9,10},{10,... | collective-permute-start | bytes 417800 | tf_op jit(solution)/shard_map/ppermute | solution.py:316
  (17 other events, 114.9 us)
where the time goes:
time: 156 us
  waiting for transfers between devices  61.9 us (40%)
  starting transfers between devices  61.1 us (39%)
  Pallas kernels  29.8 us (19%)
  local copies, waits for them, and re-layouts  2.98 us (2%)
    ppermute x59, waiting for transfers between devices, move(): return lax.ppermute(value, ('ka', 'ba'), pairs_of)  61.9 us
    ppermute x59, starting transfers between devices, move(): return lax.ppermute(value, ('ka', 'ba'), pairs_of)  61.1 us
    pallas_call x2, Pallas kernels, local(): call(second_kernel, [shape((count, own * LANE + LANE), i16)] * nb, [chunk...  8.07 us
    pallas_call x2, Pallas kernels, local(): call(first_kernel, [chunk_shape] + [shape((count, half * LANE), bf16)] *...  7.79 us
  transfers between devices with their start and end apart: 59, of which 23 were waited for; matrix products, arithmetic and copies ran while one was open for 0% of the time, Pallas kernels for 15%

commit v1 on v0

v1 whole, which is shorter than its diff:
```python
import functools
ACUTS = 2
ECUTS = 2

import jax
import jax.numpy as jnp
from jax import lax
from jax.experimental import pallas as pl
from jax.experimental.pallas import tpu as pltpu
from jax.sharding import PartitionSpec as P

NB = 64
TILE = 128
ND = 4
REACH = 2
LANE = 2 * NB
SPAN = (2 * REACH + 1) * TILE
PACK = 16

step_size = 0.25
f32, bf16, i16, i32 = jnp.float32, jnp.bfloat16, jnp.int16, jnp.int32
SMEM = pl.BlockSpec(memory_space=pltpu.SMEM)
VMEM = pl.BlockSpec(memory_space=pltpu.VMEM)


def call(kernel, out, scratch=(), specs=None, n_in=0, work=1.0):
    return pl.pallas_call(
        kernel,
        out_shape=out,
        in_specs=specs if specs is not None else [SMEM] + [VMEM] * n_in,
        scratch_shapes=scratch,
        compiler_params=pltpu.CompilerParams(vmem_limit_bytes=48 * 2**20),
        cost_estimate=pl.CostEstimate(flops=0, bytes_accessed=int(work * 3.6e6), transcendentals=0),
    )


def half_lanes(shape):
    return lax.broadcasted_iota(i32, shape, 1) < NB


def rows_of(real, imag):
    low = half_lanes(real.shape)
    even = jnp.where(low, real, pltpu.roll(imag, NB, 1))
    odd = jnp.where(low, pltpu.roll(real, NB, 1), imag)
    return even, odd


def parts_of(even, odd):
    low = half_lanes(even.shape)
    real = jnp.where(low, even, pltpu.roll(odd, NB, 1))
    imag = jnp.where(low, pltpu.roll(even, NB, 1), odd)
    return real, imag


def encode(values, peak):
    power = jnp.ceil(jnp.log2(jnp.maximum(peak, 1e-30)))
    scale = jnp.exp2(15.0 - power)
    codes = [jnp.clip(jnp.round(v * scale), -32767.0, 32767.0).astype(i32).astype(i16) for v in values]
    return codes, power


def own_lane(shape):
    return lax.broadcasted_iota(i32, shape, 0) == lax.broadcasted_iota(i32, shape, 1)


def put_power(out, at, power):
    wide = jnp.where(own_lane((power.shape[0], LANE)), power, 0.0)
    line = jnp.sum(wide, axis=0, keepdims=True)
    out[at : at + PACK, :] = jnp.broadcast_to(line, (PACK, LANE)).astype(i32).astype(i16)


def get_scale(piece, at, count):
    line = piece[at : at + PACK, :].astype(i32).astype(f32)[:1]
    wide = jnp.where(own_lane((count, LANE)), jnp.broadcast_to(line, (count, LANE)), 0.0)
    return jnp.broadcast_to(jnp.exp2(jnp.sum(wide, axis=1, keepdims=True) - 15.0), (count, LANE))


def round_kernel(density, *outs):
    width = density.shape[2] // len(outs)
    for n, out in enumerate(outs):
        for t in range(width // LANE):
            cols = slice(n * width + t * LANE, n * width + (t + 1) * LANE)
            even, odd = rows_of(density[0, :, cols], density[1, :, cols])
            out[:, 2 * t * LANE : (2 * t + 1) * LANE] = even.astype(bf16)
            out[:, (2 * t + 1) * LANE : (2 * t + 2) * LANE] = odd.astype(bf16)


def split_kernel(place, density, *outs):
    j = place[1]
    rows = outs[0].shape[0]
    for k, out in enumerate(outs):
        at = pl.ds(pl.multiple_of((j ^ k) * rows, rows), rows)
        for t in range(density.shape[2] // LANE):
            cols = slice(t * LANE, (t + 1) * LANE)
            even, odd = rows_of(density[0, at, cols], density[1, at, cols])
            out[:, 2 * t * LANE : (2 * t + 1) * LANE] = even
            out[:, (2 * t + 1) * LANE : (2 * t + 2) * LANE] = odd


def step_of(count):
    return count + 8


def matrices_from_rows(rows, out):
    count = out.shape[0]

    def body(m, carry):
        out[m] = rows[pl.ds(m, NB, stride=step_of(count)), :]
        return carry

    lax.fori_loop(0, count, body, 0, unroll=8)


def hamilton_kernel(h, out, rows):
    count = out.shape[0]
    for t in range(h.shape[2] // LANE):
        cols = slice(t * LANE, (t + 1) * LANE)
        even, odd = rows_of(h[0, :, cols], h[1, :, cols])
        for a, value in ((2 * t, even), (2 * t + 1, odd)):
            rows[a * step_of(count) : a * step_of(count) + count, :] = value
    matrices_from_rows(rows, out)


def state_kernel(place, *refs):
    pieces, out, rows = refs[:-2], refs[-2], refs[-1]
    j = place[1]
    count = out.shape[0]
    own = pieces[0].shape[1] // LANE
    for k, piece in enumerate(pieces):
        for a in range(own):
            at = pl.multiple_of(((j ^ k) * own + a) * step_of(count), 8)
            rows[pl.ds(at, count), :] = piece[:, a * LANE : (a + 1) * LANE]
    matrices_from_rows(rows, out)


def coupling_kernel(total, place, donors, counts, coupling, out):
    tiles = coupling.shape[0]
    blocks = {}
    for t in range(tiles):
        for o in range(2 * REACH + 1):
            block = jnp.zeros((TILE, TILE), f32)
            for s in range(ND):
                shift = lax.rem(donors[t, s] - (place[2] + t) + REACH + total, total)
                used = jnp.logical_and(shift == o, s < counts[t])
                block = block - coupling[t, s].astype(f32) * jnp.where(used, 1.0, 0.0)
            blocks[t, t + o] = block.astype(bf16)
    empty = jnp.zeros((TILE, TILE), bf16)
    for t in range(tiles):
        for n in range(3 * tiles):
            mirror = (2 - n // tiles) * tiles + n % tiles
            value = jnp.where(place[0] == 1, blocks.get((t, n), empty), blocks.get((t, mirror), empty))
            out[t * TILE : (t + 1) * TILE, n * TILE : (n + 1) * TILE] = value


def field(place, weights, states, codes, powers, outs, chunks):
    j = place[1]
    ways = len(outs) // chunks
    sigma = jnp.dot(weights, states, preferred_element_type=f32)
    (code,), power = encode([sigma], jnp.max(jnp.abs(sigma), axis=1, keepdims=True))
    codes[...] = code
    powers[...] = jnp.broadcast_to(power, powers.shape)
    blocks = codes.shape[1] // LANE
    count = (outs[0].shape[0] - PACK) // blocks
    for c in range(chunks):
        for k in range(ways):
            at = pl.ds(pl.multiple_of(((j ^ k) * chunks + c) * count, count), count)
            out = outs[c * ways + k]
            for a in range(blocks):
                out[a * count : (a + 1) * count, :] = codes[at, a * LANE : (a + 1) * LANE]
            put_power(out, blocks * count, powers[at, :1])


def field_one_kernel(place, dense, mine, swap, passed, *refs):
    outs, (codes, powers) = refs[:-2], refs[-2:]
    states = jnp.concatenate([swap[...], mine[...], passed[...]], 0)
    field(place, dense[...], states, codes, powers, outs, 1)


def field_two_kernel(chunks, cuts, place, dense, *refs):
    n = 3 * chunks * cuts
    states, outs, (codes, powers, window) = refs[:n], refs[n:-3], refs[-3:]
    j = place[1]
    ways = len(outs) // chunks
    for c in range(chunks):
        for q in range(cuts):
            for b in range(3):
                ref = states[(c * cuts + q) * 3 + b]
                count, width = ref.shape[0] // ways, ref.shape[1]
                for k in range(ways):
                    at = ((b * ways + (j ^ k)) * chunks + c) * count
                    window[pl.ds(pl.multiple_of(at, count), count), q * width : (q + 1) * width] = ref[
                        k * count : (k + 1) * count, :
                    ]
    field(place, dense[...], window[...], codes, powers, outs, chunks)


def two_parts(values):
    high = values.astype(bf16)
    return high, (values - high.astype(f32)).astype(bf16)


def turned(rows):
    moved = pltpu.roll(rows, NB, 1)
    return jnp.where(half_lanes(rows.shape), moved, -moved)


def rate(h, s):
    h_high, h_low = two_parts(h)
    s_high, s_low = two_parts(s)
    left = jnp.concatenate(
        [jnp.concatenate([h_high, -s_high], 1), jnp.concatenate([h_low, -s_low], 1)], 0
    )
    right = [
        jnp.concatenate([turned(sp), sp, turned(hp), hp], 0) for sp, hp in ((s_high, h_high), (s_low, h_low))
    ]
    o = jnp.dot(left, jnp.concatenate(right, 1), preferred_element_type=f32)
    return (o[:NB, :LANE] + o[NB:, :LANE]) + (o[:NB, LANE:] + o[NB:, LANE:])


def unpack_field(place, cuts, count, first_row, pieces, rows):
    j = place[1]
    ways = len(pieces) // cuts
    whole = pieces[0].shape[0] - PACK
    own = NB // cuts // ways
    stride = whole // own
    for q in range(cuts):
        for k in range(ways):
            piece = pieces[q * ways + k]
            first = ((j ^ k) * cuts + q) * own
            scale = get_scale(piece, whole, stride)[first_row : first_row + count]
            for a in range(own):
                at = pl.multiple_of((first + a) * step_of(count), 8)
                code = piece[a * stride + first_row : a * stride + first_row + count, :]
                rows[pl.ds(at, count), :] = code.astype(i32).astype(f32) * scale


def first_kernel(cuts, n, first_row, place, h, s, *refs):
    pieces, middle, outs, rows, back = refs[:n], refs[n], refs[n + 1 : -2], refs[-2], refs[-1]
    j = place[1]
    count = middle.shape[0]
    step = step_of(count)
    unpack_field(place, cuts, count, first_row, pieces, rows)

    def body(m, carry):
        state = s[m]
        value = state + 0.5 * step_size * rate(h[m] + rows[pl.ds(m, NB, stride=step), :], state)
        middle[m] = value
        back[pl.ds(m, NB, stride=step), :] = value
        return carry

    lax.fori_loop(0, count, body, 0, unroll=16)
    own = outs[0].shape[1] // LANE
    for k, out in enumerate(outs):
        for a in range(own):
            at = pl.multiple_of(((j ^ k) * own + a) * step, 8)
            out[:, a * LANE : (a + 1) * LANE] = back[pl.ds(at, count), :].astype(bf16)


def second_kernel(ways, place, h, s, *refs):
    pieces, outs, rows, back = refs[:ways], refs[ways:-2], refs[-2], refs[-1]
    j = place[1]
    count = h.shape[0]
    step = step_of(count)
    unpack_field(place, 1, count, 0, pieces, rows)

    def body(m, carry):
        back[pl.ds(m, NB, stride=step), :] = rate(h[m] + rows[pl.ds(m, NB, stride=step), :], s[m])
        return carry

    lax.fori_loop(0, count, body, 0, unroll=16)
    own = (outs[0].shape[0] - PACK) // count
    for k, out in enumerate(outs):
        first = (j ^ k) * own
        values = [back[pl.ds(pl.multiple_of((first + a) * step, 8), count), :] for a in range(own)]
        peak = functools.reduce(jnp.maximum, [jnp.abs(v) for v in values])
        codes, power = encode(values, jnp.max(peak, axis=1, keepdims=True))
        for a in range(own):
            out[a * count : (a + 1) * count, :] = codes[a]
        put_power(out, own * count, power)


def last_kernel(chunks, place, density, *refs):
    pieces, out = refs[:-1], refs[-1]
    j = place[1]
    ways = len(pieces) // chunks
    own = 2 * density.shape[2] // LANE
    count = (pieces[0].shape[0] - PACK) // own
    for c in range(chunks):
        for k in range(ways):
            piece = pieces[c * ways + k]
            at = pl.ds(pl.multiple_of(((j ^ k) * chunks + c) * count, count), count)
            scale = get_scale(piece, own * count, count) * step_size
            block = lambda a: piece[a * count : (a + 1) * count, :].astype(i32).astype(f32) * scale
            for t in range(own // 2):
                real, imag = parts_of(block(2 * t), block(2 * t + 1))
                cols = slice(t * LANE, (t + 1) * LANE)
                out[0, at, cols] = density[0, at, cols] + real
                out[1, at, cols] = density[1, at, cols] + imag


def join_kernel(cuts, *refs):
    pieces, outs = refs[:-cuts], refs[-cuts:]
    count, width = pieces[0].shape[0], outs[0].shape[1]
    for q, out in enumerate(outs):
        for k, piece in enumerate(pieces):
            out[k * count : (k + 1) * count, :] = piece[:, q * width : (q + 1) * width]


def tie(values, *others):
    return lax.optimization_barrier((values, others))[0]


def local(density, h_bands, coupling, donors, counts):
    nka, nb = lax.axis_size("ka"), lax.axis_size("ba")
    i, j = lax.axis_index("ka"), lax.axis_index("ba")
    tiles, mom, pairs = coupling.shape[0], density.shape[1], density.shape[2]
    assert mom == tiles * TILE == REACH * TILE and nka % 2 == 0
    own = pairs // NB
    band = mom // nb
    chunks = 2 if band % 32 == 0 else 1
    count = band // chunks
    place = jnp.stack([i % 2, j, i * tiles]).astype(i32)

    def move(value, target):
        pairs_of = []
        for a in range(nka):
            for b in range(nb):
                ta, tb = target(a, b)
                pairs_of.append((a * nb + b, (ta % nka) * nb + tb))
        return lax.ppermute(value, ("ka", "ba"), pairs_of)

    def in_group(value, k):
        return value if k == 0 else move(value, lambda a, b: (a, b ^ k))

    def across(value):
        return move(value, lambda a, b: (a ^ 1, b))

    def onward(value):
        return move(value, lambda a, b: (a - 2 if a % 2 else a + 2, b))

    shape = jax.ShapeDtypeStruct
    cuts = max(n for n in (1, 2, 4) if n <= ACUTS and own % (2 * n) == 0)
    ecuts = max(n for n in (1, 2, 4) if n <= ECUTS and own % (2 * n) == 0)
    part = own // cuts
    mine = call(round_kernel, [shape((mom, part * LANE), bf16)] * cuts, specs=[VMEM])(density)
    swap = [across(v) for v in mine]
    passed = [onward(v) for v in swap]
    dense = call(
        functools.partial(coupling_kernel, nka * tiles),
        shape((mom, 3 * mom), bf16),
        specs=[SMEM, SMEM, SMEM, VMEM],
    )(place, donors, counts, coupling)
    sent = call(split_kernel, [shape((band, own * LANE), f32)] * nb, n_in=1)(place, density)
    states = [in_group(v, k) for k, v in enumerate(sent)]
    matrices = shape((band, NB, LANE), f32)
    rows = pltpu.VMEM((step_of(band) * NB, LANE), f32)
    hamilton = call(hamilton_kernel, matrices, [rows], specs=[VMEM])(h_bands)
    hamilton, passed[0] = lax.optimization_barrier((hamilton, passed[0]))

    got, fields = [], []
    for q in range(cuts):
        fields = call(
            field_one_kernel,
            [shape((part * band + PACK, LANE), i16)] * nb,
            [pltpu.VMEM((mom, part * LANE), i16), pltpu.VMEM((mom, LANE), f32)],
            n_in=4,
        )(place, dense, mine[q], swap[q], passed[q])
        got += [in_group(v, k) for k, v in enumerate(fields)]
    state = call(state_kernel, matrices, [rows], n_in=nb)(place, *states)

    chunk_rows = pltpu.VMEM((step_of(count) * NB, LANE), f32)
    chunk_shape = shape((count, NB, LANE), f32)
    middles, parts = [], []
    for c in range(chunks):
        at = slice(c * count, (c + 1) * count)
        hc, sc = hamilton[at], state[at]
        middle, *outs = call(
            functools.partial(first_kernel, cuts, nb * cuts, c * count),
            [chunk_shape] + [shape((count, own * LANE), bf16)] * nb,
            [chunk_rows, chunk_rows],
            n_in=2 + nb * cuts,
        )(place, hc, sc, *got)
        middles.append(middle)
        back = [in_group(v, k) for k, v in enumerate(outs)]
        joined = [shape((nb * count, own // ecuts * LANE), bf16)] * ecuts
        mine = call(functools.partial(join_kernel, ecuts), joined, specs=[VMEM] * nb)(*back)
        for q in range(ecuts):
            swap = across(mine[q])
            parts += [swap, mine[q], onward(swap)]

    fields = call(
        functools.partial(field_two_kernel, chunks, ecuts),
        [shape((own * count + PACK, LANE), i16)] * (nb * chunks),
        [pltpu.VMEM((mom, own * LANE), i16), pltpu.VMEM((mom, LANE), f32), pltpu.VMEM((3 * mom, own * LANE), bf16)],
        n_in=1 + len(parts),
    )(place, dense, *parts)
    got = [[in_group(fields[c * nb + k], k) for k in range(nb)] for c in range(chunks)]
    rates = []
    for c in range(chunks):
        hc, sc = hamilton[c * count : (c + 1) * count], middles[c]
        outs = call(
            functools.partial(second_kernel, nb),
            [shape((own * count + PACK, LANE), i16)] * nb,
            [chunk_rows, chunk_rows],
            n_in=2 + nb,
        )(place, hc, sc, *got[c])
        rates += [in_group(v, k) for k, v in enumerate(outs)]
    return call(
        functools.partial(last_kernel, chunks), shape(density.shape, f32), n_in=1 + nb * chunks
    )(place, density, *rates)


def solution(mesh):
    placed = (
        P(None, "ka", "ba"),
        P(None, ("ka", "ba"), None),
        P("ka", None, None, None),
        P("ka", None),
        P("ka"),
    )
    return jax.shard_map(
        local, mesh=mesh, in_specs=placed, out_specs=P(None, "ka", "ba"), check_vma=False
    )
```

time: 156 us -> 132 us (0.85)
  starting transfers between devices: 61.1 us -> 30.2 us
  waiting for transfers between devices: 61.9 us -> 77.2 us
  Pallas kernels: 29.8 us -> 21.9 us
    ppermute x59 -> x39, starting transfers between devices: 61.1 us -> 30.2 us  [move(): return lax.ppermute(value, ('ka', 'ba'), pairs_of)]
    ppermute x59 -> x39, waiting for transfers between devices: 61.9 us -> 77.2 us  [move(): return lax.ppermute(value, ('ka', 'ba'), pairs_of)]
    pallas_call x12 -> x11, Pallas kernels: 21.9 us -> 15.4 us  [the longest x2 4.11 us: local(): call(functools.partial(second_kernel, nb), [shape((own * count + PACK, LA...]
  transfers between devices with their start and end apart: 59 -> 39, of which waited for: 23 -> 21; matrix products, arithmetic and copies ran while one was open for 0% -> 0% of each run, Pallas kernels for 15% -> 11%
where the time goes in v1:
time: 132 us
  waiting for transfers between devices  77.2 us (58%)
  starting transfers between devices  30.2 us (23%)
  Pallas kernels  21.9 us (17%)
  local copies, waits for them, and re-layouts  2.04 us (2%)
    ppermute x39, waiting for transfers between devices, move(): return lax.ppermute(value, ('ka', 'ba'), pairs_of)  77.2 us
    ppermute x39, starting transfers between devices, move(): return lax.ppermute(value, ('ka', 'ba'), pairs_of)  30.2 us
    pallas_call x2, Pallas kernels, local(): call(functools.partial(second_kernel, nb), [shape((own * count + PACK, LA...  4.11 us
    pallas_call x2, Pallas kernels, local(): call(field_one_kernel, [shape((part * band + PACK, LANE), i16)] * nb, [pl...  3.87 us
    pallas_call x2, Pallas kernels, local(): call(functools.partial(first_kernel, cuts, nb * cuts, c * count), [chunk_...  3.75 us
    pallas_call x1, Pallas kernels, local(): call(functools.partial(last_kernel, chunks), shape(density.shape, f32), n...  3.28 us
  transfers between devices with their start and end apart: 39, of which 21 were waited for; matrix products, arithmetic and copies ran while one was open for 0% of the time, Pallas kernels for 11%

profile of v1, /device:TPU:0, one launch (start us, length us, event | category | flops | bytes accessed | tf_op | source)
XLA Modules:
  0.0 131.7 jit_solution(5778031338337500011)
XLA Ops:
  0.0 1.6 %copy-done = f32[2,256,1024]{2,1,0:T(8,128)S(1)} copy-done((f32[2,256,1024]{2,1,0:T(8,128)S(1)}, f32[2,256,1024]{2,1,0:T(8,128)}, u32[]{:S(2)}) %copy-start) | copy-done | bytes 2097176
  2.0 3.0 %collective-permute-start.8 = (bf16[256,1024]{1,0:T(8,128)(2,1)S(1)}, bf16[256,1024]{1,0:T(8,128)(2,1)}, u32[]{:S(2)}, u32[]{:S(2)}) collective-permute-start(bf16[256,1024]{1,0:T(8,128)(2,1)S(1)} %get-tuple-element.62.mine), channel_id=1, source_target_pairs={{0,4},{1,5},{2,6},{3,7},{4,0},{5,1},{6,2},{7,3},{8,12},{9,13},{10,... | collective-permute-start | bytes 1572872 | tf_op jit(solution)/shard_map/ppermute | solution.py:330
  5.2 1.1 shard_map.57
  6.4 2.0 %collective-permute-start.3 = (f32[64,2048]{1,0:T(8,128)S(1)}, f32[64,2048]{1,0:T(8,128)S(1)}, u32[]{:S(2)}, u32[]{:S(2)}) collective-permute-start(f32[64,2048]{1,0:T(8,128)S(1)} %get-tuple-element.55), channel_id=1, source_target_pairs={{0,2},{1,3},{2,0},{3,1},{4,6},{5,7},{6,4},{7,5},{8,10},{9,11},{10,... | collective-permute-start | bytes 1572872 | tf_op jit(solution)/shard_map/ppermute | solution.py:330
  8.6 9.3 %collective-permute-done.8.swap = bf16[256,1024]{1,0:T(8,128)(2,1)} collective-permute-done((bf16[256,1024]{1,0:T(8,128)(2,1)S(1)}, bf16[256,1024]{1,0:T(8,128)(2,1)}, u32[]{:S(2)}, u32[]{:S(2)}) %collective-permute-start.8) | collective-permute-done | bytes 524320 | tf_op jit(solution)/shard_map/ppermute | solution.py:330
  17.9 2.1 %collective-permute-start.9 = (bf16[256,1024]{1,0:T(8,128)(2,1)}, bf16[256,1024]{1,0:T(8,128)(2,1)S(1)}, u32[]{:S(2)}, u32[]{:S(2)}) collective-permute-start(bf16[256,1024]{1,0:T(8,128)(2,1)} %collective-permute-done.8.swap), channel_id=1, source_target_pairs={{0,8},{1,9},{2,10},{3,11},{4,28},{5,29},{6,30},{7,31},{8,16},{9,17... | collective-permute-start | bytes 1572872 | tf_op jit(solution)/shard_map/ppermute | solution.py:330
  20.0 8.3 %collective-permute-done.swap = bf16[256,1024]{1,0:T(8,128)(2,1)} collective-permute-done((bf16[256,1024]{1,0:T(8,128)(2,1)S(1)}, bf16[256,1024]{1,0:T(8,128)(2,1)}, u32[]{:S(2)}, u32[]{:S(2)}) %collective-permute-start) | collective-permute-done | bytes 524320 | tf_op jit(solution)/shard_map/ppermute | solution.py:330
  28.3 1.8 %collective-permute-start.1 = (bf16[256,1024]{1,0:T(8,128)(2,1)}, bf16[256,1024]{1,0:T(8,128)(2,1)S(1)}, u32[]{:S(2)}, u32[]{:S(2)}) collective-permute-start(bf16[256,1024]{1,0:T(8,128)(2,1)} %collective-permute-done.swap), channel_id=1, source_target_pairs={{0,8},{1,9},{2,10},{3,11},{4,28},{5,29},{6,30},{7,31},{8,16},{9,17... | collective-permute-start | bytes 1572872 | tf_op jit(solution)/shard_map/ppermute | solution.py:330
  30.1 1.0 shard_map.55
  32.0 1.1 shard_map.58
  33.1 1.9 %shard_map.61 = (s16[528,128]{1,0:T(8,128)(2,1)S(1)}, s16[528,128]{1,0:T(8,128)(2,1)S(1)}, s16[528,128]{1,0:T(8,128)(2,1)S(1)}, s16[528,128]{1,0:T(8,128)(2,1)S(1)}) custom-call(s32[3]{0:T(128)S(1)} %pad_add_fusion.place, bf16[256,768]{1,0:T(8,128)(2,1)S(1)} %shard_map.59.dense, bf16[256,1024]{1,0:T(8,128)(2,1)S(1)} %get-tuple-element.62.mine, ...), custom_call_target="tpu_custom_call" | custom-call | bytes 3600000 | tf_op jit(solution)/shard_map/pallas_call | solution.py:362
  35.6 1.6 %collective-permute-start.11 = (s16[528,128]{1,0:T(8,128)(2,1)S(1)}, s16[528,128]{1,0:T(8,128)(2,1)S(1)}, u32[]{:S(2)}, u32[]{:S(2)}) collective-permute-start(s16[528,128]{1,0:T(8,128)(2,1)S(1)} %get-tuple-element.65), channel_id=1, source_target_pairs={{0,2},{1,3},{2,0},{3,1},{4,6},{5,7},{6,4},{7,5},{8,10},{9,11},{10,... | collective-permute-start | bytes 405512 | tf_op jit(solution)/shard_map/ppermute | solution.py:330
  37.2 6.2 %collective-permute-done.1.passed = bf16[256,1024]{1,0:T(8,128)(2,1)S(1)} collective-permute-done((bf16[256,1024]{1,0:T(8,128)(2,1)}, bf16[256,1024]{1,0:T(8,128)(2,1)S(1)}, u32[]{:S(2)}, u32[]{:S(2)}) %collective-permute-start.1) | collective-permute-done | bytes 524320 | tf_op jit(solution)/shard_map/ppermute | solution.py:330
  43.4 1.9 %shard_map.60 = (s16[528,128]{1,0:T(8,128)(2,1)S(1)}, s16[528,128]{1,0:T(8,128)(2,1)S(1)}, s16[528,128]{1,0:T(8,128)(2,1)S(1)}, s16[528,128]{1,0:T(8,128)(2,1)S(1)}) custom-call(s32[3]{0:T(128)S(1)} %pad_add_fusion.place, bf16[256,768]{1,0:T(8,128)(2,1)S(1)} %shard_map.59.dense, bf16[256,1024]{1,0:T(8,128)(2,1)S(1)} %copy-done.4, ...), custom_call_target="tpu_custom_call" | custom-call | bytes 3600000 | tf_op jit(solution)/shard_map/pallas_call | solution.py:362
  45.4 1.6 %collective-permute-start.6 = (s16[528,128]{1,0:T(8,128)(2,1)S(1)}, s16[528,128]{1,0:T(8,128)(2,1)S(1)}, u32[]{:S(2)}, u32[]{:S(2)}) collective-permute-start(s16[528,128]{1,0:T(8,128)(2,1)S(1)} %get-tuple-element.60), channel_id=1, source_target_pairs={{0,2},{1,3},{2,0},{3,1},{4,6},{5,7},{6,4},{7,5},{8,10},{9,11},{10,... | collective-permute-start | bytes 405512 | tf_op jit(solution)/shard_map/ppermute | solution.py:330
  47.6 4.3 %collective-permute-done.6.refs_2_ = s16[528,128]{1,0:T(8,128)(2,1)S(1)} collective-permute-done((s16[528,128]{1,0:T(8,128)(2,1)S(1)}, s16[528,128]{1,0:T(8,128)(2,1)S(1)}, u32[]{:S(2)}, u32[]{:S(2)}) %collective-permute-start.6) | collective-permute-done | bytes 135200 | tf_op jit(solution)/shard_map/ppermute | solution.py:330
  51.9 2.0 %collective-permute-done.7.refs_3_ = s16[528,128]{1,0:T(8,128)(2,1)S(1)} collective-permute-done((s16[528,128]{1,0:T(8,128)(2,1)S(1)}, s16[528,128]{1,0:T(8,128)(2,1)S(1)}, u32[]{:S(2)}, u32[]{:S(2)}) %collective-permute-start.7) | collective-permute-done | bytes 135200 | tf_op jit(solution)/shard_map/ppermute | solution.py:330
  53.9 1.9 %shard_map.62 = (f32[32,64,128]{2,1,0:T(8,128)S(1)}, bf16[32,2048]{1,0:T(8,128)(2,1)S(1)}, bf16[32,2048]{1,0:T(8,128)(2,1)S(1)}, bf16[32,2048]{1,0:T(8,128)(2,1)S(1)}, bf16[32,2048]{1,0:T(8,128)(2,1)S(1)}) custom-call(s32[3]{0:T(128)S(1)} %pad_add_fusion.place, f32[32,64,128]{2,1,0:T(8,128)S(1)} %get-tuple-element.100.h, ...), custom_call_target="tpu_custom_call" | custom-call | bytes 3600000 | tf_op jit(solution)/shard_map/pallas_call | solution.py:377
  56.1 1.5 %collective-permute-start.14 = (bf16[32,2048]{1,0:T(8,128)(2,1)S(1)}, bf16[32,2048]{1,0:T(8,128)(2,1)S(1)}, u32[]{:S(2)}, u32[]{:S(2)}) collective-permute-start(bf16[32,2048]{1,0:T(8,128)(2,1)S(1)} %get-tuple-element.70), channel_id=1, source_target_pairs={{0,2},{1,3},{2,0},{3,1},{4,6},{5,7},{6,4},{7,5},{8,10},{9,11},{10,... | collective-permute-start | bytes 393224 | tf_op jit(solution)/shard_map/ppermute | solution.py:330
  57.7 1.9 %shard_map.64 = (f32[32,64,128]{2,1,0:T(8,128)S(1)}, bf16[32,2048]{1,0:T(8,128)(2,1)S(1)}, bf16[32,2048]{1,0:T(8,128)(2,1)S(1)}, bf16[32,2048]{1,0:T(8,128)(2,1)S(1)}, bf16[32,2048]{1,0:T(8,128)(2,1)S(1)}) custom-call(s32[3]{0:T(128)S(1)} %pad_add_fusion.place, f32[32,64,128]{2,1,0:T(8,128)S(1)} %get-tuple-element.99.h, ...), custom_call_target="tpu_custom_call" | custom-call | bytes 3600000 | tf_op jit(solution)/shard_map/pallas_call | solution.py:377
  60.2 1.5 %collective-permute-start.21 = (bf16[32,2048]{1,0:T(8,128)(2,1)S(1)}, bf16[32,2048]{1,0:T(8,128)(2,1)S(1)}, u32[]{:S(2)}, u32[]{:S(2)}) collective-permute-start(bf16[32,2048]{1,0:T(8,128)(2,1)S(1)} %get-tuple-element.76), channel_id=1, source_target_pairs={{0,2},{1,3},{2,0},{3,1},{4,6},{5,7},{6,4},{7,5},{8,10},{9,11},{10,... | collective-permute-start | bytes 393224 | tf_op jit(solution)/shard_map/ppermute | solution.py:330
  62.4 1.8 %collective-permute-done.15.refs_3_ = bf16[32,2048]{1,0:T(8,128)(2,1)S(1)} collective-permute-done((bf16[32,2048]{1,0:T(8,128)(2,1)S(1)}, bf16[32,2048]{1,0:T(8,128)(2,1)S(1)}, u32[]{:S(2)}, u32[]{:S(2)}) %collective-permute-start.15) | collective-permute-done | bytes 131104 | tf_op jit(solution)/shard_map/ppermute | solution.py:330
  64.3 0.9 collective-permute-start.16
  65.2 1.2 collective-permute-start.18
  66.4 1.6 %collective-permute-done.21.refs_2_ = bf16[32,2048]{1,0:T(8,128)(2,1)S(1)} collective-permute-done((bf16[32,2048]{1,0:T(8,128)(2,1)S(1)}, bf16[32,2048]{1,0:T(8,128)(2,1)S(1)}, u32[]{:S(2)}, u32[]{:S(2)}) %collective-permute-start.21) | collective-permute-done | bytes 131104 | tf_op jit(solution)/shard_map/ppermute | solution.py:330
  68.0 1.4 %collective-permute-done.22.refs_3_ = bf16[32,2048]{1,0:T(8,128)(2,1)S(1)} collective-permute-done((bf16[32,2048]{1,0:T(8,128)(2,1)S(1)}, bf16[32,2048]{1,0:T(8,128)(2,1)S(1)}, u32[]{:S(2)}, u32[]{:S(2)}) %collective-permute-start.22) | collective-permute-done | bytes 131104 | tf_op jit(solution)/shard_map/ppermute | solution.py:330
  69.5 0.9 collective-permute-start.23
  70.4 1.2 collective-permute-start.25
  71.6 2.0 %collective-permute-done.16.refs_0_ = bf16[128,1024]{1,0:T(8,128)(2,1)S(1)} collective-permute-done((bf16[128,1024]{1,0:T(8,128)(2,1)S(1)}, bf16[128,1024]{1,0:T(8,128)(2,1)S(1)}, u32[]{:S(2)}, u32[]{:S(2)}) %collective-permute-start.16) | collective-permute-done | bytes 262176 | tf_op jit(solution)/shard_map/ppermute | solution.py:330
  73.5 5.6 %collective-permute-done.18.refs_3_ = bf16[128,1024]{1,0:T(8,128)(2,1)S(1)} collective-permute-done((bf16[128,1024]{1,0:T(8,128)(2,1)S(1)}, bf16[128,1024]{1,0:T(8,128)(2,1)S(1)}, u32[]{:S(2)}, u32[]{:S(2)}) %collective-permute-start.18) | collective-permute-done | bytes 262176 | tf_op jit(solution)/shard_map/ppermute | solution.py:330
  79.2 5.6 %collective-permute-done.23.refs_6_ = bf16[128,1024]{1,0:T(8,128)(2,1)S(1)} collective-permute-done((bf16[128,1024]{1,0:T(8,128)(2,1)S(1)}, bf16[128,1024]{1,0:T(8,128)(2,1)S(1)}, u32[]{:S(2)}, u32[]{:S(2)}) %collective-permute-start.23) | collective-permute-done | bytes 262176 | tf_op jit(solution)/shard_map/ppermute | solution.py:330
  84.8 5.4 %collective-permute-done.25.refs_9_ = bf16[128,1024]{1,0:T(8,128)(2,1)S(1)} collective-permute-done((bf16[128,1024]{1,0:T(8,128)(2,1)S(1)}, bf16[128,1024]{1,0:T(8,128)(2,1)S(1)}, u32[]{:S(2)}, u32[]{:S(2)}) %collective-permute-start.25) | collective-permute-done | bytes 262176 | tf_op jit(solution)/shard_map/ppermute | solution.py:330
  90.2 4.3 %collective-permute-done.24.refs_8_ = bf16[128,1024]{1,0:T(8,128)(2,1)S(1)} collective-permute-done((bf16[128,1024]{1,0:T(8,128)(2,1)S(1)}, bf16[128,1024]{1,0:T(8,128)(2,1)S(1)}, u32[]{:S(2)}, u32[]{:S(2)}) %collective-permute-start.24) | collective-permute-done | bytes 262176 | tf_op jit(solution)/shard_map/ppermute | solution.py:330
  94.5 5.6 %collective-permute-done.26.refs_11_ = bf16[128,1024]{1,0:T(8,128)(2,1)S(1)} collective-permute-done((bf16[128,1024]{1,0:T(8,128)(2,1)S(1)}, bf16[128,1024]{1,0:T(8,128)(2,1)S(1)}, u32[]{:S(2)}, u32[]{:S(2)}) %collective-permute-start.26) | collective-permute-done | bytes 262176 | tf_op jit(solution)/shard_map/ppermute | solution.py:330
  100.2 2.3 %shard_map.66 = (s16[528,128]{1,0:T(8,128)(2,1)S(1)}, s16[528,128]{1,0:T(8,128)(2,1)S(1)}, s16[528,128]{1,0:T(8,128)(2,1)S(1)}, s16[528,128]{1,0:T(8,128)(2,1)S(...) custom-call(s32[3]{0:T(128)S(1)} %pad_add_fusion.place, ...), custom_call_target="tpu_custom_call" | custom-call | bytes 3600000 | tf_op jit(solution)/shard_map/pallas_call | solution.py:391
  102.6 1.8 %collective-permute-start.28 = (s16[528,128]{1,0:T(8,128)(2,1)S(1)}, s16[528,128]{1,0:T(8,128)(2,1)S(1)}, u32[]{:S(2)}, u32[]{:S(2)}) collective-permute-start(s16[528,128]{1,0:T(8,128)(2,1)S(1)} %get-tuple-element.82), channel_id=1, source_target_pairs={{0,2},{1,3},{2,0},{3,1},{4,6},{5,7},{6,4},{7,5},{8,10},{9,11},{10,... | collective-permute-start | bytes 405512 | tf_op jit(solution)/shard_map/ppermute | solution.py:330
  104.8 1.7 %collective-permute-start.34 = (s16[528,128]{1,0:T(8,128)(2,1)S(1)}, s16[528,128]{1,0:T(8,128)(2,1)S(1)}, u32[]{:S(2)}, u32[]{:S(2)}) collective-permute-start(s16[528,128]{1,0:T(8,128)(2,1)S(1)} %get-tuple-element.91), channel_id=1, source_target_pairs={{0,2},{1,3},{2,0},{3,1},{4,6},{5,7},{6,4},{7,5},{8,10},{9,11},{10,... | collective-permute-start | bytes 405512 | tf_op jit(solution)/shard_map/ppermute | solution.py:330
  106.5 2.5 %collective-permute-done.28.refs_2_ = s16[528,128]{1,0:T(8,128)(2,1)S(1)} collective-permute-done((s16[528,128]{1,0:T(8,128)(2,1)S(1)}, s16[528,128]{1,0:T(8,128)(2,1)S(1)}, u32[]{:S(2)}, u32[]{:S(2)}) %collective-permute-start.28) | collective-permute-done | bytes 135200 | tf_op jit(solution)/shard_map/ppermute | solution.py:330
  109.0 2.1 %collective-permute-done.29.refs_3_ = s16[528,128]{1,0:T(8,128)(2,1)S(1)} collective-permute-done((s16[528,128]{1,0:T(8,128)(2,1)S(1)}, s16[528,128]{1,0:T(8,128)(2,1)S(1)}, u32[]{:S(2)}, u32[]{:S(2)}) %collective-permute-start.29) | collective-permute-done | bytes 135200 | tf_op jit(solution)/shard_map/ppermute | solution.py:330
  111.2 2.1 %shard_map.67 = (s16[528,128]{1,0:T(8,128)(2,1)S(1)}, s16[528,128]{1,0:T(8,128)(2,1)S(1)}, s16[528,128]{1,0:T(8,128)(2,1)S(1)}, s16[528,128]{1,0:T(8,128)(2,1)S(1)}) custom-call(s32[3]{0:T(128)S(1)} %pad_add_fusion.place, f32[32,64,128]{2,1,0:T(8,128)S(1)} %get-tuple-element.100.h, f32[32,64,128]{2,1,0:T(8,128)S(1)} %get-tuple-element.67.s, ...), custom_call_target="tpu_custom_call" | custom-call | bytes 3600000 | tf_op jit(solution)/shard_map/pallas_call | solution.py:401
  113.9 1.7 %collective-permute-start.31 = (s16[528,128]{1,0:T(8,128)(2,1)S(1)}, s16[528,128]{1,0:T(8,128)(2,1)S(1)}, u32[]{:S(2)}, u32[]{:S(2)}) collective-permute-start(s16[528,128]{1,0:T(8,128)(2,1)S(1)} %get-tuple-element.86), channel_id=1, source_target_pairs={{0,2},{1,3},{2,0},{3,1},{4,6},{5,7},{6,4},{7,5},{8,10},{9,11},{10,... | collective-permute-start | bytes 405512 | tf_op jit(solution)/shard_map/ppermute | solution.py:330
  115.6 1.3 %collective-permute-done.35.refs_3_ = s16[528,128]{1,0:T(8,128)(2,1)S(1)} collective-permute-done((s16[528,128]{1,0:T(8,128)(2,1)S(1)}, s16[528,128]{1,0:T(8,128)(2,1)S(1)}, u32[]{:S(2)}, u32[]{:S(2)}) %collective-permute-start.35) | collective-permute-done | bytes 135200 | tf_op jit(solution)/shard_map/ppermute | solution.py:330
  116.9 2.1 %shard_map.68 = (s16[528,128]{1,0:T(8,128)(2,1)S(1)}, s16[528,128]{1,0:T(8,128)(2,1)S(1)}, s16[528,128]{1,0:T(8,128)(2,1)S(1)}, s16[528,128]{1,0:T(8,128)(2,1)S(1)}) custom-call(s32[3]{0:T(128)S(1)} %pad_add_fusion.place, f32[32,64,128]{2,1,0:T(8,128)S(1)} %get-tuple-element.99.h, f32[32,64,128]{2,1,0:T(8,128)S(1)} %get-tuple-element.88.s, ...), custom_call_target="tpu_custom_call" | custom-call | bytes 3600000 | tf_op jit(solution)/shard_map/pallas_call | solution.py:401
  119.7 1.7 %collective-permute-start.37 = (s16[528,128]{1,0:T(8,128)(2,1)S(1)}, s16[528,128]{1,0:T(8,128)(2,1)S(1)}, u32[]{:S(2)}, u32[]{:S(2)}) collective-permute-start(s16[528,128]{1,0:T(8,128)(2,1)S(1)} %get-tuple-element.95), channel_id=1, source_target_pairs={{0,2},{1,3},{2,0},{3,1},{4,6},{5,7},{6,4},{7,5},{8,10},{9,11},{10,... | collective-permute-start | bytes 405512 | tf_op jit(solution)/shard_map/ppermute | solution.py:330
  121.4 1.3 %collective-permute-done.32.refs_3_ = s16[528,128]{1,0:T(8,128)(2,1)S(1)} collective-permute-done((s16[528,128]{1,0:T(8,128)(2,1)S(1)}, s16[528,128]{1,0:T(8,128)(2,1)S(1)}, u32[]{:S(2)}, u32[]{:S(2)}) %collective-permute-start.32) | collective-permute-done | bytes 135200 | tf_op jit(solution)/shard_map/ppermute | solution.py:330
  122.7 3.7 %collective-permute-done.37.refs_6_ = s16[528,128]{1,0:T(8,128)(2,1)S(1)} collective-permute-done((s16[528,128]{1,0:T(8,128)(2,1)S(1)}, s16[528,128]{1,0:T(8,128)(2,1)S(1)}, u32[]{:S(2)}, u32[]{:S(2)}) %collective-permute-start.37) | collective-permute-done | bytes 135200 | tf_op jit(solution)/shard_map/ppermute | solution.py:330
  126.4 2.0 %collective-permute-done.38.refs_7_ = s16[528,128]{1,0:T(8,128)(2,1)S(1)} collective-permute-done((s16[528,128]{1,0:T(8,128)(2,1)S(1)}, s16[528,128]{1,0:T(8,128)(2,1)S(1)}, u32[]{:S(2)}, u32[]{:S(2)}) %collective-permute-start.38) | collective-permute-done | bytes 135200 | tf_op jit(solution)/shard_map/ppermute | solution.py:330
  128.4 3.3 %shard_map.69 = f32[2,256,1024]{2,1,0:T(8,128)} custom-call(s32[3]{0:T(128)S(1)} %pad_add_fusion.place, f32[2,256,1024]{2,1,0:T(8,128)S(1)} %copy-done.1, s16[528,128]{1,0:T(8,128)(2,1)S(1)} %get-tuple-element.84.refs_0_, s16[528,128]{1,0:T(8,128)(2,1)S(1)} %collective-permute-done.30.refs_1_, s16[528,128]{1,0:T(8,128)(2,1)S(1)} %collective-permute-done.31.refs_2_, ...), custom_call_target="tpu_custom_call" | custom-call | bytes 3600000 | tf_op jit(solution)/shard_map/pallas_call | solution.py:408
  (64 shorter events, 6.6 us)
Async XLA Ops:
  0.0 1.6 %copy-start = (f32[2,256,1024]{2,1,0:T(8,128)S(1)}, f32[2,256,1024]{2,1,0:T(8,128)}, u32[]{:S(2)}) copy-start(f32[2,256,1024]{2,1,0:T(8,128)} %density.5) | copy-start | bytes 6291460
  1.6 3.6 %copy-start.1 = (f32[2,256,1024]{2,1,0:T(8,128)S(1)}, f32[2,256,1024]{2,1,0:T(8,128)}, u32[]{:S(2)}) copy-start(f32[2,256,1024]{2,1,0:T(8,128)} %density.5) | copy-start | bytes 6291460
  2.0 29.1 %copy-start.3 = (bf16[256,1024]{1,0:T(8,128)(2,1)}, bf16[256,1024]{1,0:T(8,128)(2,1)S(1)}, u32[]{:S(2)}) copy-start(bf16[256,1024]{1,0:T(8,128)(2,1)S(1)} %get-tuple-element.51.mine) | copy-start | bytes 1572868
  2.0 15.9 %collective-permute-start.8 = (bf16[256,1024]{1,0:T(8,128)(2,1)S(1)}, bf16[256,1024]{1,0:T(8,128)(2,1)}, u32[]{:S(2)}, u32[]{:S(2)}) collective-permute-start(bf16[256,1024]{1,0:T(8,128)(2,1)S(1)} %get-tuple-element.62.mine), channel_id=1, source_target_pairs={{0,4},{1,5},{2,6},{3,7},{4,0},{5,1},{6,2},{7,3},{8,12},{9,13},{10,... | collective-permute-start | bytes 1572872 | tf_op jit(solution)/shard_map/ppermute | solution.py:330
  5.0 23.3 %collective-permute-start = (bf16[256,1024]{1,0:T(8,128)(2,1)S(1)}, bf16[256,1024]{1,0:T(8,128)(2,1)}, u32[]{:S(2)}, u32[]{:S(2)}) collective-permute-start(bf16[256,1024]{1,0:T(8,128)(2,1)S(1)} %get-tuple-element.51.mine), channel_id=1, source_target_pairs={{0,4},{1,5},{2,6},{3,7},{4,0},{5,1},{6,2},{7,3},{8,12},{9,13},{10,... | collective-permute-start | bytes 1572872 | tf_op jit(solution)/shard_map/ppermute | solution.py:330
  5.1 25.0 %copy-start.2 = (f32[2,64,4096]{2,1,0:T(8,128)S(1)}, f32[2,64,4096]{2,1,0:T(8,128)}, u32[]{:S(2)}) copy-start(f32[2,64,4096]{2,1,0:T(8,128)} %h.1) | copy-start | bytes 6291460
  6.3 25.6 %collective-permute-start.2 = (f32[64,2048]{1,0:T(8,128)S(1)}, f32[64,2048]{1,0:T(8,128)S(1)}, u32[]{:S(2)}, u32[]{:S(2)}) collective-permute-start(f32[64,2048]{1,0:T(8,128)S(1)} %get-tuple-element.54), channel_id=1, source_target_pairs={{0,1},{1,0},{2,3},{3,2},{4,5},{5,4},{6,7},{7,6},{8,9},{9,8},{10,11... | collective-permute-start | bytes 1572872 | tf_op jit(solution)/shard_map/ppermute | solution.py:330
  6.4 25.6 %collective-permute-start.3 = (f32[64,2048]{1,0:T(8,128)S(1)}, f32[64,2048]{1,0:T(8,128)S(1)}, u32[]{:S(2)}, u32[]{:S(2)}) collective-permute-start(f32[64,2048]{1,0:T(8,128)S(1)} %get-tuple-element.55), channel_id=1, source_target_pairs={{0,2},{1,3},{2,0},{3,1},{4,6},{5,7},{6,4},{7,5},{8,10},{9,11},{10,... | collective-permute-start | bytes 1572872 | tf_op jit(solution)/shard_map/ppermute | solution.py:330
  8.5 22.7 %copy-start.5 = (bf16[2,4,128,128]{3,2,1,0:T(8,128)(2,1)S(1)}, bf16[2,4,128,128]{3,2,1,0:T(8,128)(2,1)}, u32[]{:S(2)}) copy-start(bf16[2,4,128,128]{3,2,1,0:T(8,128)(2,1)} %coupling.1) | copy-start | bytes 786436
  8.5 22.7 %copy-start.6 = (s32[2,4]{1,0:T(2,128)S(1)}, s32[2,4]{1,0:T(2,128)}, u32[]{:S(2)}) copy-start(s32[2,4]{1,0:T(2,128)} %donors.1) | copy-start | bytes 100
  8.5 22.7 %copy-start.7 = (s32[2]{0:T(128)S(1)}, s32[2]{0:T(128)}, u32[]{:S(2)}) copy-start(s32[2]{0:T(128)} %counts.1) | copy-start | bytes 28
  8.5 23.5 %collective-permute-start.4 = (f32[64,2048]{1,0:T(8,128)S(1)}, f32[64,2048]{1,0:T(8,128)S(1)}, u32[]{:S(2)}, u32[]{:S(2)}) collective-permute-start(f32[64,2048]{1,0:T(8,128)S(1)} %get-tuple-element.56), channel_id=1, source_target_pairs={{0,3},{1,2},{2,1},{3,0},{4,7},{5,6},{6,5},{7,4},{8,11},{9,10},{10,... | collective-permute-start | bytes 1572872 | tf_op jit(solution)/shard_map/ppermute | solution.py:330
  17.9 15.2 %collective-permute-start.9 = (bf16[256,1024]{1,0:T(8,128)(2,1)}, bf16[256,1024]{1,0:T(8,128)(2,1)S(1)}, u32[]{:S(2)}, u32[]{:S(2)}) collective-permute-start(bf16[256,1024]{1,0:T(8,128)(2,1)} %collective-permute-done.8.swap), channel_id=1, source_target_pairs={{0,8},{1,9},{2,10},{3,11},{4,28},{5,29},{6,30},{7,31},{8,16},{9,17... | collective-permute-start | bytes 1572872 | tf_op jit(solution)/shard_map/ppermute | solution.py:330
  28.3 15.1 %collective-permute-start.1 = (bf16[256,1024]{1,0:T(8,128)(2,1)}, bf16[256,1024]{1,0:T(8,128)(2,1)S(1)}, u32[]{:S(2)}, u32[]{:S(2)}) collective-permute-start(bf16[256,1024]{1,0:T(8,128)(2,1)} %collective-permute-done.swap), channel_id=1, source_target_pairs={{0,8},{1,9},{2,10},{3,11},{4,28},{5,29},{6,30},{7,31},{8,16},{9,17... | collective-permute-start | bytes 1572872 | tf_op jit(solution)/shard_map/ppermute | solution.py:330
  35.0 8.4 %copy-start.4 = (bf16[256,1024]{1,0:T(8,128)(2,1)S(1)}, bf16[256,1024]{1,0:T(8,128)(2,1)}, u32[]{:S(2)}) copy-start(bf16[256,1024]{1,0:T(8,128)(2,1)} %copy-done.3) | copy-start | bytes 1572868
  35.1 12.0 %collective-permute-start.10 = (s16[528,128]{1,0:T(8,128)(2,1)S(1)}, s16[528,128]{1,0:T(8,128)(2,1)S(1)}, u32[]{:S(2)}, u32[]{:S(2)}) collective-permute-start(s16[528,128]{1,0:T(8,128)(2,1)S(1)} %get-tuple-element.64), channel_id=1, source_target_pairs={{0,1},{1,0},{2,3},{3,2},{4,5},{5,4},{6,7},{7,6},{8,9},{9,8},{10,11... | collective-permute-start | bytes 405512 | tf_op jit(solution)/shard_map/ppermute | solution.py:330
  35.6 11.9 %collective-permute-start.11 = (s16[528,128]{1,0:T(8,128)(2,1)S(1)}, s16[528,128]{1,0:T(8,128)(2,1)S(1)}, u32[]{:S(2)}, u32[]{:S(2)}) collective-permute-start(s16[528,128]{1,0:T(8,128)(2,1)S(1)} %get-tuple-element.65), channel_id=1, source_target_pairs={{0,2},{1,3},{2,0},{3,1},{4,6},{5,7},{6,4},{7,5},{8,10},{9,11},{10,... | collective-permute-start | bytes 405512 | tf_op jit(solution)/shard_map/ppermute | solution.py:330
  37.2 10.4 %collective-permute-start.12 = (s16[528,128]{1,0:T(8,128)(2,1)S(1)}, s16[528,128]{1,0:T(8,128)(2,1)S(1)}, u32[]{:S(2)}, u32[]{:S(2)}) collective-permute-start(s16[528,128]{1,0:T(8,128)(2,1)S(1)} %get-tuple-element.66), channel_id=1, source_target_pairs={{0,3},{1,2},{2,1},{3,0},{4,7},{5,6},{6,5},{7,4},{8,11},{9,10},{10,... | collective-permute-start | bytes 405512 | tf_op jit(solution)/shard_map/ppermute | solution.py:330
  45.3 2.2 %collective-permute-start.5 = (s16[528,128]{1,0:T(8,128)(2,1)S(1)}, s16[528,128]{1,0:T(8,128)(2,1)S(1)}, u32[]{:S(2)}, u32[]{:S(2)}) collective-permute-start(s16[528,128]{1,0:T(8,128)(2,1)S(1)} %get-tuple-element.59), channel_id=1, source_target_pairs={{0,1},{1,0},{2,3},{3,2},{4,5},{5,4},{6,7},{7,6},{8,9},{9,8},{10,11... | collective-permute-start | bytes 405512 | tf_op jit(solution)/shard_map/ppermute | solution.py:330
  45.4 6.5 %collective-permute-start.6 = (s16[528,128]{1,0:T(8,128)(2,1)S(1)}, s16[528,128]{1,0:T(8,128)(2,1)S(1)}, u32[]{:S(2)}, u32[]{:S(2)}) collective-permute-start(s16[528,128]{1,0:T(8,128)(2,1)S(1)} %get-tuple-element.60), channel_id=1, source_target_pairs={{0,2},{1,3},{2,0},{3,1},{4,6},{5,7},{6,4},{7,5},{8,10},{9,11},{10,... | collective-permute-start | bytes 405512 | tf_op jit(solution)/shard_map/ppermute | solution.py:330
  47.0 6.9 %collective-permute-start.7 = (s16[528,128]{1,0:T(8,128)(2,1)S(1)}, s16[528,128]{1,0:T(8,128)(2,1)S(1)}, u32[]{:S(2)}, u32[]{:S(2)}) collective-permute-start(s16[528,128]{1,0:T(8,128)(2,1)S(1)} %get-tuple-element.61), channel_id=1, source_target_pairs={{0,3},{1,2},{2,1},{3,0},{4,7},{5,6},{6,5},{7,4},{8,11},{9,10},{10,... | collective-permute-start | bytes 405512 | tf_op jit(solution)/shard_map/ppermute | solution.py:330
  55.7 6.0 %collective-permute-start.13 = (bf16[32,2048]{1,0:T(8,128)(2,1)S(1)}, bf16[32,2048]{1,0:T(8,128)(2,1)S(1)}, u32[]{:S(2)}, u32[]{:S(2)}) collective-permute-start(bf16[32,2048]{1,0:T(8,128)(2,1)S(1)} %get-tuple-element.69), channel_id=1, source_target_pairs={{0,1},{1,0},{2,3},{3,2},{4,5},{5,4},{6,7},{7,6},{8,9},{9,8},{10,11... | collective-permute-start | bytes 393224 | tf_op jit(solution)/shard_map/ppermute | solution.py:330
  56.1 6.3 %collective-permute-start.14 = (bf16[32,2048]{1,0:T(8,128)(2,1)S(1)}, bf16[32,2048]{1,0:T(8,128)(2,1)S(1)}, u32[]{:S(2)}, u32[]{:S(2)}) collective-permute-start(bf16[32,2048]{1,0:T(8,128)(2,1)S(1)} %get-tuple-element.70), channel_id=1, source_target_pairs={{0,2},{1,3},{2,0},{3,1},{4,6},{5,7},{6,4},{7,5},{8,10},{9,11},{10,... | collective-permute-start | bytes 393224 | tf_op jit(solution)/shard_map/ppermute | solution.py:330
  57.6 6.7 %collective-permute-start.15 = (bf16[32,2048]{1,0:T(8,128)(2,1)S(1)}, bf16[32,2048]{1,0:T(8,128)(2,1)S(1)}, u32[]{:S(2)}, u32[]{:S(2)}) collective-permute-start(bf16[32,2048]{1,0:T(8,128)(2,1)S(1)} %get-tuple-element.71), channel_id=1, source_target_pairs={{0,3},{1,2},{2,1},{3,0},{4,7},{5,6},{6,5},{7,4},{8,11},{9,10},{10,... | collective-permute-start | bytes 393224 | tf_op jit(solution)/shard_map/ppermute | solution.py:330
  59.6 6.8 %collective-permute-start.20 = (bf16[32,2048]{1,0:T(8,128)(2,1)S(1)}, bf16[32,2048]{1,0:T(8,128)(2,1)S(1)}, u32[]{:S(2)}, u32[]{:S(2)}) collective-permute-start(bf16[32,2048]{1,0:T(8,128)(2,1)S(1)} %get-tuple-element.75), channel_id=1, source_target_pairs={{0,1},{1,0},{2,3},{3,2},{4,5},{5,4},{6,7},{7,6},{8,9},{9,8},{10,11... | collective-permute-start | bytes 393224 | tf_op jit(solution)/shard_map/ppermute | solution.py:330
  60.2 7.9 %collective-permute-start.21 = (bf16[32,2048]{1,0:T(8,128)(2,1)S(1)}, bf16[32,2048]{1,0:T(8,128)(2,1)S(1)}, u32[]{:S(2)}, u32[]{:S(2)}) collective-permute-start(bf16[32,2048]{1,0:T(8,128)(2,1)S(1)} %get-tuple-element.76), channel_id=1, source_target_pairs={{0,2},{1,3},{2,0},{3,1},{4,6},{5,7},{6,4},{7,5},{8,10},{9,11},{10,... | collective-permute-start | bytes 393224 | tf_op jit(solution)/shard_map/ppermute | solution.py:330
  61.7 7.7 %collective-permute-start.22 = (bf16[32,2048]{1,0:T(8,128)(2,1)S(1)}, bf16[32,2048]{1,0:T(8,128)(2,1)S(1)}, u32[]{:S(2)}, u32[]{:S(2)}) collective-permute-start(bf16[32,2048]{1,0:T(8,128)(2,1)S(1)} %get-tuple-element.77), channel_id=1, source_target_pairs={{0,3},{1,2},{2,1},{3,0},{4,7},{5,6},{6,5},{7,4},{8,11},{9,10},{10,... | collective-permute-start | bytes 393224 | tf_op jit(solution)/shard_map/ppermute | solution.py:330
  64.3 9.2 %collective-permute-start.16 = (bf16[128,1024]{1,0:T(8,128)(2,1)S(1)}, bf16[128,1024]{1,0:T(8,128)(2,1)S(1)}, u32[]{:S(2)}, u32[]{:S(2)}) collective-permute-start(bf16[128,1024]{1,0:T(8,128)(2,1)S(1)} %get-tuple-element.72.refs_1_), channel_id=1, source_target_pairs={{0,4},{1,5},{2,6},{3,7},{4,0},{5,1},{6,2},{7,3},{8,12},{9,13},{10,... | collective-permute-start | bytes 786440 | tf_op jit(solution)/shard_map/ppermute | solution.py:330
  65.2 13.9 %collective-permute-start.18 = (bf16[128,1024]{1,0:T(8,128)(2,1)S(1)}, bf16[128,1024]{1,0:T(8,128)(2,1)S(1)}, u32[]{:S(2)}, u32[]{:S(2)}) collective-permute-start(bf16[128,1024]{1,0:T(8,128)(2,1)S(1)} %get-tuple-element.73.refs_4_), channel_id=1, source_target_pairs={{0,4},{1,5},{2,6},{3,7},{4,0},{5,1},{6,2},{7,3},{8,12},{9,13},{10,... | collective-permute-start | bytes 786440 | tf_op jit(solution)/shard_map/ppermute | solution.py:330
  69.5 15.3 %collective-permute-start.23 = (bf16[128,1024]{1,0:T(8,128)(2,1)S(1)}, bf16[128,1024]{1,0:T(8,128)(2,1)S(1)}, u32[]{:S(2)}, u32[]{:S(2)}) collective-permute-start(bf16[128,1024]{1,0:T(8,128)(2,1)S(1)} %get-tuple-element.78.refs_7_), channel_id=1, source_target_pairs={{0,4},{1,5},{2,6},{3,7},{4,0},{5,1},{6,2},{7,3},{8,12},{9,13},{10,... | collective-permute-start | bytes 786440 | tf_op jit(solution)/shard_map/ppermute | solution.py:330
  70.4 19.8 %collective-permute-start.25 = (bf16[128,1024]{1,0:T(8,128)(2,1)S(1)}, bf16[128,1024]{1,0:T(8,128)(2,1)S(1)}, u32[]{:S(2)}, u32[]{:S(2)}) collective-permute-start(bf16[128,1024]{1,0:T(8,128)(2,1)S(1)} %get-tuple-element.79.refs_10_), channel_id=1, source_target_pairs={{0,4},{1,5},{2,6},{3,7},{4,0},{5,1},{6,2},{7,3},{8,12},{9,13},{10,... | collective-permute-start | bytes 786440 | tf_op jit(solution)/shard_map/ppermute | solution.py:330
  73.5 16.7 %collective-permute-start.17 = (bf16[128,1024]{1,0:T(8,128)(2,1)S(1)}, bf16[128,1024]{1,0:T(8,128)(2,1)S(1)}, u32[]{:S(2)}, u32[]{:S(2)}) collective-permute-start(bf16[128,1024]{1,0:T(8,128)(2,1)S(1)} %collective-permute-done.16.refs_0_), channel_id=1, source_target_pairs={{0,8},{1,9},{2,10},{3,11},{4,28},{5,29},{6,30},{7,31},{8,16},{9,17... | collective-permute-start | bytes 786440 | tf_op jit(solution)/shard_map/ppermute | solution.py:330
  79.2 11.1 %collective-permute-start.19 = (bf16[128,1024]{1,0:T(8,128)(2,1)S(1)}, bf16[128,1024]{1,0:T(8,128)(2,1)S(1)}, u32[]{:S(2)}, u32[]{:S(2)}) collective-permute-start(bf16[128,1024]{1,0:T(8,128)(2,1)S(1)} %collective-permute-done.18.refs_3_), channel_id=1, source_target_pairs={{0,8},{1,9},{2,10},{3,11},{4,28},{5,29},{6,30},{7,31},{8,16},{9,17... | collective-permute-start | bytes 786440 | tf_op jit(solution)/shard_map/ppermute | solution.py:330
  84.8 9.8 %collective-permute-start.24 = (bf16[128,1024]{1,0:T(8,128)(2,1)S(1)}, bf16[128,1024]{1,0:T(8,128)(2,1)S(1)}, u32[]{:S(2)}, u32[]{:S(2)}) collective-permute-start(bf16[128,1024]{1,0:T(8,128)(2,1)S(1)} %collective-permute-done.23.refs_6_), channel_id=1, source_target_pairs={{0,8},{1,9},{2,10},{3,11},{4,28},{5,29},{6,30},{7,31},{8,16},{9,17... | collective-permute-start | bytes 786440 | tf_op jit(solution)/shard_map/ppermute | solution.py:330
  90.2 9.9 %collective-permute-start.26 = (bf16[128,1024]{1,0:T(8,128)(2,1)S(1)}, bf16[128,1024]{1,0:T(8,128)(2,1)S(1)}, u32[]{:S(2)}, u32[]{:S(2)}) collective-permute-start(bf16[128,1024]{1,0:T(8,128)(2,1)S(1)} %collective-permute-done.25.refs_9_), channel_id=1, source_target_pairs={{0,8},{1,9},{2,10},{3,11},{4,28},{5,29},{6,30},{7,31},{8,16},{9,17... | collective-permute-start | bytes 786440 | tf_op jit(solution)/shard_map/ppermute | solution.py:330
  102.5 4.0 %collective-permute-start.27 = (s16[528,128]{1,0:T(8,128)(2,1)S(1)}, s16[528,128]{1,0:T(8,128)(2,1)S(1)}, u32[]{:S(2)}, u32[]{:S(2)}) collective-permute-start(s16[528,128]{1,0:T(8,128)(2,1)S(1)} %get-tuple-element.81), channel_id=1, source_target_pairs={{0,1},{1,0},{2,3},{3,2},{4,5},{5,4},{6,7},{7,6},{8,9},{9,8},{10,11... | collective-permute-start | bytes 405512 | tf_op jit(solution)/shard_map/ppermute | solution.py:330
  102.6 6.5 %collective-permute-start.28 = (s16[528,128]{1,0:T(8,128)(2,1)S(1)}, s16[528,128]{1,0:T(8,128)(2,1)S(1)}, u32[]{:S(2)}, u32[]{:S(2)}) collective-permute-start(s16[528,128]{1,0:T(8,128)(2,1)S(1)} %get-tuple-element.82), channel_id=1, source_target_pairs={{0,2},{1,3},{2,0},{3,1},{4,6},{5,7},{6,4},{7,5},{8,10},{9,11},{10,... | collective-permute-start | bytes 405512 | tf_op jit(solution)/shard_map/ppermute | solution.py:330
  104.3 6.8 %collective-permute-start.29 = (s16[528,128]{1,0:T(8,128)(2,1)S(1)}, s16[528,128]{1,0:T(8,128)(2,1)S(1)}, u32[]{:S(2)}, u32[]{:S(2)}) collective-permute-start(s16[528,128]{1,0:T(8,128)(2,1)S(1)} %get-tuple-element.83), channel_id=1, source_target_pairs={{0,3},{1,2},{2,1},{3,0},{4,7},{5,6},{6,5},{7,4},{8,11},{9,10},{10,... | collective-permute-start | bytes 405512 | tf_op jit(solution)/shard_map/ppermute | solution.py:330
  104.5 11.1 %collective-permute-start.33 = (s16[528,128]{1,0:T(8,128)(2,1)S(1)}, s16[528,128]{1,0:T(8,128)(2,1)S(1)}, u32[]{:S(2)}, u32[]{:S(2)}) collective-permute-start(s16[528,128]{1,0:T(8,128)(2,1)S(1)} %get-tuple-element.90), channel_id=1, source_target_pairs={{0,1},{1,0},{2,3},{3,2},{4,5},{5,4},{6,7},{7,6},{8,9},{9,8},{10,11... | collective-permute-start | bytes 405512 | tf_op jit(solution)/shard_map/ppermute | solution.py:330
  104.8 10.8 %collective-permute-start.34 = (s16[528,128]{1,0:T(8,128)(2,1)S(1)}, s16[528,128]{1,0:T(8,128)(2,1)S(1)}, u32[]{:S(2)}, u32[]{:S(2)}) collective-permute-start(s16[528,128]{1,0:T(8,128)(2,1)S(1)} %get-tuple-element.91), channel_id=1, source_target_pairs={{0,2},{1,3},{2,0},{3,1},{4,6},{5,7},{6,4},{7,5},{8,10},{9,11},{10,... | collective-permute-start | bytes 405512 | tf_op jit(solution)/shard_map/ppermute | solution.py:330
  106.5 10.4 %collective-permute-start.35 = (s16[528,128]{1,0:T(8,128)(2,1)S(1)}, s16[528,128]{1,0:T(8,128)(2,1)S(1)}, u32[]{:S(2)}, u32[]{:S(2)}) collective-permute-start(s16[528,128]{1,0:T(8,128)(2,1)S(1)} %get-tuple-element.92), channel_id=1, source_target_pairs={{0,3},{1,2},{2,1},{3,0},{4,7},{5,6},{6,5},{7,4},{8,11},{9,10},{10,... | collective-permute-start | bytes 405512 | tf_op jit(solution)/shard_map/ppermute | solution.py:330
  113.2 8.2 %collective-permute-start.30 = (s16[528,128]{1,0:T(8,128)(2,1)S(1)}, s16[528,128]{1,0:T(8,128)(2,1)S(1)}, u32[]{:S(2)}, u32[]{:S(2)}) collective-permute-start(s16[528,128]{1,0:T(8,128)(2,1)S(1)} %get-tuple-element.85), channel_id=1, source_target_pairs={{0,1},{1,0},{2,3},{3,2},{4,5},{5,4},{6,7},{7,6},{8,9},{9,8},{10,11... | collective-permute-start | bytes 405512 | tf_op jit(solution)/shard_map/ppermute | solution.py:330
  113.9 7.5 %collective-permute-start.31 = (s16[528,128]{1,0:T(8,128)(2,1)S(1)}, s16[528,128]{1,0:T(8,128)(2,1)S(1)}, u32[]{:S(2)}, u32[]{:S(2)}) collective-permute-start(s16[528,128]{1,0:T(8,128)(2,1)S(1)} %get-tuple-element.86), channel_id=1, source_target_pairs={{0,2},{1,3},{2,0},{3,1},{4,6},{5,7},{6,4},{7,5},{8,10},{9,11},{10,... | collective-permute-start | bytes 405512 | tf_op jit(solution)/shard_map/ppermute | solution.py:330
  115.6 7.1 %collective-permute-start.32 = (s16[528,128]{1,0:T(8,128)(2,1)S(1)}, s16[528,128]{1,0:T(8,128)(2,1)S(1)}, u32[]{:S(2)}, u32[]{:S(2)}) collective-permute-start(s16[528,128]{1,0:T(8,128)(2,1)S(1)} %get-tuple-element.87), channel_id=1, source_target_pairs={{0,3},{1,2},{2,1},{3,0},{4,7},{5,6},{6,5},{7,4},{8,11},{9,10},{10,... | collective-permute-start | bytes 405512 | tf_op jit(solution)/shard_map/ppermute | solution.py:330
  119.0 3.7 %collective-permute-start.36 = (s16[528,128]{1,0:T(8,128)(2,1)S(1)}, s16[528,128]{1,0:T(8,128)(2,1)S(1)}, u32[]{:S(2)}, u32[]{:S(2)}) collective-permute-start(s16[528,128]{1,0:T(8,128)(2,1)S(1)} %get-tuple-element.94), channel_id=1, source_target_pairs={{0,1},{1,0},{2,3},{3,2},{4,5},{5,4},{6,7},{7,6},{8,9},{9,8},{10,11... | collective-permute-start | bytes 405512 | tf_op jit(solution)/shard_map/ppermute | solution.py:330
  119.7 6.7 %collective-permute-start.37 = (s16[528,128]{1,0:T(8,128)(2,1)S(1)}, s16[528,128]{1,0:T(8,128)(2,1)S(1)}, u32[]{:S(2)}, u32[]{:S(2)}) collective-permute-start(s16[528,128]{1,0:T(8,128)(2,1)S(1)} %get-tuple-element.95), channel_id=1, source_target_pairs={{0,2},{1,3},{2,0},{3,1},{4,6},{5,7},{6,4},{7,5},{8,10},{9,11},{10,... | collective-permute-start | bytes 405512 | tf_op jit(solution)/shard_map/ppermute | solution.py:330
  121.4 7.0 %collective-permute-start.38 = (s16[528,128]{1,0:T(8,128)(2,1)S(1)}, s16[528,128]{1,0:T(8,128)(2,1)S(1)}, u32[]{:S(2)}, u32[]{:S(2)}) collective-permute-start(s16[528,128]{1,0:T(8,128)(2,1)S(1)} %get-tuple-element.96), channel_id=1, source_target_pairs={{0,3},{1,2},{2,1},{3,0},{4,7},{5,6},{6,5},{7,4},{8,11},{9,10},{10,... | collective-permute-start | bytes 405512 | tf_op jit(solution)/shard_map/ppermute | solution.py:330

commit v2 on v1

--- a/solution.py
+++ b/solution.py
@@ -1,6 +1,5 @@
 import functools
-ACUTS = 2
-ECUTS = 2
+CUTS = 3
 
 import jax
 import jax.numpy as jnp
@@ -29,7 +28,7 @@
         out_shape=out,
         in_specs=specs if specs is not None else [SMEM] + [VMEM] * n_in,
         scratch_shapes=scratch,
-        compiler_params=pltpu.CompilerParams(vmem_limit_bytes=48 * 2**20),
+        compiler_params=pltpu.CompilerParams(vmem_limit_bytes=20 * 2**20),
         cost_estimate=pl.CostEstimate(flops=0, bytes_accessed=int(work * 3.6e6), transcendentals=0),
     )
 
@@ -40,16 +39,14 @@
 
 def rows_of(real, imag):
     low = half_lanes(real.shape)
-    even = jnp.where(low, real, pltpu.roll(imag, NB, 1))
-    odd = jnp.where(low, pltpu.roll(real, NB, 1), imag)
-    return even, odd
+    crossed = pltpu.roll(jnp.where(low, imag, real), NB, 1)
+    return jnp.where(low, real, crossed), jnp.where(low, crossed, imag)
 
 
 def parts_of(even, odd):
     low = half_lanes(even.shape)
-    real = jnp.where(low, even, pltpu.roll(odd, NB, 1))
-    imag = jnp.where(low, pltpu.roll(even, NB, 1), odd)
-    return real, imag
+    crossed = pltpu.roll(jnp.where(low, odd, even), NB, 1)
+    return jnp.where(low, even, crossed), jnp.where(low, crossed, odd)
 
 
 def encode(values, peak):
@@ -76,10 +73,11 @@
 
 
 def round_kernel(density, *outs):
-    width = density.shape[2] // len(outs)
-    for n, out in enumerate(outs):
-        for t in range(width // LANE):
-            cols = slice(n * width + t * LANE, n * width + (t + 1) * LANE)
+    at = 0
+    for out in outs:
+        for t in range(out.shape[1] // LANE // 2):
+            cols = slice(at, at + LANE)
+            at += LANE
             even, odd = rows_of(density[0, :, cols], density[1, :, cols])
             out[:, 2 * t * LANE : (2 * t + 1) * LANE] = even.astype(bf16)
             out[:, (2 * t + 1) * LANE : (2 * t + 2) * LANE] = odd.astype(bf16)
@@ -152,46 +150,51 @@
             out[t * TILE : (t + 1) * TILE, n * TILE : (n + 1) * TILE] = value
 
 
-def field(place, weights, states, codes, powers, outs, chunks):
-    j = place[1]
-    ways = len(outs) // chunks
+def field(place, weights, states, codes, powers, outs):
+    j = place[1]
     sigma = jnp.dot(weights, states, preferred_element_type=f32)
     (code,), power = encode([sigma], jnp.max(jnp.abs(sigma), axis=1, keepdims=True))
     codes[...] = code
     powers[...] = jnp.broadcast_to(power, powers.shape)
     blocks = codes.shape[1] // LANE
     count = (outs[0].shape[0] - PACK) // blocks
-    for c in range(chunks):
-        for k in range(ways):
-            at = pl.ds(pl.multiple_of(((j ^ k) * chunks + c) * count, count), count)
-            out = outs[c * ways + k]
-            for a in range(blocks):
-                out[a * count : (a + 1) * count, :] = codes[at, a * LANE : (a + 1) * LANE]
-            put_power(out, blocks * count, powers[at, :1])
+    for k, out in enumerate(outs):
+        at = pl.ds(pl.multiple_of((j ^ k) * count, count), count)
+        for a in range(blocks):
+            out[a * count : (a + 1) * count, :] = codes[at, a * LANE : (a + 1) * LANE]
+        put_power(out, blocks * count, powers[at, :1])
 
 
 def field_one_kernel(place, dense, mine, swap, passed, *refs):
     outs, (codes, powers) = refs[:-2], refs[-2:]
     states = jnp.concatenate([swap[...], mine[...], passed[...]], 0)
-    field(place, dense[...], states, codes, powers, outs, 1)
-
-
-def field_two_kernel(chunks, cuts, place, dense, *refs):
-    n = 3 * chunks * cuts
-    states, outs, (codes, powers, window) = refs[:n], refs[n:-3], refs[-3:]
-    j = place[1]
-    ways = len(outs) // chunks
-    for c in range(chunks):
-        for q in range(cuts):
-            for b in range(3):
-                ref = states[(c * cuts + q) * 3 + b]
-                count, width = ref.shape[0] // ways, ref.shape[1]
-                for k in range(ways):
-                    at = ((b * ways + (j ^ k)) * chunks + c) * count
-                    window[pl.ds(pl.multiple_of(at, count), count), q * width : (q + 1) * width] = ref[
-                        k * count : (k + 1) * count, :
-                    ]
-    field(place, dense[...], window[...], codes, powers, outs, chunks)
+    field(place, dense[...], states, codes, powers, outs)
+
+
+def rows_for(dense, ways, start, count):
+    band = dense.shape[0] // ways
+    return jnp.concatenate([dense[w * band + start : w * band + start + count, :] for w in range(ways)], 0)
+
+
+def window_field_kernel(spots, start, place, dense, *refs):
+    n = len(spots)
+    states, outs, (window, codes, powers) = refs[:n], refs[n:-3], refs[-3:]
+    j = place[1]
+    ways = len(outs)
+    band = window.shape[0] // 3 // ways
+    for ref, (b, first, lane) in zip(states, spots):
+        count, width = ref.shape[0] // ways, ref.shape[1]
+        for k in range(ways):
+            at = pl.multiple_of((b * ways + (j ^ k)) * band + first, PACK)
+            window[pl.ds(at, count), lane : lane + width] = ref[k * count : (k + 1) * count, :]
+    count = codes.shape[0] // ways
+    field(place, rows_for(dense, ways, start, count), window[...], codes, powers, outs)
+
+
+def field_kernel(start, place, dense, window, *refs):
+    outs, (codes, powers) = refs[:-2], refs[-2:]
+    count = codes.shape[0] // len(outs)
+    field(place, rows_for(dense, len(outs), start, count), window[...], codes, powers, outs)
 
 
 def two_parts(values):
@@ -217,29 +220,30 @@
     return (o[:NB, :LANE] + o[NB:, :LANE]) + (o[:NB, LANE:] + o[NB:, LANE:])
 
 
-def unpack_field(place, cuts, count, first_row, pieces, rows):
+def unpack_field(place, cuts, count, first_row, stride, pieces, rows):
     j = place[1]
     ways = len(pieces) // cuts
-    whole = pieces[0].shape[0] - PACK
-    own = NB // cuts // ways
-    stride = whole // own
+    offset = 0
     for q in range(cuts):
+        whole = pieces[q * ways].shape[0] - PACK
+        own = whole // stride
         for k in range(ways):
             piece = pieces[q * ways + k]
-            first = ((j ^ k) * cuts + q) * own
+            first = (j ^ k) * (NB // ways) + offset
             scale = get_scale(piece, whole, stride)[first_row : first_row + count]
             for a in range(own):
                 at = pl.multiple_of((first + a) * step_of(count), 8)
                 code = piece[a * stride + first_row : a * stride + first_row + count, :]
                 rows[pl.ds(at, count), :] = code.astype(i32).astype(f32) * scale
-
-
-def first_kernel(cuts, n, first_row, place, h, s, *refs):
+        offset += own
+
+
+def first_kernel(cuts, n, first_row, band, place, h, s, *refs):
     pieces, middle, outs, rows, back = refs[:n], refs[n], refs[n + 1 : -2], refs[-2], refs[-1]
     j = place[1]
     count = middle.shape[0]
     step = step_of(count)
-    unpack_field(place, cuts, count, first_row, pieces, rows)
+    unpack_field(place, cuts, count, first_row, band, pieces, rows)
 
     def body(m, carry):
         state = s[m]
@@ -261,7 +265,7 @@
     j = place[1]
     count = h.shape[0]
     step = step_of(count)
-    unpack_field(place, 1, count, 0, pieces, rows)
+    unpack_field(place, 1, count, 0, count, pieces, rows)
 
     def body(m, carry):
         back[pl.ds(m, NB, stride=step), :] = rate(h[m] + rows[pl.ds(m, NB, stride=step), :], s[m])
@@ -279,35 +283,58 @@
         put_power(out, own * count, power)
 
 
-def last_kernel(chunks, place, density, *refs):
-    pieces, out = refs[:-1], refs[-1]
-    j = place[1]
-    ways = len(pieces) // chunks
-    own = 2 * density.shape[2] // LANE
-    count = (pieces[0].shape[0] - PACK) // own
+def last_kernel(chunks, place, *refs):
+    states, pieces, (out, done, sems) = refs[: -3 - len(refs[:-3]) * chunks // (1 + chunks)], refs[:-3], refs[-3:]
+    ways = len(states)
+    pieces = pieces[ways:]
+    j = place[1]
+    own = states[0].shape[1] // LANE
+    count = states[0].shape[0] // chunks
+    copies = []
     for c in range(chunks):
         for k in range(ways):
             piece = pieces[c * ways + k]
+            here = slice(c * count, (c + 1) * count)
             at = pl.ds(pl.multiple_of(((j ^ k) * chunks + c) * count, count), count)
+            spot = (c * ways + k) * count
             scale = get_scale(piece, own * count, count) * step_size
-            block = lambda a: piece[a * count : (a + 1) * count, :].astype(i32).astype(f32) * scale
+
+            def block(a):
+                code = piece[a * count : (a + 1) * count, :]
+                return states[k][here, a * LANE : (a + 1) * LANE] + code.astype(i32).astype(f32) * scale
+
             for t in range(own // 2):
                 real, imag = parts_of(block(2 * t), block(2 * t + 1))
-                cols = slice(t * LANE, (t + 1) * LANE)
-                out[0, at, cols] = density[0, at, cols] + real
-                out[1, at, cols] = density[1, at, cols] + imag
+                done[0, spot : spot + count, t * LANE : (t + 1) * LANE] = real
+                done[1, spot : spot + count, t * LANE : (t + 1) * LANE] = imag
+            copies.append(
+                pltpu.make_async_copy(
+                    done.at[:, spot : spot + count, :], out.at[:, at, :], sems.at[c * ways + k]
+                )
+            )
+            copies[-1].start()
+    for copy in copies:
+        copy.wait()
 
 
 def join_kernel(cuts, *refs):
     pieces, outs = refs[:-cuts], refs[-cuts:]
-    count, width = pieces[0].shape[0], outs[0].shape[1]
-    for q, out in enumerate(outs):
+    count = pieces[0].shape[0]
+    at = 0
+    for out in outs:
+        width = out.shape[1]
         for k, piece in enumerate(pieces):
-            out[k * count : (k + 1) * count, :] = piece[:, q * width : (q + 1) * width]
+            out[k * count : (k + 1) * count, :] = piece[:, at : at + width]
+        at += width
 
 
 def tie(values, *others):
     return lax.optimization_barrier((values, others))[0]
+
+
+def split_rows(own, parts):
+    parts = min(parts, own // 2)
+    return [2 * ((own // 2 + parts - 1 - n) // parts) for n in range(parts)]
 
 
 def local(density, h_bands, coupling, donors, counts):
@@ -339,12 +366,16 @@
         return move(value, lambda a, b: (a - 2 if a % 2 else a + 2, b))
 
     shape = jax.ShapeDtypeStruct
-    cuts = max(n for n in (1, 2, 4) if n <= ACUTS and own % (2 * n) == 0)
-    ecuts = max(n for n in (1, 2, 4) if n <= ECUTS and own % (2 * n) == 0)
-    part = own // cuts
-    mine = call(round_kernel, [shape((mom, part * LANE), bf16)] * cuts, specs=[VMEM])(density)
+    widths = split_rows(own, CUTS)
+    cuts = len(widths)
+    ecuts = 2 if own % 4 == 0 else 1
+    mine = call(round_kernel, [shape((mom, w * LANE), bf16) for w in widths], specs=[VMEM])(density)
     swap = [across(v) for v in mine]
-    passed = [onward(v) for v in swap]
+    passed = []
+    for q, value in enumerate(swap):
+        if q > 1:
+            value = tie(value, passed[q - 2])
+        passed.append(onward(value))
     dense = call(
         functools.partial(coupling_kernel, nka * tiles),
         shape((mom, 3 * mom), bf16),
@@ -357,12 +388,16 @@
     hamilton = call(hamilton_kernel, matrices, [rows], specs=[VMEM])(h_bands)
     hamilton, passed[0] = lax.optimization_barrier((hamilton, passed[0]))
 
+    if cuts > 2:
+        passed[1] = tie(passed[1], states)
     got, fields = [], []
     for q in range(cuts):
+        if q > 1:
+            passed[q] = tie(passed[q], got[(q - 2) * nb : (q - 1) * nb])
         fields = call(
             field_one_kernel,
-            [shape((part * band + PACK, LANE), i16)] * nb,
-            [pltpu.VMEM((mom, part * LANE), i16), pltpu.VMEM((mom, LANE), f32)],
+            [shape((widths[q] * band + PACK, LANE), i16)] * nb,
+            [pltpu.VMEM((mom, widths[q] * LANE), i16), pltpu.VMEM((mom, LANE), f32)],
             n_in=4,
         )(place, dense, mine[q], swap[q], passed[q])
         got += [in_group(v, k) for k, v in enumerate(fields)]
@@ -370,30 +405,36 @@
 
     chunk_rows = pltpu.VMEM((step_of(count) * NB, LANE), f32)
     chunk_shape = shape((count, NB, LANE), f32)
-    middles, parts = [], []
+    middles, parts, spots = [], [], []
     for c in range(chunks):
         at = slice(c * count, (c + 1) * count)
         hc, sc = hamilton[at], state[at]
         middle, *outs = call(
-            functools.partial(first_kernel, cuts, nb * cuts, c * count),
+            functools.partial(first_kernel, cuts, nb * cuts, c * count, band),
             [chunk_shape] + [shape((count, own * LANE), bf16)] * nb,
             [chunk_rows, chunk_rows],
             n_in=2 + nb * cuts,
         )(place, hc, sc, *got)
         middles.append(middle)
         back = [in_group(v, k) for k, v in enumerate(outs)]
-        joined = [shape((nb * count, own // ecuts * LANE), bf16)] * ecuts
-        mine = call(functools.partial(join_kernel, ecuts), joined, specs=[VMEM] * nb)(*back)
-        for q in range(ecuts):
+        ewidths = [own // ecuts] * ecuts
+        joined = [shape((nb * count, w * LANE), bf16) for w in ewidths]
+        mine = call(functools.partial(join_kernel, len(ewidths)), joined, specs=[VMEM] * nb)(*back)
+        for q in range(len(ewidths)):
             swap = across(mine[q])
             parts += [swap, mine[q], onward(swap)]
-
-    fields = call(
-        functools.partial(field_two_kernel, chunks, ecuts),
-        [shape((own * count + PACK, LANE), i16)] * (nb * chunks),
-        [pltpu.VMEM((mom, own * LANE), i16), pltpu.VMEM((mom, LANE), f32), pltpu.VMEM((3 * mom, own * LANE), bf16)],
+            spots += [(b, c * count, sum(ewidths[:q]) * LANE) for b in range(3)]
+
+    pieces = [shape((own * count + PACK, LANE), i16)] * nb
+    room = [pltpu.VMEM((nb * count, own * LANE), i16), pltpu.VMEM((nb * count, LANE), f32)]
+    *fields, window = call(
+        functools.partial(window_field_kernel, spots, 0),
+        pieces + [shape((3 * mom, own * LANE), bf16)],
+        room,
         n_in=1 + len(parts),
     )(place, dense, *parts)
+    for c in range(1, chunks):
+        fields += call(functools.partial(field_kernel, c * count), pieces, room, n_in=2)(place, dense, window)
     got = [[in_group(fields[c * nb + k], k) for k in range(nb)] for c in range(chunks)]
     rates = []
     for c in range(chunks):
@@ -405,9 +446,14 @@
             n_in=2 + nb,
         )(place, hc, sc, *got[c])
         rates += [in_group(v, k) for k, v in enumerate(outs)]
-    return call(
-        functools.partial(last_kernel, chunks), shape(density.shape, f32), n_in=1 + nb * chunks
-    )(place, density, *rates)
+    return pl.pallas_call(
+        functools.partial(last_kernel, chunks),
+        out_shape=shape(density.shape, f32),
+        in_specs=[SMEM] + [VMEM] * (nb + nb * chunks),
+        out_specs=pl.BlockSpec(memory_space=pl.ANY),
+        scratch_shapes=[pltpu.VMEM(density.shape, f32), pltpu.SemaphoreType.DMA((nb * chunks,))],
+        compiler_params=pltpu.CompilerParams(vmem_limit_bytes=20 * 2**20),
+    )(place, *sent, *rates)
 
 
 def solution(mesh):

time: 132 us -> 129 us (0.977)
  waiting for transfers between devices: 77.2 us -> 62.6 us
  starting transfers between devices: 30.2 us -> 42.2 us
    ppermute x39 -> x44, waiting for transfers between devices: 77.2 us -> 62.6 us  [move(): return lax.ppermute(value, ('ka', 'ba'), pairs_of)]
    ppermute x39 -> x44, starting transfers between devices: 30.2 us -> 42.2 us  [move(): return lax.ppermute(value, ('ka', 'ba'), pairs_of)]
    pallas_call x9 -> x11, Pallas kernels: 13.7 us -> 13.4 us  [the longest x2 3.76 us: local(): call(functools.partial(first_kernel, cuts, nb * cuts, c * count, band), [...]
  transfers between devices with their start and end apart: 39 -> 44, of which waited for: 21 -> 24; matrix products, arithmetic and copies ran while one was open for 0% -> 0% of each run, Pallas kernels for 11% -> 11%
where the time goes in v2:
time: 129 us; the launch traced here: 128 us
  waiting for transfers between devices  62.6 us (49%)
  starting transfers between devices  42.2 us (33%)
  Pallas kernels  21.1 us (16%)
  local copies, waits for them, and re-layouts  2.04 us (2%)
    ppermute x44, waiting for transfers between devices, move(): return lax.ppermute(value, ('ka', 'ba'), pairs_of)  62.6 us
    ppermute x44, starting transfers between devices, move(): return lax.ppermute(value, ('ka', 'ba'), pairs_of)  42.2 us
    pallas_call x2, Pallas kernels, local(): call(functools.partial(second_kernel, nb), [shape((own * count + PACK, LA...  4.12 us
    pallas_call x2, Pallas kernels, local(): call(functools.partial(first_kernel, cuts, nb * cuts, c * count, band), [...  3.76 us
    pallas_call x3, Pallas kernels, local(): call(field_one_kernel, [shape((widths[q] * band + PACK, LANE), i16)] * nb...  3.75 us
  transfers between devices with their start and end apart: 44, of which 24 were waited for; matrix products, arithmetic and copies ran while one was open for 0% of the time, Pallas kernels for 11%

profile of v2, /device:TPU:0, one launch (start us, length us, event | category | flops | bytes accessed | tf_op | source)
XLA Modules:
  0.0 128.4 jit_solution(18194955838614880864)
XLA Ops:
  0.1 1.6 %copy-done = f32[2,256,1024]{2,1,0:T(8,128)S(1)} copy-done((f32[2,256,1024]{2,1,0:T(8,128)S(1)}, f32[2,256,1024]{2,1,0:T(8,128)}, u32[]{:S(2)}) %copy-start) | copy-done | bytes 2097176
  3.7 3.0 %collective-permute-start = (bf16[256,768]{1,0:T(8,128)(2,1)S(1)}, bf16[256,768]{1,0:T(8,128)(2,1)S(1)}, u32[]{:S(2)}, u32[]{:S(2)}) collective-permute-start(bf16[256,768]{1,0:T(8,128)(2,1)S(1)} %get-tuple-element.64.mine), channel_id=1, source_target_pairs={{0,4},{1,5},{2,6},{3,7},{4,0},{5,1},{6,2},{7,3},{8,12},{9,13},{10,... | collective-permute-start | bytes 1179656 | tf_op jit(solution)/shard_map/ppermute | solution.py:357
  6.8 2.0 %collective-permute-start.3 = (f32[64,2048]{1,0:T(8,128)S(1)}, f32[64,2048]{1,0:T(8,128)S(1)}, u32[]{:S(2)}, u32[]{:S(2)}) collective-permute-start(f32[64,2048]{1,0:T(8,128)S(1)} %get-tuple-element.62.refs_2_), channel_id=1, source_target_pairs={{0,2},{1,3},{2,0},{3,1},{4,6},{5,7},{6,4},{7,5},{8,10},{9,11},{10,... | collective-permute-start | bytes 1572872 | tf_op jit(solution)/shard_map/ppermute | solution.py:357
  8.7 7.9 %collective-permute-done.swap = bf16[256,768]{1,0:T(8,128)(2,1)S(1)} collective-permute-done((bf16[256,768]{1,0:T(8,128)(2,1)S(1)}, bf16[256,768]{1,0:T(8,128)(2,1)S(1)}, u32[]{:S(2)}, u32[]{:S(2)}) %collective-permute-start) | collective-permute-done | bytes 393248 | tf_op jit(solution)/shard_map/ppermute | solution.py:357
  16.6 2.1 %collective-permute-start.1 = (bf16[256,768]{1,0:T(8,128)(2,1)S(1)}, bf16[256,768]{1,0:T(8,128)(2,1)S(1)}, u32[]{:S(2)}, u32[]{:S(2)}) collective-permute-start(bf16[256,768]{1,0:T(8,128)(2,1)S(1)} %collective-permute-done.swap), channel_id=1, source_target_pairs={{0,8},{1,9},{2,10},{3,11},{4,28},{5,29},{6,30},{7,31},{8,16},{9,17... | collective-permute-start | bytes 1179656 | tf_op jit(solution)/shard_map/ppermute | solution.py:357
  18.8 5.5 %collective-permute-done.8.swap = bf16[256,768]{1,0:T(8,128)(2,1)S(1)} collective-permute-done((bf16[256,768]{1,0:T(8,128)(2,1)S(1)}, bf16[256,768]{1,0:T(8,128)(2,1)S(1)}, u32[]{:S(2)}, u32[]{:S(2)}) %collective-permute-start.8) | collective-permute-done | bytes 393248 | tf_op jit(solution)/shard_map/ppermute | solution.py:357
  24.3 1.8 %collective-permute-start.9 = (bf16[256,768]{1,0:T(8,128)(2,1)S(1)}, bf16[256,768]{1,0:T(8,128)(2,1)S(1)}, u32[]{:S(2)}, u32[]{:S(2)}) collective-permute-start(bf16[256,768]{1,0:T(8,128)(2,1)S(1)} %collective-permute-done.8.swap), channel_id=1, source_target_pairs={{0,8},{1,9},{2,10},{3,11},{4,28},{5,29},{6,30},{7,31},{8,16},{9,17... | collective-permute-start | bytes 1179656 | tf_op jit(solution)/shard_map/ppermute | solution.py:357
  26.1 3.6 %collective-permute-start.13 = (bf16[256,512]{1,0:T(8,128)(2,1)S(1)}, bf16[256,512]{1,0:T(8,128)(2,1)S(1)}, u32[]{:S(2)}, u32[]{:S(2)}) collective-permute-start(bf16[256,512]{1,0:T(8,128)(2,1)S(1)} %get-tuple-element.77.mine), channel_id=1, source_target_pairs={{0,4},{1,5},{2,6},{3,7},{4,0},{5,1},{6,2},{7,3},{8,12},{9,13},{10,... | collective-permute-start | bytes 786440 | tf_op jit(solution)/shard_map/ppermute | solution.py:357
  31.3 1.1 shard_map.58
  32.4 2.5 %collective-permute-done.13.swap = bf16[256,512]{1,0:T(8,128)(2,1)S(1)} collective-permute-done((bf16[256,512]{1,0:T(8,128)(2,1)S(1)}, bf16[256,512]{1,0:T(8,128)(2,1)S(1)}, u32[]{:S(2)}, u32[]{:S(2)}) %collective-permute-start.13) | collective-permute-done | bytes 262176 | tf_op jit(solution)/shard_map/ppermute | solution.py:357
  34.9 1.3 %shard_map.60 = (s16[400,128]{1,0:T(8,128)(2,1)S(1)}, s16[400,128]{1,0:T(8,128)(2,1)S(1)}, s16[400,128]{1,0:T(8,128)(2,1)S(1)}, s16[400,128]{1,0:T(8,128)(2,1)S(1)}) custom-call(s32[3]{0:T(128)S(1)} %pad_add_fusion.place, bf16[256,768]{1,0:T(8,128)(2,1)S(1)} %shard_map.59.dense, bf16[256,768]{1,0:T(8,128)(2,1)S(1)} %get-tuple-element.64.mine, ...), custom_call_target="tpu_custom_call" | custom-call | bytes 3600000 | tf_op jit(solution)/shard_map/pallas_call | solution.py:397
  36.3 1.6 %collective-permute-start.6 = (s16[400,128]{1,0:T(8,128)(2,1)S(1)}, s16[400,128]{1,0:T(8,128)(2,1)S(1)}, u32[]{:S(2)}, u32[]{:S(2)}) collective-permute-start(s16[400,128]{1,0:T(8,128)(2,1)S(1)} %get-tuple-element.69), channel_id=1, source_target_pairs={{0,2},{1,3},{2,0},{3,1},{4,6},{5,7},{6,4},{7,5},{8,10},{9,11},{10,... | collective-permute-start | bytes 307208 | tf_op jit(solution)/shard_map/ppermute | solution.py:357
  38.2 1.3 %shard_map.61 = (s16[400,128]{1,0:T(8,128)(2,1)S(1)}, s16[400,128]{1,0:T(8,128)(2,1)S(1)}, s16[400,128]{1,0:T(8,128)(2,1)S(1)}, s16[400,128]{1,0:T(8,128)(2,1)S(1)}) custom-call(s32[3]{0:T(128)S(1)} %pad_add_fusion.place, bf16[256,768]{1,0:T(8,128)(2,1)S(1)} %shard_map.59.dense, bf16[256,768]{1,0:T(8,128)(2,1)S(1)} %get-tuple-element.71.mine, ...), custom_call_target="tpu_custom_call" | custom-call | bytes 3600000 | tf_op jit(solution)/shard_map/pallas_call | solution.py:397
  40.1 1.6 %collective-permute-start.11 = (s16[400,128]{1,0:T(8,128)(2,1)S(1)}, s16[400,128]{1,0:T(8,128)(2,1)S(1)}, u32[]{:S(2)}, u32[]{:S(2)}) collective-permute-start(s16[400,128]{1,0:T(8,128)(2,1)S(1)} %get-tuple-element.75), channel_id=1, source_target_pairs={{0,2},{1,3},{2,0},{3,1},{4,6},{5,7},{6,4},{7,5},{8,10},{9,11},{10,... | collective-permute-start | bytes 307208 | tf_op jit(solution)/shard_map/ppermute | solution.py:357
  43.4 1.1 shard_map.62
  45.3 1.5 %collective-permute-start.16 = (s16[272,128]{1,0:T(8,128)(2,1)S(1)}, s16[272,128]{1,0:T(8,128)(2,1)S(1)}, u32[]{:S(2)}, u32[]{:S(2)}) collective-permute-start(s16[272,128]{1,0:T(8,128)(2,1)S(1)} %get-tuple-element.82), channel_id=1, source_target_pairs={{0,2},{1,3},{2,0},{3,1},{4,6},{5,7},{6,4},{7,5},{8,10},{9,11},{10,... | collective-permute-start | bytes 208904 | tf_op jit(solution)/shard_map/ppermute | solution.py:357
  47.8 1.9 %collective-permute-done.16.refs_10_ = s16[272,128]{1,0:T(8,128)(2,1)S(1)} collective-permute-done((s16[272,128]{1,0:T(8,128)(2,1)S(1)}, s16[272,128]{1,0:T(8,128)(2,1)S(1)}, u32[]{:S(2)}, u32[]{:S(2)}) %collective-permute-start.16) | collective-permute-done | bytes 69664 | tf_op jit(solution)/shard_map/ppermute | solution.py:357
  49.7 1.6 %collective-permute-done.17.refs_11_ = s16[272,128]{1,0:T(8,128)(2,1)S(1)} collective-permute-done((s16[272,128]{1,0:T(8,128)(2,1)S(1)}, s16[272,128]{1,0:T(8,128)(2,1)S(1)}, u32[]{:S(2)}, u32[]{:S(2)}) %collective-permute-start.17) | collective-permute-done | bytes 69664 | tf_op jit(solution)/shard_map/ppermute | solution.py:357
  51.3 1.9 %shard_map.63 = (f32[32,64,128]{2,1,0:T(8,128)S(1)}, bf16[32,2048]{1,0:T(8,128)(2,1)S(1)}, bf16[32,2048]{1,0:T(8,128)(2,1)S(1)}, bf16[32,2048]{1,0:T(8,128)(2,1)S(1)}, bf16[32,2048]{1,0:T(8,128)(2,1)S(1)}) custom-call(s32[3]{0:T(128)S(1)} %pad_add_fusion.place, f32[32,64,128]{2,1,0:T(8,128)S(1)} %get-tuple-element.118.h, ...), custom_call_target="tpu_custom_call" | custom-call | bytes 3600000 | tf_op jit(solution)/shard_map/pallas_call | solution.py:412
  53.3 1.2 collective-permute-start.19
  55.1 1.9 %shard_map.65 = (f32[32,64,128]{2,1,0:T(8,128)S(1)}, bf16[32,2048]{1,0:T(8,128)(2,1)S(1)}, bf16[32,2048]{1,0:T(8,128)(2,1)S(1)}, bf16[32,2048]{1,0:T(8,128)(2,1)S(1)}, bf16[32,2048]{1,0:T(8,128)(2,1)S(1)}) custom-call(s32[3]{0:T(128)S(1)} %pad_add_fusion.place, f32[32,64,128]{2,1,0:T(8,128)S(1)} %get-tuple-element.117.h, ...), custom_call_target="tpu_custom_call" | custom-call | bytes 3600000 | tf_op jit(solution)/shard_map/pallas_call | solution.py:412
  57.4 1.2 collective-permute-start.26
  59.6 1.9 %collective-permute-done.20.refs_3_ = bf16[32,2048]{1,0:T(8,128)(2,1)S(1)} collective-permute-done((bf16[32,2048]{1,0:T(8,128)(2,1)S(1)}, bf16[32,2048]{1,0:T(8,128)(2,1)S(1)}, u32[]{:S(2)}, u32[]{:S(2)}) %collective-permute-start.20) | collective-permute-done | bytes 131104 | tf_op jit(solution)/shard_map/ppermute | solution.py:357
  61.5 2.6 %collective-permute-start.21 = (bf16[128,1024]{1,0:T(8,128)(2,1)S(1)}, bf16[128,1024]{1,0:T(8,128)(2,1)S(1)}, u32[]{:S(2)}, u32[]{:S(2)}) collective-permute-start(bf16[128,1024]{1,0:T(8,128)(2,1)S(1)} %get-tuple-element.89.refs_1_), channel_id=1, source_target_pairs={{0,4},{1,5},{2,6},{3,7},{4,0},{5,1},{6,2},{7,3},{8,12},{9,13},{10,... | collective-permute-start | bytes 786440 | tf_op jit(solution)/shard_map/ppermute | solution.py:357
  65.2 1.9 %collective-permute-done.27.refs_3_ = bf16[32,2048]{1,0:T(8,128)(2,1)S(1)} collective-permute-done((bf16[32,2048]{1,0:T(8,128)(2,1)S(1)}, bf16[32,2048]{1,0:T(8,128)(2,1)S(1)}, u32[]{:S(2)}, u32[]{:S(2)}) %collective-permute-start.27) | collective-permute-done | bytes 131104 | tf_op jit(solution)/shard_map/ppermute | solution.py:357
  67.2 2.6 %collective-permute-start.28 = (bf16[128,1024]{1,0:T(8,128)(2,1)S(1)}, bf16[128,1024]{1,0:T(8,128)(2,1)S(1)}, u32[]{:S(2)}, u32[]{:S(2)}) collective-permute-start(bf16[128,1024]{1,0:T(8,128)(2,1)S(1)} %get-tuple-element.95.refs_7_), channel_id=1, source_target_pairs={{0,4},{1,5},{2,6},{3,7},{4,0},{5,1},{6,2},{7,3},{8,12},{9,13},{10,... | collective-permute-start | bytes 786440 | tf_op jit(solution)/shard_map/ppermute | solution.py:357
  69.8 1.4 %collective-permute-done.21.refs_0_ = bf16[128,1024]{1,0:T(8,128)(2,1)S(1)} collective-permute-done((bf16[128,1024]{1,0:T(8,128)(2,1)S(1)}, bf16[128,1024]{1,0:T(8,128)(2,1)S(1)}, u32[]{:S(2)}, u32[]{:S(2)}) %collective-permute-start.21) | collective-permute-done | bytes 262176 | tf_op jit(solution)/shard_map/ppermute | solution.py:357
  71.2 1.3 collective-permute-start.22
  72.5 4.4 %collective-permute-done.23.refs_3_ = bf16[128,1024]{1,0:T(8,128)(2,1)S(1)} collective-permute-done((bf16[128,1024]{1,0:T(8,128)(2,1)S(1)}, bf16[128,1024]{1,0:T(8,128)(2,1)S(1)}, u32[]{:S(2)}, u32[]{:S(2)}) %collective-permute-start.23) | collective-permute-done | bytes 262176 | tf_op jit(solution)/shard_map/ppermute | solution.py:357
  76.8 1.3 collective-permute-start.24
  78.1 4.4 %collective-permute-done.28.refs_6_ = bf16[128,1024]{1,0:T(8,128)(2,1)S(1)} collective-permute-done((bf16[128,1024]{1,0:T(8,128)(2,1)S(1)}, bf16[128,1024]{1,0:T(8,128)(2,1)S(1)}, u32[]{:S(2)}, u32[]{:S(2)}) %collective-permute-start.28) | collective-permute-done | bytes 262176 | tf_op jit(solution)/shard_map/ppermute | solution.py:357
  82.5 1.3 collective-permute-start.29
  83.7 4.4 %collective-permute-done.30.refs_9_ = bf16[128,1024]{1,0:T(8,128)(2,1)S(1)} collective-permute-done((bf16[128,1024]{1,0:T(8,128)(2,1)S(1)}, bf16[128,1024]{1,0:T(8,128)(2,1)S(1)}, u32[]{:S(2)}, u32[]{:S(2)}) %collective-permute-start.30) | collective-permute-done | bytes 262176 | tf_op jit(solution)/shard_map/ppermute | solution.py:357
  88.1 1.3 collective-permute-start.31
  89.3 3.4 %collective-permute-done.29.refs_8_ = bf16[128,1024]{1,0:T(8,128)(2,1)S(1)} collective-permute-done((bf16[128,1024]{1,0:T(8,128)(2,1)S(1)}, bf16[128,1024]{1,0:T(8,128)(2,1)S(1)}, u32[]{:S(2)}, u32[]{:S(2)}) %collective-permute-start.29) | collective-permute-done | bytes 262176 | tf_op jit(solution)/shard_map/ppermute | solution.py:357
  92.7 5.6 %collective-permute-done.31.refs_11_ = bf16[128,1024]{1,0:T(8,128)(2,1)S(1)} collective-permute-done((bf16[128,1024]{1,0:T(8,128)(2,1)S(1)}, bf16[128,1024]{1,0:T(8,128)(2,1)S(1)}, u32[]{:S(2)}, u32[]{:S(2)}) %collective-permute-start.31) | collective-permute-done | bytes 262176 | tf_op jit(solution)/shard_map/ppermute | solution.py:357
  98.3 1.6 %shard_map.67 = (s16[528,128]{1,0:T(8,128)(2,1)S(1)}, s16[528,128]{1,0:T(8,128)(2,1)S(1)}, s16[528,128]{1,0:T(8,128)(2,1)S(1)}, s16[528,128]{1,0:T(8,128)(2,1)S(1)}, bf16[768,2048]{1,0:T(8,128)(2,1)S(1)}) custom-call(s32[3]{0:T(128)S(1)} %pad_add_fusion.place, bf16[256,768]{1,0:T(8,128)(2,1)S(1)} %shard_map.59.dense, ...), custom_call_target="tpu_custom_call" | custom-call | bytes 3600000 | tf_op jit(solution)/shard_map/pallas_call | solution.py:430
  100.9 1.1 collective-permute-start.34
  101.9 1.4 %shard_map.69 = (s16[528,128]{1,0:T(8,128)(2,1)S(1)}, s16[528,128]{1,0:T(8,128)(2,1)S(1)}, s16[528,128]{1,0:T(8,128)(2,1)S(1)}, s16[528,128]{1,0:T(8,128)(2,1)S(1)}) custom-call(s32[3]{0:T(128)S(1)} %pad_add_fusion.place, bf16[256,768]{1,0:T(8,128)(2,1)S(1)} %shard_map.59.dense, bf16[768,2048]{1,0:T(8,128)(2,1)S(1)} %get-tuple-element.106.window), custom_call_target="tpu_custom_call" | custom-call | bytes 3600000 | tf_op jit(solution)/shard_map/pallas_call | solution.py:437
  105.3 1.2 collective-permute-done.33.refs_2_
  106.5 2.0 %collective-permute-done.34.refs_3_ = s16[528,128]{1,0:T(8,128)(2,1)S(1)} collective-permute-done((s16[528,128]{1,0:T(8,128)(2,1)S(1)}, s16[528,128]{1,0:T(8,128)(2,1)S(1)}, u32[]{:S(2)}, u32[]{:S(2)}) %collective-permute-start.34) | collective-permute-done | bytes 135200 | tf_op jit(solution)/shard_map/ppermute | solution.py:357
  108.5 2.1 %shard_map.68 = (s16[528,128]{1,0:T(8,128)(2,1)S(1)}, s16[528,128]{1,0:T(8,128)(2,1)S(1)}, s16[528,128]{1,0:T(8,128)(2,1)S(1)}, s16[528,128]{1,0:T(8,128)(2,1)S(1)}) custom-call(s32[3]{0:T(128)S(1)} %pad_add_fusion.place, f32[32,64,128]{2,1,0:T(8,128)S(1)} %get-tuple-element.118.h, f32[32,64,128]{2,1,0:T(8,128)S(1)} %get-tuple-element.84.s, ...), custom_call_target="tpu_custom_call" | custom-call | bytes 3600000 | tf_op jit(solution)/shard_map/pallas_call | solution.py:442
  112.8 1.5 %collective-permute-done.40.refs_3_ = s16[528,128]{1,0:T(8,128)(2,1)S(1)} collective-permute-done((s16[528,128]{1,0:T(8,128)(2,1)S(1)}, s16[528,128]{1,0:T(8,128)(2,1)S(1)}, u32[]{:S(2)}, u32[]{:S(2)}) %collective-permute-start.40) | collective-permute-done | bytes 135200 | tf_op jit(solution)/shard_map/ppermute | solution.py:357
  114.3 2.1 %shard_map.70 = (s16[528,128]{1,0:T(8,128)(2,1)S(1)}, s16[528,128]{1,0:T(8,128)(2,1)S(1)}, s16[528,128]{1,0:T(8,128)(2,1)S(1)}, s16[528,128]{1,0:T(8,128)(2,1)S(1)}) custom-call(s32[3]{0:T(128)S(1)} %pad_add_fusion.place, f32[32,64,128]{2,1,0:T(8,128)S(1)} %get-tuple-element.117.h, f32[32,64,128]{2,1,0:T(8,128)S(1)} %get-tuple-element.105.s, ...), custom_call_target="tpu_custom_call" | custom-call | bytes 3600000 | tf_op jit(solution)/shard_map/pallas_call | solution.py:442
  118.6 1.5 %collective-permute-done.37.refs_7_ = s16[528,128]{1,0:T(8,128)(2,1)S(1)} collective-permute-done((s16[528,128]{1,0:T(8,128)(2,1)S(1)}, s16[528,128]{1,0:T(8,128)(2,1)S(1)}, u32[]{:S(2)}, u32[]{:S(2)}) %collective-permute-start.37) | collective-permute-done | bytes 135200 | tf_op jit(solution)/shard_map/ppermute | solution.py:357
  120.1 3.8 %collective-permute-done.42.refs_10_ = s16[528,128]{1,0:T(8,128)(2,1)S(1)} collective-permute-done((s16[528,128]{1,0:T(8,128)(2,1)S(1)}, s16[528,128]{1,0:T(8,128)(2,1)S(1)}, u32[]{:S(2)}, u32[]{:S(2)}) %collective-permute-start.42) | collective-permute-done | bytes 135200 | tf_op jit(solution)/shard_map/ppermute | solution.py:357
  123.9 2.0 %collective-permute-done.43.refs_11_ = s16[528,128]{1,0:T(8,128)(2,1)S(1)} collective-permute-done((s16[528,128]{1,0:T(8,128)(2,1)S(1)}, s16[528,128]{1,0:T(8,128)(2,1)S(1)}, u32[]{:S(2)}, u32[]{:S(2)}) %collective-permute-start.43) | collective-permute-done | bytes 135200 | tf_op jit(solution)/shard_map/ppermute | solution.py:357
  125.9 2.3 %shard_map.71 = f32[2,256,1024]{2,1,0:T(8,128)} custom-call(s32[3]{0:T(128)S(1)} %pad_add_fusion.place, f32[64,2048]{1,0:T(8,128)S(1)} %get-tuple-element.60.refs_0_, f32[64,2048]{1,0:T(8,128)S(1)} %get-tuple-element.61.refs_1_, f32[64,2048]{1,0:T(8,128)S(1)} %get-tuple-element.62.refs_2_, f32[64,2048]{1,0:T(8,128)S(1)} %get-tuple-element.63.refs_3_, ...), custom_call_target="tpu_custom_call" | custom-call | tf_op jit(solution)/shard_map/pallas_call | solution.py:449
  (72 shorter events, 18.8 us)
Async XLA Ops:
  1.7 28.0 %copy-start.2 = (f32[2,64,4096]{2,1,0:T(8,128)S(1)}, f32[2,64,4096]{2,1,0:T(8,128)}, u32[]{:S(2)}) copy-start(f32[2,64,4096]{2,1,0:T(8,128)} %h.1) | copy-start | bytes 6291460
  2.6 23.5 %collective-permute-start.2 = (f32[64,2048]{1,0:T(8,128)S(1)}, f32[64,2048]{1,0:T(8,128)S(1)}, u32[]{:S(2)}, u32[]{:S(2)}) collective-permute-start(f32[64,2048]{1,0:T(8,128)S(1)} %get-tuple-element.61.refs_1_), channel_id=1, source_target_pairs={{0,1},{1,0},{2,3},{3,2},{4,5},{5,4},{6,7},{7,6},{8,9},{9,8},{10,11... | collective-permute-start | bytes 1572872 | tf_op jit(solution)/shard_map/ppermute | solution.py:357
  3.7 12.9 %collective-permute-start = (bf16[256,768]{1,0:T(8,128)(2,1)S(1)}, bf16[256,768]{1,0:T(8,128)(2,1)S(1)}, u32[]{:S(2)}, u32[]{:S(2)}) collective-permute-start(bf16[256,768]{1,0:T(8,128)(2,1)S(1)} %get-tuple-element.64.mine), channel_id=1, source_target_pairs={{0,4},{1,5},{2,6},{3,7},{4,0},{5,1},{6,2},{7,3},{8,12},{9,13},{10,... | collective-permute-start | bytes 1179656 | tf_op jit(solution)/shard_map/ppermute | solution.py:357
  6.7 17.6 %collective-permute-start.8 = (bf16[256,768]{1,0:T(8,128)(2,1)S(1)}, bf16[256,768]{1,0:T(8,128)(2,1)S(1)}, u32[]{:S(2)}, u32[]{:S(2)}) collective-permute-start(bf16[256,768]{1,0:T(8,128)(2,1)S(1)} %get-tuple-element.71.mine), channel_id=1, source_target_pairs={{0,4},{1,5},{2,6},{3,7},{4,0},{5,1},{6,2},{7,3},{8,12},{9,13},{10,... | collective-permute-start | bytes 1179656 | tf_op jit(solution)/shard_map/ppermute | solution.py:357
  6.8 24.6 %collective-permute-start.3 = (f32[64,2048]{1,0:T(8,128)S(1)}, f32[64,2048]{1,0:T(8,128)S(1)}, u32[]{:S(2)}, u32[]{:S(2)}) collective-permute-start(f32[64,2048]{1,0:T(8,128)S(1)} %get-tuple-element.62.refs_2_), channel_id=1, source_target_pairs={{0,2},{1,3},{2,0},{3,1},{4,6},{5,7},{6,4},{7,5},{8,10},{9,11},{10,... | collective-permute-start | bytes 1572872 | tf_op jit(solution)/shard_map/ppermute | solution.py:357
  8.7 22.6 %collective-permute-start.4 = (f32[64,2048]{1,0:T(8,128)S(1)}, f32[64,2048]{1,0:T(8,128)S(1)}, u32[]{:S(2)}, u32[]{:S(2)}) collective-permute-start(f32[64,2048]{1,0:T(8,128)S(1)} %get-tuple-element.63.refs_3_), channel_id=1, source_target_pairs={{0,3},{1,2},{2,1},{3,0},{4,7},{5,6},{6,5},{7,4},{8,11},{9,10},{10,... | collective-permute-start | bytes 1572872 | tf_op jit(solution)/shard_map/ppermute | solution.py:357
  16.6 18.3 %collective-permute-start.1 = (bf16[256,768]{1,0:T(8,128)(2,1)S(1)}, bf16[256,768]{1,0:T(8,128)(2,1)S(1)}, u32[]{:S(2)}, u32[]{:S(2)}) collective-permute-start(bf16[256,768]{1,0:T(8,128)(2,1)S(1)} %collective-permute-done.swap), channel_id=1, source_target_pairs={{0,8},{1,9},{2,10},{3,11},{4,28},{5,29},{6,30},{7,31},{8,16},{9,17... | collective-permute-start | bytes 1179656 | tf_op jit(solution)/shard_map/ppermute | solution.py:357
  24.3 13.9 %collective-permute-start.9 = (bf16[256,768]{1,0:T(8,128)(2,1)S(1)}, bf16[256,768]{1,0:T(8,128)(2,1)S(1)}, u32[]{:S(2)}, u32[]{:S(2)}) collective-permute-start(bf16[256,768]{1,0:T(8,128)(2,1)S(1)} %collective-permute-done.8.swap), channel_id=1, source_target_pairs={{0,8},{1,9},{2,10},{3,11},{4,28},{5,29},{6,30},{7,31},{8,16},{9,17... | collective-permute-start | bytes 1179656 | tf_op jit(solution)/shard_map/ppermute | solution.py:357
  26.1 4.4 %copy-start.3 = (bf16[2,4,128,128]{3,2,1,0:T(8,128)(2,1)S(1)}, bf16[2,4,128,128]{3,2,1,0:T(8,128)(2,1)}, u32[]{:S(2)}) copy-start(bf16[2,4,128,128]{3,2,1,0:T(8,128)(2,1)} %coupling.1) | copy-start | bytes 786436
  26.1 4.4 %copy-start.4 = (s32[2,4]{1,0:T(2,128)S(1)}, s32[2,4]{1,0:T(2,128)}, u32[]{:S(2)}) copy-start(s32[2,4]{1,0:T(2,128)} %donors.1) | copy-start | bytes 100
  26.1 4.4 %copy-start.5 = (s32[2]{0:T(128)S(1)}, s32[2]{0:T(128)}, u32[]{:S(2)}) copy-start(s32[2]{0:T(128)} %counts.1) | copy-start | bytes 28
  26.1 8.8 %collective-permute-start.13 = (bf16[256,512]{1,0:T(8,128)(2,1)S(1)}, bf16[256,512]{1,0:T(8,128)(2,1)S(1)}, u32[]{:S(2)}, u32[]{:S(2)}) collective-permute-start(bf16[256,512]{1,0:T(8,128)(2,1)S(1)} %get-tuple-element.77.mine), channel_id=1, source_target_pairs={{0,4},{1,5},{2,6},{3,7},{4,0},{5,1},{6,2},{7,3},{8,12},{9,13},{10,... | collective-permute-start | bytes 786440 | tf_op jit(solution)/shard_map/ppermute | solution.py:357
  34.9 8.4 %collective-permute-start.14 = (bf16[256,512]{1,0:T(8,128)(2,1)S(1)}, bf16[256,512]{1,0:T(8,128)(2,1)S(1)}, u32[]{:S(2)}, u32[]{:S(2)}) collective-permute-start(bf16[256,512]{1,0:T(8,128)(2,1)S(1)} %collective-permute-done.13.swap), channel_id=1, source_target_pairs={{0,8},{1,9},{2,10},{3,11},{4,28},{5,29},{6,30},{7,31},{8,16},{9,17... | collective-permute-start | bytes 786440 | tf_op jit(solution)/shard_map/ppermute | solution.py:357
  36.2 3.8 %collective-permute-start.5 = (s16[400,128]{1,0:T(8,128)(2,1)S(1)}, s16[400,128]{1,0:T(8,128)(2,1)S(1)}, u32[]{:S(2)}, u32[]{:S(2)}) collective-permute-start(s16[400,128]{1,0:T(8,128)(2,1)S(1)} %get-tuple-element.68), channel_id=1, source_target_pairs={{0,1},{1,0},{2,3},{3,2},{4,5},{5,4},{6,7},{7,6},{8,9},{9,8},{10,11... | collective-permute-start | bytes 307208 | tf_op jit(solution)/shard_map/ppermute | solution.py:357
  36.3 5.7 %collective-permute-start.6 = (s16[400,128]{1,0:T(8,128)(2,1)S(1)}, s16[400,128]{1,0:T(8,128)(2,1)S(1)}, u32[]{:S(2)}, u32[]{:S(2)}) collective-permute-start(s16[400,128]{1,0:T(8,128)(2,1)S(1)} %get-tuple-element.69), channel_id=1, source_target_pairs={{0,2},{1,3},{2,0},{3,1},{4,6},{5,7},{6,4},{7,5},{8,10},{9,11},{10,... | collective-permute-start | bytes 307208 | tf_op jit(solution)/shard_map/ppermute | solution.py:357
  37.9 5.5 %collective-permute-start.7 = (s16[400,128]{1,0:T(8,128)(2,1)S(1)}, s16[400,128]{1,0:T(8,128)(2,1)S(1)}, u32[]{:S(2)}, u32[]{:S(2)}) collective-permute-start(s16[400,128]{1,0:T(8,128)(2,1)S(1)} %get-tuple-element.70), channel_id=1, source_target_pairs={{0,3},{1,2},{2,1},{3,0},{4,7},{5,6},{6,5},{7,4},{8,11},{9,10},{10,... | collective-permute-start | bytes 307208 | tf_op jit(solution)/shard_map/ppermute | solution.py:357
  39.5 7.3 %collective-permute-start.10 = (s16[400,128]{1,0:T(8,128)(2,1)S(1)}, s16[400,128]{1,0:T(8,128)(2,1)S(1)}, u32[]{:S(2)}, u32[]{:S(2)}) collective-permute-start(s16[400,128]{1,0:T(8,128)(2,1)S(1)} %get-tuple-element.74), channel_id=1, source_target_pairs={{0,1},{1,0},{2,3},{3,2},{4,5},{5,4},{6,7},{7,6},{8,9},{9,8},{10,11... | collective-permute-start | bytes 307208 | tf_op jit(solution)/shard_map/ppermute | solution.py:357
  40.1 6.9 %collective-permute-start.11 = (s16[400,128]{1,0:T(8,128)(2,1)S(1)}, s16[400,128]{1,0:T(8,128)(2,1)S(1)}, u32[]{:S(2)}, u32[]{:S(2)}) collective-permute-start(s16[400,128]{1,0:T(8,128)(2,1)S(1)} %get-tuple-element.75), channel_id=1, source_target_pairs={{0,2},{1,3},{2,0},{3,1},{4,6},{5,7},{6,4},{7,5},{8,10},{9,11},{10,... | collective-permute-start | bytes 307208 | tf_op jit(solution)/shard_map/ppermute | solution.py:357
  42.1 5.7 %collective-permute-start.12 = (s16[400,128]{1,0:T(8,128)(2,1)S(1)}, s16[400,128]{1,0:T(8,128)(2,1)S(1)}, u32[]{:S(2)}, u32[]{:S(2)}) collective-permute-start(s16[400,128]{1,0:T(8,128)(2,1)S(1)} %get-tuple-element.76), channel_id=1, source_target_pairs={{0,3},{1,2},{2,1},{3,0},{4,7},{5,6},{6,5},{7,4},{8,11},{9,10},{10,... | collective-permute-start | bytes 307208 | tf_op jit(solution)/shard_map/ppermute | solution.py:357
  44.5 3.2 %collective-permute-start.15 = (s16[272,128]{1,0:T(8,128)(2,1)S(1)}, s16[272,128]{1,0:T(8,128)(2,1)S(1)}, u32[]{:S(2)}, u32[]{:S(2)}) collective-permute-start(s16[272,128]{1,0:T(8,128)(2,1)S(1)} %get-tuple-element.81), channel_id=1, source_target_pairs={{0,1},{1,0},{2,3},{3,2},{4,5},{5,4},{6,7},{7,6},{8,9},{9,8},{10,11... | collective-permute-start | bytes 208904 | tf_op jit(solution)/shard_map/ppermute | solution.py:357
  45.3 4.4 %collective-permute-start.16 = (s16[272,128]{1,0:T(8,128)(2,1)S(1)}, s16[272,128]{1,0:T(8,128)(2,1)S(1)}, u32[]{:S(2)}, u32[]{:S(2)}) collective-permute-start(s16[272,128]{1,0:T(8,128)(2,1)S(1)} %get-tuple-element.82), channel_id=1, source_target_pairs={{0,2},{1,3},{2,0},{3,1},{4,6},{5,7},{6,4},{7,5},{8,10},{9,11},{10,... | collective-permute-start | bytes 208904 | tf_op jit(solution)/shard_map/ppermute | solution.py:357
  46.8 4.5 %collective-permute-start.17 = (s16[272,128]{1,0:T(8,128)(2,1)S(1)}, s16[272,128]{1,0:T(8,128)(2,1)S(1)}, u32[]{:S(2)}, u32[]{:S(2)}) collective-permute-start(s16[272,128]{1,0:T(8,128)(2,1)S(1)} %get-tuple-element.83), channel_id=1, source_target_pairs={{0,3},{1,2},{2,1},{3,0},{4,7},{5,6},{6,5},{7,4},{8,11},{9,10},{10,... | collective-permute-start | bytes 208904 | tf_op jit(solution)/shard_map/ppermute | solution.py:357
  53.2 5.4 %collective-permute-start.18 = (bf16[32,2048]{1,0:T(8,128)(2,1)S(1)}, bf16[32,2048]{1,0:T(8,128)(2,1)S(1)}, u32[]{:S(2)}, u32[]{:S(2)}) collective-permute-start(bf16[32,2048]{1,0:T(8,128)(2,1)S(1)} %get-tuple-element.86), channel_id=1, source_target_pairs={{0,1},{1,0},{2,3},{3,2},{4,5},{5,4},{6,7},{7,6},{8,9},{9,8},{10,11... | collective-permute-start | bytes 393224 | tf_op jit(solution)/shard_map/ppermute | solution.py:357
  53.3 6.3 %collective-permute-start.19 = (bf16[32,2048]{1,0:T(8,128)(2,1)S(1)}, bf16[32,2048]{1,0:T(8,128)(2,1)S(1)}, u32[]{:S(2)}, u32[]{:S(2)}) collective-permute-start(bf16[32,2048]{1,0:T(8,128)(2,1)S(1)} %get-tuple-element.87), channel_id=1, source_target_pairs={{0,2},{1,3},{2,0},{3,1},{4,6},{5,7},{6,4},{7,5},{8,10},{9,11},{10,... | collective-permute-start | bytes 393224 | tf_op jit(solution)/shard_map/ppermute | solution.py:357
  54.5 7.0 %collective-permute-start.20 = (bf16[32,2048]{1,0:T(8,128)(2,1)S(1)}, bf16[32,2048]{1,0:T(8,128)(2,1)S(1)}, u32[]{:S(2)}, u32[]{:S(2)}) collective-permute-start(bf16[32,2048]{1,0:T(8,128)(2,1)S(1)} %get-tuple-element.88), channel_id=1, source_target_pairs={{0,3},{1,2},{2,1},{3,0},{4,7},{5,6},{6,5},{7,4},{8,11},{9,10},{10,... | collective-permute-start | bytes 393224 | tf_op jit(solution)/shard_map/ppermute | solution.py:357
  57.0 7.2 %collective-permute-start.25 = (bf16[32,2048]{1,0:T(8,128)(2,1)S(1)}, bf16[32,2048]{1,0:T(8,128)(2,1)S(1)}, u32[]{:S(2)}, u32[]{:S(2)}) collective-permute-start(bf16[32,2048]{1,0:T(8,128)(2,1)S(1)} %get-tuple-element.92), channel_id=1, source_target_pairs={{0,1},{1,0},{2,3},{3,2},{4,5},{5,4},{6,7},{7,6},{8,9},{9,8},{10,11... | collective-permute-start | bytes 393224 | tf_op jit(solution)/shard_map/ppermute | solution.py:357
  57.4 7.8 %collective-permute-start.26 = (bf16[32,2048]{1,0:T(8,128)(2,1)S(1)}, bf16[32,2048]{1,0:T(8,128)(2,1)S(1)}, u32[]{:S(2)}, u32[]{:S(2)}) collective-permute-start(bf16[32,2048]{1,0:T(8,128)(2,1)S(1)} %get-tuple-element.93), channel_id=1, source_target_pairs={{0,2},{1,3},{2,0},{3,1},{4,6},{5,7},{6,4},{7,5},{8,10},{9,11},{10,... | collective-permute-start | bytes 393224 | tf_op jit(solution)/shard_map/ppermute | solution.py:357
  58.6 8.5 %collective-permute-start.27 = (bf16[32,2048]{1,0:T(8,128)(2,1)S(1)}, bf16[32,2048]{1,0:T(8,128)(2,1)S(1)}, u32[]{:S(2)}, u32[]{:S(2)}) collective-permute-start(bf16[32,2048]{1,0:T(8,128)(2,1)S(1)} %get-tuple-element.94), channel_id=1, source_target_pairs={{0,3},{1,2},{2,1},{3,0},{4,7},{5,6},{6,5},{7,4},{8,11},{9,10},{10,... | collective-permute-start | bytes 393224 | tf_op jit(solution)/shard_map/ppermute | solution.py:357
  61.5 9.7 %collective-permute-start.21 = (bf16[128,1024]{1,0:T(8,128)(2,1)S(1)}, bf16[128,1024]{1,0:T(8,128)(2,1)S(1)}, u32[]{:S(2)}, u32[]{:S(2)}) collective-permute-start(bf16[128,1024]{1,0:T(8,128)(2,1)S(1)} %get-tuple-element.89.refs_1_), channel_id=1, source_target_pairs={{0,4},{1,5},{2,6},{3,7},{4,0},{5,1},{6,2},{7,3},{8,12},{9,13},{10,... | collective-permute-start | bytes 786440 | tf_op jit(solution)/shard_map/ppermute | solution.py:357
  64.1 12.7 %collective-permute-start.23 = (bf16[128,1024]{1,0:T(8,128)(2,1)S(1)}, bf16[128,1024]{1,0:T(8,128)(2,1)S(1)}, u32[]{:S(2)}, u32[]{:S(2)}) collective-permute-start(bf16[128,1024]{1,0:T(8,128)(2,1)S(1)} %get-tuple-element.90.refs_4_), channel_id=1, source_target_pairs={{0,4},{1,5},{2,6},{3,7},{4,0},{5,1},{6,2},{7,3},{8,12},{9,13},{10,... | collective-permute-start | bytes 786440 | tf_op jit(solution)/shard_map/ppermute | solution.py:357
  67.2 15.3 %collective-permute-start.28 = (bf16[128,1024]{1,0:T(8,128)(2,1)S(1)}, bf16[128,1024]{1,0:T(8,128)(2,1)S(1)}, u32[]{:S(2)}, u32[]{:S(2)}) collective-permute-start(bf16[128,1024]{1,0:T(8,128)(2,1)S(1)} %get-tuple-element.95.refs_7_), channel_id=1, source_target_pairs={{0,4},{1,5},{2,6},{3,7},{4,0},{5,1},{6,2},{7,3},{8,12},{9,13},{10,... | collective-permute-start | bytes 786440 | tf_op jit(solution)/shard_map/ppermute | solution.py:357
  69.7 18.3 %collective-permute-start.30 = (bf16[128,1024]{1,0:T(8,128)(2,1)S(1)}, bf16[128,1024]{1,0:T(8,128)(2,1)S(1)}, u32[]{:S(2)}, u32[]{:S(2)}) collective-permute-start(bf16[128,1024]{1,0:T(8,128)(2,1)S(1)} %get-tuple-element.96.refs_10_), channel_id=1, source_target_pairs={{0,4},{1,5},{2,6},{3,7},{4,0},{5,1},{6,2},{7,3},{8,12},{9,13},{10,... | collective-permute-start | bytes 786440 | tf_op jit(solution)/shard_map/ppermute | solution.py:357
  71.2 18.1 %collective-permute-start.22 = (bf16[128,1024]{1,0:T(8,128)(2,1)S(1)}, bf16[128,1024]{1,0:T(8,128)(2,1)S(1)}, u32[]{:S(2)}, u32[]{:S(2)}) collective-permute-start(bf16[128,1024]{1,0:T(8,128)(2,1)S(1)} %collective-permute-done.21.refs_0_), channel_id=1, source_target_pairs={{0,8},{1,9},{2,10},{3,11},{4,28},{5,29},{6,30},{7,31},{8,16},{9,17... | collective-permute-start | bytes 786440 | tf_op jit(solution)/shard_map/ppermute | solution.py:357
  76.8 12.5 %collective-permute-start.24 = (bf16[128,1024]{1,0:T(8,128)(2,1)S(1)}, bf16[128,1024]{1,0:T(8,128)(2,1)S(1)}, u32[]{:S(2)}, u32[]{:S(2)}) collective-permute-start(bf16[128,1024]{1,0:T(8,128)(2,1)S(1)} %collective-permute-done.23.refs_3_), channel_id=1, source_target_pairs={{0,8},{1,9},{2,10},{3,11},{4,28},{5,29},{6,30},{7,31},{8,16},{9,17... | collective-permute-start | bytes 786440 | tf_op jit(solution)/shard_map/ppermute | solution.py:357
  82.5 10.3 %collective-permute-start.29 = (bf16[128,1024]{1,0:T(8,128)(2,1)S(1)}, bf16[128,1024]{1,0:T(8,128)(2,1)S(1)}, u32[]{:S(2)}, u32[]{:S(2)}) collective-permute-start(bf16[128,1024]{1,0:T(8,128)(2,1)S(1)} %collective-permute-done.28.refs_6_), channel_id=1, source_target_pairs={{0,8},{1,9},{2,10},{3,11},{4,28},{5,29},{6,30},{7,31},{8,16},{9,17... | collective-permute-start | bytes 786440 | tf_op jit(solution)/shard_map/ppermute | solution.py:357
  88.1 10.3 %collective-permute-start.31 = (bf16[128,1024]{1,0:T(8,128)(2,1)S(1)}, bf16[128,1024]{1,0:T(8,128)(2,1)S(1)}, u32[]{:S(2)}, u32[]{:S(2)}) collective-permute-start(bf16[128,1024]{1,0:T(8,128)(2,1)S(1)} %collective-permute-done.30.refs_9_), channel_id=1, source_target_pairs={{0,8},{1,9},{2,10},{3,11},{4,28},{5,29},{6,30},{7,31},{8,16},{9,17... | collective-permute-start | bytes 786440 | tf_op jit(solution)/shard_map/ppermute | solution.py:357
  100.0 4.5 %collective-permute-start.32 = (s16[528,128]{1,0:T(8,128)(2,1)S(1)}, s16[528,128]{1,0:T(8,128)(2,1)S(1)}, u32[]{:S(2)}, u32[]{:S(2)}) collective-permute-start(s16[528,128]{1,0:T(8,128)(2,1)S(1)} %get-tuple-element.98), channel_id=1, source_target_pairs={{0,1},{1,0},{2,3},{3,2},{4,5},{5,4},{6,7},{7,6},{8,9},{9,8},{10,11... | collective-permute-start | bytes 405512 | tf_op jit(solution)/shard_map/ppermute | solution.py:357
  100.1 6.5 %collective-permute-start.33 = (s16[528,128]{1,0:T(8,128)(2,1)S(1)}, s16[528,128]{1,0:T(8,128)(2,1)S(1)}, u32[]{:S(2)}, u32[]{:S(2)}) collective-permute-start(s16[528,128]{1,0:T(8,128)(2,1)S(1)} %get-tuple-element.99), channel_id=1, source_target_pairs={{0,2},{1,3},{2,0},{3,1},{4,6},{5,7},{6,4},{7,5},{8,10},{9,11},{10,... | collective-permute-start | bytes 405512 | tf_op jit(solution)/shard_map/ppermute | solution.py:357
  100.9 7.6 %collective-permute-start.34 = (s16[528,128]{1,0:T(8,128)(2,1)S(1)}, s16[528,128]{1,0:T(8,128)(2,1)S(1)}, u32[]{:S(2)}, u32[]{:S(2)}) collective-permute-start(s16[528,128]{1,0:T(8,128)(2,1)S(1)} %get-tuple-element.100), channel_id=1, source_target_pairs={{0,3},{1,2},{2,1},{3,0},{4,7},{5,6},{6,5},{7,4},{8,11},{9,10},{10,... | collective-permute-start | bytes 405512 | tf_op jit(solution)/shard_map/ppermute | solution.py:357
  103.4 8.7 %collective-permute-start.38 = (s16[528,128]{1,0:T(8,128)(2,1)S(1)}, s16[528,128]{1,0:T(8,128)(2,1)S(1)}, u32[]{:S(2)}, u32[]{:S(2)}) collective-permute-start(s16[528,128]{1,0:T(8,128)(2,1)S(1)} %get-tuple-element.108), channel_id=1, source_target_pairs={{0,1},{1,0},{2,3},{3,2},{4,5},{5,4},{6,7},{7,6},{8,9},{9,8},{10,11... | collective-permute-start | bytes 405512 | tf_op jit(solution)/shard_map/ppermute | solution.py:357
  103.8 9.0 %collective-permute-start.39 = (s16[528,128]{1,0:T(8,128)(2,1)S(1)}, s16[528,128]{1,0:T(8,128)(2,1)S(1)}, u32[]{:S(2)}, u32[]{:S(2)}) collective-permute-start(s16[528,128]{1,0:T(8,128)(2,1)S(1)} %get-tuple-element.109), channel_id=1, source_target_pairs={{0,2},{1,3},{2,0},{3,1},{4,6},{5,7},{6,4},{7,5},{8,10},{9,11},{10,... | collective-permute-start | bytes 405512 | tf_op jit(solution)/shard_map/ppermute | solution.py:357
  104.5 9.8 %collective-permute-start.40 = (s16[528,128]{1,0:T(8,128)(2,1)S(1)}, s16[528,128]{1,0:T(8,128)(2,1)S(1)}, u32[]{:S(2)}, u32[]{:S(2)}) collective-permute-start(s16[528,128]{1,0:T(8,128)(2,1)S(1)} %get-tuple-element.110), channel_id=1, source_target_pairs={{0,3},{1,2},{2,1},{3,0},{4,7},{5,6},{6,5},{7,4},{8,11},{9,10},{10,... | collective-permute-start | bytes 405512 | tf_op jit(solution)/shard_map/ppermute | solution.py:357
  110.6 7.3 %collective-permute-start.35 = (s16[528,128]{1,0:T(8,128)(2,1)S(1)}, s16[528,128]{1,0:T(8,128)(2,1)S(1)}, u32[]{:S(2)}, u32[]{:S(2)}) collective-permute-start(s16[528,128]{1,0:T(8,128)(2,1)S(1)} %get-tuple-element.102), channel_id=1, source_target_pairs={{0,1},{1,0},{2,3},{3,2},{4,5},{5,4},{6,7},{7,6},{8,9},{9,8},{10,11... | collective-permute-start | bytes 405512 | tf_op jit(solution)/shard_map/ppermute | solution.py:357
  111.4 7.2 %collective-permute-start.36 = (s16[528,128]{1,0:T(8,128)(2,1)S(1)}, s16[528,128]{1,0:T(8,128)(2,1)S(1)}, u32[]{:S(2)}, u32[]{:S(2)}) collective-permute-start(s16[528,128]{1,0:T(8,128)(2,1)S(1)} %get-tuple-element.103), channel_id=1, source_target_pairs={{0,2},{1,3},{2,0},{3,1},{4,6},{5,7},{6,4},{7,5},{8,10},{9,11},{10,... | collective-permute-start | bytes 405512 | tf_op jit(solution)/shard_map/ppermute | solution.py:357
  112.1 8.0 %collective-permute-start.37 = (s16[528,128]{1,0:T(8,128)(2,1)S(1)}, s16[528,128]{1,0:T(8,128)(2,1)S(1)}, u32[]{:S(2)}, u32[]{:S(2)}) collective-permute-start(s16[528,128]{1,0:T(8,128)(2,1)S(1)} %get-tuple-element.104), channel_id=1, source_target_pairs={{0,3},{1,2},{2,1},{3,0},{4,7},{5,6},{6,5},{7,4},{8,11},{9,10},{10,... | collective-permute-start | bytes 405512 | tf_op jit(solution)/shard_map/ppermute | solution.py:357
  116.4 3.7 %collective-permute-start.41 = (s16[528,128]{1,0:T(8,128)(2,1)S(1)}, s16[528,128]{1,0:T(8,128)(2,1)S(1)}, u32[]{:S(2)}, u32[]{:S(2)}) collective-permute-start(s16[528,128]{1,0:T(8,128)(2,1)S(1)} %get-tuple-element.112), channel_id=1, source_target_pairs={{0,1},{1,0},{2,3},{3,2},{4,5},{5,4},{6,7},{7,6},{8,9},{9,8},{10,11... | collective-permute-start | bytes 405512 | tf_op jit(solution)/shard_map/ppermute | solution.py:357
  117.2 6.7 %collective-permute-start.42 = (s16[528,128]{1,0:T(8,128)(2,1)S(1)}, s16[528,128]{1,0:T(8,128)(2,1)S(1)}, u32[]{:S(2)}, u32[]{:S(2)}) collective-permute-start(s16[528,128]{1,0:T(8,128)(2,1)S(1)} %get-tuple-element.113), channel_id=1, source_target_pairs={{0,2},{1,3},{2,0},{3,1},{4,6},{5,7},{6,4},{7,5},{8,10},{9,11},{10,... | collective-permute-start | bytes 405512 | tf_op jit(solution)/shard_map/ppermute | solution.py:357
  117.9 8.0 %collective-permute-start.43 = (s16[528,128]{1,0:T(8,128)(2,1)S(1)}, s16[528,128]{1,0:T(8,128)(2,1)S(1)}, u32[]{:S(2)}, u32[]{:S(2)}) collective-permute-start(s16[528,128]{1,0:T(8,128)(2,1)S(1)} %get-tuple-element.114), channel_id=1, source_target_pairs={{0,3},{1,2},{2,1},{3,0},{4,7},{5,6},{6,5},{7,4},{8,11},{9,10},{10,... | collective-permute-start | bytes 405512 | tf_op jit(solution)/shard_map/ppermute | solution.py:357
  (2 other events, 3.2 us)

commit v3 on v2

--- a/solution.py
+++ b/solution.py
@@ -260,18 +260,22 @@
             out[:, a * LANE : (a + 1) * LANE] = back[pl.ds(at, count), :].astype(bf16)
 
 
-def second_kernel(ways, place, h, s, *refs):
-    pieces, outs, rows, back = refs[:ways], refs[ways:-2], refs[-2], refs[-1]
-    j = place[1]
-    count = h.shape[0]
+def second_kernel(ways, spans, start, count, place, h, *refs):
+    n = len(spans)
+    states, pieces, outs = refs[:n], refs[n : n + ways], refs[n + ways : -2]
+    rows, back = refs[-2:]
+    j = place[1]
     step = step_of(count)
     unpack_field(place, 1, count, 0, count, pieces, rows)
-
-    def body(m, carry):
-        back[pl.ds(m, NB, stride=step), :] = rate(h[m] + rows[pl.ds(m, NB, stride=step), :], s[m])
-        return carry
-
-    lax.fori_loop(0, count, body, 0, unroll=16)
+    for s, (first, low, high) in zip(states, spans):
+
+        def body(m, carry):
+            back[pl.ds(m, NB, stride=step), :] = rate(
+                h[m] + rows[pl.ds(m, NB, stride=step), :], s[m + (start - first)]
+            )
+            return carry
+
+        lax.fori_loop(low, high, body, 0, unroll=16)
     own = (outs[0].shape[0] - PACK) // count
     for k, out in enumerate(outs):
         first = (j ^ k) * own
@@ -346,6 +350,7 @@
     band = mom // nb
     chunks = 2 if band % 32 == 0 else 1
     count = band // chunks
+    sizes1 = [count] * chunks
     place = jnp.stack([i % 2, j, i * tiles]).astype(i32)
 
     def move(value, target):
@@ -364,6 +369,9 @@
 
     def onward(value):
         return move(value, lambda a, b: (a - 2 if a % 2 else a + 2, b))
+
+    def direct(value):
+        return move(value, lambda a, b: (a + 1 if a % 2 else a - 1, b))
 
     shape = jax.ShapeDtypeStruct
     widths = split_rows(own, CUTS)
@@ -373,8 +381,9 @@
     swap = [across(v) for v in mine]
     passed = []
     for q, value in enumerate(swap):
-        if q > 1:
-            value = tie(value, passed[q - 2])
+        if q > 0 and q == cuts - 1:
+            passed.append(direct(mine[q]))
+            continue
         passed.append(onward(value))
     dense = call(
         functools.partial(coupling_kernel, nka * tiles),
@@ -406,24 +415,26 @@
     chunk_rows = pltpu.VMEM((step_of(count) * NB, LANE), f32)
     chunk_shape = shape((count, NB, LANE), f32)
     middles, parts, spots = [], [], []
-    for c in range(chunks):
-        at = slice(c * count, (c + 1) * count)
-        hc, sc = hamilton[at], state[at]
+    start = 0
+    for size in sizes1:
+        hc, sc = hamilton[start : start + size], state[start : start + size]
         middle, *outs = call(
-            functools.partial(first_kernel, cuts, nb * cuts, c * count, band),
-            [chunk_shape] + [shape((count, own * LANE), bf16)] * nb,
-            [chunk_rows, chunk_rows],
+            functools.partial(first_kernel, cuts, nb * cuts, start, band),
+            [shape((size, NB, LANE), f32)] + [shape((size, own * LANE), bf16)] * nb,
+            [pltpu.VMEM((step_of(size) * NB, LANE), f32)] * 2,
             n_in=2 + nb * cuts,
         )(place, hc, sc, *got)
-        middles.append(middle)
+        middles.append((middle, start, size))
         back = [in_group(v, k) for k, v in enumerate(outs)]
-        ewidths = [own // ecuts] * ecuts
-        joined = [shape((nb * count, w * LANE), bf16) for w in ewidths]
+        ewidths = [own // 2] * 2 if size > 16 and own % 4 == 0 else [own]
+        joined = [shape((nb * size, w * LANE), bf16) for w in ewidths]
         mine = call(functools.partial(join_kernel, len(ewidths)), joined, specs=[VMEM] * nb)(*back)
         for q in range(len(ewidths)):
             swap = across(mine[q])
-            parts += [swap, mine[q], onward(swap)]
-            spots += [(b, c * count, sum(ewidths[:q]) * LANE) for b in range(3)]
+            last = start + size == band and q == len(ewidths) - 1 and start > 0
+            parts += [swap, mine[q], direct(mine[q]) if last else onward(swap)]
+            spots += [(b, start, sum(ewidths[:q]) * LANE) for b in range(3)]
+        start += size
 
     pieces = [shape((own * count + PACK, LANE), i16)] * nb
     room = [pltpu.VMEM((nb * count, own * LANE), i16), pltpu.VMEM((nb * count, LANE), f32)]
@@ -438,13 +449,18 @@
     got = [[in_group(fields[c * nb + k], k) for k in range(nb)] for c in range(chunks)]
     rates = []
     for c in range(chunks):
-        hc, sc = hamilton[c * count : (c + 1) * count], middles[c]
+        start = c * count
+        spans = [
+            (m, first, max(first, start) - start, min(first + size, start + count) - start)
+            for m, first, size in middles
+            if first < start + count and first + size > start
+        ]
         outs = call(
-            functools.partial(second_kernel, nb),
-            [shape((own * count + PACK, LANE), i16)] * nb,
-            [chunk_rows, chunk_rows],
-            n_in=2 + nb,
-        )(place, hc, sc, *got[c])
+            functools.partial(second_kernel, nb, [v[1:] for v in spans], start, count),
+            pieces,
+            [pltpu.VMEM((step_of(count) * NB, LANE), f32)] * 2,
+            n_in=1 + len(spans) + nb,
+        )(place, hamilton[start : start + count], *[v[0] for v in spans], *got[c])
         rates += [in_group(v, k) for k, v in enumerate(outs)]
     return pl.pallas_call(
         functools.partial(last_kernel, chunks),

time: 129 us -> 129 us (level)
  transfers between devices with their start and end apart: 44 -> 44, of which waited for: 24 -> 22; matrix products, arithmetic and copies ran while one was open for 0% -> 0% of each run, Pallas kernels for 11% -> 12%
where the time goes in v3:
time: 129 us; the launch traced here: 128 us
  waiting for transfers between devices  61.9 us (48%)
  starting transfers between devices  42.6 us (33%)
  Pallas kernels  21.5 us (17%)
  local copies, waits for them, and re-layouts  1.88 us (1%)
    ppermute x44, waiting for transfers between devices, move(): return lax.ppermute(value, ('ka', 'ba'), pairs_of)  61.9 us
    ppermute x44, starting transfers between devices, move(): return lax.ppermute(value, ('ka', 'ba'), pairs_of)  42.6 us
    pallas_call x3, Pallas kernels, local(): call(field_one_kernel, [shape((widths[q] * band + PACK, LANE), i16)] * nb...  4.23 us
    pallas_call x2, Pallas kernels, local(): call(functools.partial(second_kernel, nb, [v[1:] for v in spans], start,...  4.12 us
    pallas_call x2, Pallas kernels, local(): call(functools.partial(first_kernel, cuts, nb * cuts, start, band), [shap...  3.76 us
  transfers between devices with their start and end apart: 44, of which 22 were waited for; matrix products, arithmetic and copies ran while one was open for 0% of the time, Pallas kernels for 12%

profile of v3, /device:TPU:0, one launch (start us, length us, event | category | flops | bytes accessed | tf_op | source)
XLA Modules:
  0.0 128.4 jit_solution(1582277042252575666)
XLA Ops:
  0.0 1.6 %copy-done = f32[2,256,1024]{2,1,0:T(8,128)S(1)} copy-done((f32[2,256,1024]{2,1,0:T(8,128)S(1)}, f32[2,256,1024]{2,1,0:T(8,128)}, u32[]{:S(2)}) %copy-start) | copy-done | bytes 2097176
  2.0 3.0 %collective-permute-start = (bf16[256,768]{1,0:T(8,128)(2,1)S(1)}, bf16[256,768]{1,0:T(8,128)(2,1)}, u32[]{:S(2)}, u32[]{:S(2)}) collective-permute-start(bf16[256,768]{1,0:T(8,128)(2,1)S(1)} %get-tuple-element.63.mine), channel_id=1, source_target_pairs={{0,4},{1,5},{2,6},{3,7},{4,0},{5,1},{6,2},{7,3},{8,12},{9,13},{10,... | collective-permute-start | bytes 1179656 | tf_op jit(solution)/shard_map/ppermute | solution.py:362
  6.2 2.0 %collective-permute-start.3 = (f32[64,2048]{1,0:T(8,128)S(1)}, f32[64,2048]{1,0:T(8,128)S(1)}, u32[]{:S(2)}, u32[]{:S(2)}) collective-permute-start(f32[64,2048]{1,0:T(8,128)S(1)} %get-tuple-element.61.refs_2_), channel_id=1, source_target_pairs={{0,2},{1,3},{2,0},{3,1},{4,6},{5,7},{6,4},{7,5},{8,10},{9,11},{10,... | collective-permute-start | bytes 1572872 | tf_op jit(solution)/shard_map/ppermute | solution.py:362
  8.3 6.8 %collective-permute-done.swap = bf16[256,768]{1,0:T(8,128)(2,1)} collective-permute-done((bf16[256,768]{1,0:T(8,128)(2,1)S(1)}, bf16[256,768]{1,0:T(8,128)(2,1)}, u32[]{:S(2)}, u32[]{:S(2)}) %collective-permute-start) | collective-permute-done | bytes 393248 | tf_op jit(solution)/shard_map/ppermute | solution.py:362
  15.1 2.1 %collective-permute-start.1 = (bf16[256,768]{1,0:T(8,128)(2,1)}, bf16[256,768]{1,0:T(8,128)(2,1)S(1)}, u32[]{:S(2)}, u32[]{:S(2)}) collective-permute-start(bf16[256,768]{1,0:T(8,128)(2,1)} %collective-permute-done.swap), channel_id=1, source_target_pairs={{0,8},{1,9},{2,10},{3,11},{4,28},{5,29},{6,30},{7,31},{8,16},{9,17... | collective-permute-start | bytes 1179656 | tf_op jit(solution)/shard_map/ppermute | solution.py:362
  17.2 5.3 %collective-permute-done.8.swap = bf16[256,768]{1,0:T(8,128)(2,1)S(1)} collective-permute-done((bf16[256,768]{1,0:T(8,128)(2,1)S(1)}, bf16[256,768]{1,0:T(8,128)(2,1)S(1)}, u32[]{:S(2)}, u32[]{:S(2)}) %collective-permute-start.8) | collective-permute-done | bytes 393248 | tf_op jit(solution)/shard_map/ppermute | solution.py:362
  22.5 1.8 %collective-permute-start.9 = (bf16[256,768]{1,0:T(8,128)(2,1)S(1)}, bf16[256,768]{1,0:T(8,128)(2,1)S(1)}, u32[]{:S(2)}, u32[]{:S(2)}) collective-permute-start(bf16[256,768]{1,0:T(8,128)(2,1)S(1)} %collective-permute-done.8.swap), channel_id=1, source_target_pairs={{0,8},{1,9},{2,10},{3,11},{4,28},{5,29},{6,30},{7,31},{8,16},{9,17... | collective-permute-start | bytes 1179656 | tf_op jit(solution)/shard_map/ppermute | solution.py:362
  24.4 3.5 %collective-permute-start.14 = (bf16[256,512]{1,0:T(8,128)(2,1)S(1)}, bf16[256,512]{1,0:T(8,128)(2,1)S(1)}, u32[]{:S(2)}, u32[]{:S(2)}) collective-permute-start(bf16[256,512]{1,0:T(8,128)(2,1)S(1)} %get-tuple-element.76.mine), channel_id=1, source_target_pairs={{0,28},{1,29},{2,30},{3,31},{4,8},{5,9},{6,10},{7,11},{8,4},{9,5},... | collective-permute-start | bytes 786440 | tf_op jit(solution)/shard_map/ppermute | solution.py:362
  29.7 1.9 %collective-permute-done.4.refs_3_ = f32[64,2048]{1,0:T(8,128)S(1)} collective-permute-done((f32[64,2048]{1,0:T(8,128)S(1)}, f32[64,2048]{1,0:T(8,128)S(1)}, u32[]{:S(2)}, u32[]{:S(2)}) %collective-permute-start.4) | collective-permute-done | bytes 524320 | tf_op jit(solution)/shard_map/ppermute | solution.py:362
  31.6 1.1 shard_map.58
  32.7 1.8 %shard_map.60 = (s16[400,128]{1,0:T(8,128)(2,1)S(1)}, s16[400,128]{1,0:T(8,128)(2,1)S(1)}, s16[400,128]{1,0:T(8,128)(2,1)S(1)}, s16[400,128]{1,0:T(8,128)(2,1)S(1)}) custom-call(s32[3]{0:T(128)S(1)} %pad_add_fusion.place, bf16[256,768]{1,0:T(8,128)(2,1)S(1)} %shard_map.59.dense, bf16[256,768]{1,0:T(8,128)(2,1)S(1)} %get-tuple-element.63.mine, ...), custom_call_target="tpu_custom_call" | custom-call | bytes 3600000 | tf_op jit(solution)/shard_map/pallas_call | solution.py:406
  35.0 1.8 %collective-permute-start.6 = (s16[400,128]{1,0:T(8,128)(2,1)S(1)}, s16[400,128]{1,0:T(8,128)(2,1)S(1)}, u32[]{:S(2)}, u32[]{:S(2)}) collective-permute-start(s16[400,128]{1,0:T(8,128)(2,1)S(1)} %get-tuple-element.68), channel_id=1, source_target_pairs={{0,2},{1,3},{2,0},{3,1},{4,6},{5,7},{6,4},{7,5},{8,10},{9,11},{10,... | collective-permute-start | bytes 307208 | tf_op jit(solution)/shard_map/ppermute | solution.py:362
  36.8 1.3 %shard_map.61 = (s16[400,128]{1,0:T(8,128)(2,1)S(1)}, s16[400,128]{1,0:T(8,128)(2,1)S(1)}, s16[400,128]{1,0:T(8,128)(2,1)S(1)}, s16[400,128]{1,0:T(8,128)(2,1)S(1)}) custom-call(s32[3]{0:T(128)S(1)} %pad_add_fusion.place, bf16[256,768]{1,0:T(8,128)(2,1)S(1)} %shard_map.59.dense, bf16[256,768]{1,0:T(8,128)(2,1)S(1)} %get-tuple-element.70.mine, ...), custom_call_target="tpu_custom_call" | custom-call | bytes 3600000 | tf_op jit(solution)/shard_map/pallas_call | solution.py:406
  38.1 3.7 %collective-permute-done.14.passed = bf16[256,512]{1,0:T(8,128)(2,1)S(1)} collective-permute-done((bf16[256,512]{1,0:T(8,128)(2,1)S(1)}, bf16[256,512]{1,0:T(8,128)(2,1)S(1)}, u32[]{:S(2)}, u32[]{:S(2)}) %collective-permute-start.14) | collective-permute-done | bytes 262176 | tf_op jit(solution)/shard_map/ppermute | solution.py:362
  41.9 1.6 %collective-permute-start.11 = (s16[400,128]{1,0:T(8,128)(2,1)S(1)}, s16[400,128]{1,0:T(8,128)(2,1)S(1)}, u32[]{:S(2)}, u32[]{:S(2)}) collective-permute-start(s16[400,128]{1,0:T(8,128)(2,1)S(1)} %get-tuple-element.74), channel_id=1, source_target_pairs={{0,2},{1,3},{2,0},{3,1},{4,6},{5,7},{6,4},{7,5},{8,10},{9,11},{10,... | collective-permute-start | bytes 307208 | tf_op jit(solution)/shard_map/ppermute | solution.py:362
  43.9 1.1 shard_map.62
  45.4 1.5 %collective-permute-start.16 = (s16[272,128]{1,0:T(8,128)(2,1)S(1)}, s16[272,128]{1,0:T(8,128)(2,1)S(1)}, u32[]{:S(2)}, u32[]{:S(2)}) collective-permute-start(s16[272,128]{1,0:T(8,128)(2,1)S(1)} %get-tuple-element.80), channel_id=1, source_target_pairs={{0,2},{1,3},{2,0},{3,1},{4,6},{5,7},{6,4},{7,5},{8,10},{9,11},{10,... | collective-permute-start | bytes 208904 | tf_op jit(solution)/shard_map/ppermute | solution.py:362
  47.7 1.4 %collective-permute-done.12.refs_7_ = s16[400,128]{1,0:T(8,128)(2,1)S(1)} collective-permute-done((s16[400,128]{1,0:T(8,128)(2,1)S(1)}, s16[400,128]{1,0:T(8,128)(2,1)S(1)}, u32[]{:S(2)}, u32[]{:S(2)}) %collective-permute-start.12) | collective-permute-done | bytes 102432 | tf_op jit(solution)/shard_map/ppermute | solution.py:362
  49.1 2.3 %collective-permute-done.16.refs_10_ = s16[272,128]{1,0:T(8,128)(2,1)S(1)} collective-permute-done((s16[272,128]{1,0:T(8,128)(2,1)S(1)}, s16[272,128]{1,0:T(8,128)(2,1)S(1)}, u32[]{:S(2)}, u32[]{:S(2)}) %collective-permute-start.16) | collective-permute-done | bytes 69664 | tf_op jit(solution)/shard_map/ppermute | solution.py:362
  52.1 1.9 %shard_map.63 = (f32[32,64,128]{2,1,0:T(8,128)S(1)}, bf16[32,2048]{1,0:T(8,128)(2,1)S(1)}, bf16[32,2048]{1,0:T(8,128)(2,1)S(1)}, bf16[32,2048]{1,0:T(8,128)(2,1)S(1)}, bf16[32,2048]{1,0:T(8,128)(2,1)S(1)}) custom-call(s32[3]{0:T(128)S(1)} %pad_add_fusion.place, f32[32,64,128]{2,1,0:T(8,128)S(1)} %get-tuple-element.116.h, ...), custom_call_target="tpu_custom_call" | custom-call | bytes 3600000 | tf_op jit(solution)/shard_map/pallas_call | solution.py:421
  54.2 1.5 %collective-permute-start.19 = (bf16[32,2048]{1,0:T(8,128)(2,1)S(1)}, bf16[32,2048]{1,0:T(8,128)(2,1)S(1)}, u32[]{:S(2)}, u32[]{:S(2)}) collective-permute-start(bf16[32,2048]{1,0:T(8,128)(2,1)S(1)} %get-tuple-element.85), channel_id=1, source_target_pairs={{0,2},{1,3},{2,0},{3,1},{4,6},{5,7},{6,4},{7,5},{8,10},{9,11},{10,... | collective-permute-start | bytes 393224 | tf_op jit(solution)/shard_map/ppermute | solution.py:362
  55.9 1.9 %shard_map.65 = (f32[32,64,128]{2,1,0:T(8,128)S(1)}, bf16[32,2048]{1,0:T(8,128)(2,1)S(1)}, bf16[32,2048]{1,0:T(8,128)(2,1)S(1)}, bf16[32,2048]{1,0:T(8,128)(2,1)S(1)}, bf16[32,2048]{1,0:T(8,128)(2,1)S(1)}) custom-call(s32[3]{0:T(128)S(1)} %pad_add_fusion.place, f32[32,64,128]{2,1,0:T(8,128)S(1)} %get-tuple-element.115.h, ...), custom_call_target="tpu_custom_call" | custom-call | bytes 3600000 | tf_op jit(solution)/shard_map/pallas_call | solution.py:421
  58.3 1.5 %collective-permute-start.26 = (bf16[32,2048]{1,0:T(8,128)(2,1)S(1)}, bf16[32,2048]{1,0:T(8,128)(2,1)S(1)}, u32[]{:S(2)}, u32[]{:S(2)}) collective-permute-start(bf16[32,2048]{1,0:T(8,128)(2,1)S(1)} %get-tuple-element.91), channel_id=1, source_target_pairs={{0,2},{1,3},{2,0},{3,1},{4,6},{5,7},{6,4},{7,5},{8,10},{9,11},{10,... | collective-permute-start | bytes 393224 | tf_op jit(solution)/shard_map/ppermute | solution.py:362
  60.6 1.8 %collective-permute-done.20.refs_3_ = bf16[32,2048]{1,0:T(8,128)(2,1)S(1)} collective-permute-done((bf16[32,2048]{1,0:T(8,128)(2,1)S(1)}, bf16[32,2048]{1,0:T(8,128)(2,1)S(1)}, u32[]{:S(2)}, u32[]{:S(2)}) %collective-permute-start.20) | collective-permute-done | bytes 131104 | tf_op jit(solution)/shard_map/ppermute | solution.py:362
  62.9 1.6 %collective-permute-start.23 = (bf16[128,1024]{1,0:T(8,128)(2,1)S(1)}, bf16[128,1024]{1,0:T(8,128)(2,1)S(1)}, u32[]{:S(2)}, u32[]{:S(2)}) collective-permute-start(bf16[128,1024]{1,0:T(8,128)(2,1)S(1)} %get-tuple-element.88.refs_4_), channel_id=1, source_target_pairs={{0,4},{1,5},{2,6},{3,7},{4,0},{5,1},{6,2},{7,3},{8,12},{9,13},{10,... | collective-permute-start | bytes 786440 | tf_op jit(solution)/shard_map/ppermute | solution.py:362
  64.5 1.6 %collective-permute-done.26.refs_2_ = bf16[32,2048]{1,0:T(8,128)(2,1)S(1)} collective-permute-done((bf16[32,2048]{1,0:T(8,128)(2,1)S(1)}, bf16[32,2048]{1,0:T(8,128)(2,1)S(1)}, u32[]{:S(2)}, u32[]{:S(2)}) %collective-permute-start.26) | collective-permute-done | bytes 131104 | tf_op jit(solution)/shard_map/ppermute | solution.py:362
  66.2 1.6 %collective-permute-done.27.refs_3_ = bf16[32,2048]{1,0:T(8,128)(2,1)S(1)} collective-permute-done((bf16[32,2048]{1,0:T(8,128)(2,1)S(1)}, bf16[32,2048]{1,0:T(8,128)(2,1)S(1)}, u32[]{:S(2)}, u32[]{:S(2)}) %collective-permute-start.27) | collective-permute-done | bytes 131104 | tf_op jit(solution)/shard_map/ppermute | solution.py:362
  68.2 4.0 %collective-permute-start.31 = (bf16[128,1024]{1,0:T(8,128)(2,1)S(1)}, bf16[128,1024]{1,0:T(8,128)(2,1)S(1)}, u32[]{:S(2)}, u32[]{:S(2)}) collective-permute-start(bf16[128,1024]{1,0:T(8,128)(2,1)S(1)} %get-tuple-element.94.refs_10_), channel_id=1, source_target_pairs={{0,28},{1,29},{2,30},{3,31},{4,8},{5,9},{6,10},{7,11},{8,4},{9,5},... | collective-permute-start | bytes 786440 | tf_op jit(solution)/shard_map/ppermute | solution.py:362
  73.3 9.7 %collective-permute-done.23.refs_3_ = bf16[128,1024]{1,0:T(8,128)(2,1)S(1)} collective-permute-done((bf16[128,1024]{1,0:T(8,128)(2,1)S(1)}, bf16[128,1024]{1,0:T(8,128)(2,1)S(1)}, u32[]{:S(2)}, u32[]{:S(2)}) %collective-permute-start.23) | collective-permute-done | bytes 262176 | tf_op jit(solution)/shard_map/ppermute | solution.py:362
  82.9 1.6 %collective-permute-start.24 = (bf16[128,1024]{1,0:T(8,128)(2,1)S(1)}, bf16[128,1024]{1,0:T(8,128)(2,1)S(1)}, u32[]{:S(2)}, u32[]{:S(2)}) collective-permute-start(bf16[128,1024]{1,0:T(8,128)(2,1)S(1)} %collective-permute-done.23.refs_3_), channel_id=1, source_target_pairs={{0,8},{1,9},{2,10},{3,11},{4,28},{5,29},{6,30},{7,31},{8,16},{9,17... | collective-permute-start | bytes 786440 | tf_op jit(solution)/shard_map/ppermute | solution.py:362
  84.5 4.0 %collective-permute-done.28.refs_6_ = bf16[128,1024]{1,0:T(8,128)(2,1)S(1)} collective-permute-done((bf16[128,1024]{1,0:T(8,128)(2,1)S(1)}, bf16[128,1024]{1,0:T(8,128)(2,1)S(1)}, u32[]{:S(2)}, u32[]{:S(2)}) %collective-permute-start.28) | collective-permute-done | bytes 262176 | tf_op jit(solution)/shard_map/ppermute | solution.py:362
  88.5 1.6 %collective-permute-start.29 = (bf16[128,1024]{1,0:T(8,128)(2,1)S(1)}, bf16[128,1024]{1,0:T(8,128)(2,1)S(1)}, u32[]{:S(2)}, u32[]{:S(2)}) collective-permute-start(bf16[128,1024]{1,0:T(8,128)(2,1)S(1)} %collective-permute-done.28.refs_6_), channel_id=1, source_target_pairs={{0,8},{1,9},{2,10},{3,11},{4,28},{5,29},{6,30},{7,31},{8,16},{9,17... | collective-permute-start | bytes 786440 | tf_op jit(solution)/shard_map/ppermute | solution.py:362
  90.1 3.9 %collective-permute-done.30.refs_9_ = bf16[128,1024]{1,0:T(8,128)(2,1)S(1)} collective-permute-done((bf16[128,1024]{1,0:T(8,128)(2,1)S(1)}, bf16[128,1024]{1,0:T(8,128)(2,1)S(1)}, u32[]{:S(2)}, u32[]{:S(2)}) %collective-permute-start.30) | collective-permute-done | bytes 262176 | tf_op jit(solution)/shard_map/ppermute | solution.py:362
  94.0 4.3 %collective-permute-done.29.refs_8_ = bf16[128,1024]{1,0:T(8,128)(2,1)S(1)} collective-permute-done((bf16[128,1024]{1,0:T(8,128)(2,1)S(1)}, bf16[128,1024]{1,0:T(8,128)(2,1)S(1)}, u32[]{:S(2)}, u32[]{:S(2)}) %collective-permute-start.29) | collective-permute-done | bytes 262176 | tf_op jit(solution)/shard_map/ppermute | solution.py:362
  98.3 1.6 %shard_map.67 = (s16[528,128]{1,0:T(8,128)(2,1)S(1)}, s16[528,128]{1,0:T(8,128)(2,1)S(1)}, s16[528,128]{1,0:T(8,128)(2,1)S(1)}, s16[528,128]{1,0:T(8,128)(2,1)S(1)}, bf16[768,2048]{1,0:T(8,128)(2,1)S(1)}) custom-call(s32[3]{0:T(128)S(1)} %pad_add_fusion.place, bf16[256,768]{1,0:T(8,128)(2,1)S(1)} %shard_map.59.dense, ...), custom_call_target="tpu_custom_call" | custom-call | bytes 3600000 | tf_op jit(solution)/shard_map/pallas_call | solution.py:441
  100.0 1.8 %collective-permute-start.33 = (s16[528,128]{1,0:T(8,128)(2,1)S(1)}, s16[528,128]{1,0:T(8,128)(2,1)S(1)}, u32[]{:S(2)}, u32[]{:S(2)}) collective-permute-start(s16[528,128]{1,0:T(8,128)(2,1)S(1)} %get-tuple-element.97), channel_id=1, source_target_pairs={{0,2},{1,3},{2,0},{3,1},{4,6},{5,7},{6,4},{7,5},{8,10},{9,11},{10,... | collective-permute-start | bytes 405512 | tf_op jit(solution)/shard_map/ppermute | solution.py:362
  101.9 1.4 %shard_map.69 = (s16[528,128]{1,0:T(8,128)(2,1)S(1)}, s16[528,128]{1,0:T(8,128)(2,1)S(1)}, s16[528,128]{1,0:T(8,128)(2,1)S(1)}, s16[528,128]{1,0:T(8,128)(2,1)S(1)}) custom-call(s32[3]{0:T(128)S(1)} %pad_add_fusion.place, bf16[256,768]{1,0:T(8,128)(2,1)S(1)} %shard_map.59.dense, bf16[768,2048]{1,0:T(8,128)(2,1)S(1)} %get-tuple-element.104.window), custom_call_target="tpu_custom_call" | custom-call | bytes 3600000 | tf_op jit(solution)/shard_map/pallas_call | solution.py:448
  103.8 1.7 %collective-permute-start.39 = (s16[528,128]{1,0:T(8,128)(2,1)S(1)}, s16[528,128]{1,0:T(8,128)(2,1)S(1)}, u32[]{:S(2)}, u32[]{:S(2)}) collective-permute-start(s16[528,128]{1,0:T(8,128)(2,1)S(1)} %get-tuple-element.107), channel_id=1, source_target_pairs={{0,2},{1,3},{2,0},{3,1},{4,6},{5,7},{6,4},{7,5},{8,10},{9,11},{10,... | collective-permute-start | bytes 405512 | tf_op jit(solution)/shard_map/ppermute | solution.py:362
  106.5 2.1 %collective-permute-done.34.refs_4_ = s16[528,128]{1,0:T(8,128)(2,1)S(1)} collective-permute-done((s16[528,128]{1,0:T(8,128)(2,1)S(1)}, s16[528,128]{1,0:T(8,128)(2,1)S(1)}, u32[]{:S(2)}, u32[]{:S(2)}) %collective-permute-start.34) | collective-permute-done | bytes 135200 | tf_op jit(solution)/shard_map/ppermute | solution.py:362
  108.6 2.1 %shard_map.68 = (s16[528,128]{1,0:T(8,128)(2,1)S(1)}, s16[528,128]{1,0:T(8,128)(2,1)S(1)}, s16[528,128]{1,0:T(8,128)(2,1)S(1)}, s16[528,128]{1,0:T(8,128)(2,1)S(1)}) custom-call(s32[3]{0:T(128)S(1)} %pad_add_fusion.place, f32[32,64,128]{2,1,0:T(8,128)S(1)} %get-tuple-element.116.h, f32[32,64,128]{2,1,0:T(8,128)S(1)} %get-tuple-element.82.refs_0_, ...), custom_call_target="tpu_custom_call" | custom-call | bytes 3600000 | tf_op jit(solution)/shard_map/pallas_call | solution.py:458
  111.3 1.7 %collective-permute-start.36 = (s16[528,128]{1,0:T(8,128)(2,1)S(1)}, s16[528,128]{1,0:T(8,128)(2,1)S(1)}, u32[]{:S(2)}, u32[]{:S(2)}) collective-permute-start(s16[528,128]{1,0:T(8,128)(2,1)S(1)} %get-tuple-element.101), channel_id=1, source_target_pairs={{0,2},{1,3},{2,0},{3,1},{4,6},{5,7},{6,4},{7,5},{8,10},{9,11},{10,... | collective-permute-start | bytes 405512 | tf_op jit(solution)/shard_map/ppermute | solution.py:362
  113.0 1.3 %collective-permute-done.40.refs_4_ = s16[528,128]{1,0:T(8,128)(2,1)S(1)} collective-permute-done((s16[528,128]{1,0:T(8,128)(2,1)S(1)}, s16[528,128]{1,0:T(8,128)(2,1)S(1)}, u32[]{:S(2)}, u32[]{:S(2)}) %collective-permute-start.40) | collective-permute-done | bytes 135200 | tf_op jit(solution)/shard_map/ppermute | solution.py:362
  114.4 2.1 %shard_map.70 = (s16[528,128]{1,0:T(8,128)(2,1)S(1)}, s16[528,128]{1,0:T(8,128)(2,1)S(1)}, s16[528,128]{1,0:T(8,128)(2,1)S(1)}, s16[528,128]{1,0:T(8,128)(2,1)S(1)}) custom-call(s32[3]{0:T(128)S(1)} %pad_add_fusion.place, f32[32,64,128]{2,1,0:T(8,128)S(1)} %get-tuple-element.115.h, f32[32,64,128]{2,1,0:T(8,128)S(1)} %get-tuple-element.103.refs_0_, ...), custom_call_target="tpu_custom_call" | custom-call | bytes 3600000 | tf_op jit(solution)/shard_map/pallas_call | solution.py:458
  117.1 1.7 %collective-permute-start.42 = (s16[528,128]{1,0:T(8,128)(2,1)S(1)}, s16[528,128]{1,0:T(8,128)(2,1)S(1)}, u32[]{:S(2)}, u32[]{:S(2)}) collective-permute-start(s16[528,128]{1,0:T(8,128)(2,1)S(1)} %get-tuple-element.111), channel_id=1, source_target_pairs={{0,2},{1,3},{2,0},{3,1},{4,6},{5,7},{6,4},{7,5},{8,10},{9,11},{10,... | collective-permute-start | bytes 405512 | tf_op jit(solution)/shard_map/ppermute | solution.py:362
  118.8 1.3 %collective-permute-done.37.refs_7_ = s16[528,128]{1,0:T(8,128)(2,1)S(1)} collective-permute-done((s16[528,128]{1,0:T(8,128)(2,1)S(1)}, s16[528,128]{1,0:T(8,128)(2,1)S(1)}, u32[]{:S(2)}, u32[]{:S(2)}) %collective-permute-start.37) | collective-permute-done | bytes 135200 | tf_op jit(solution)/shard_map/ppermute | solution.py:362
  120.2 3.7 %collective-permute-done.42.refs_10_ = s16[528,128]{1,0:T(8,128)(2,1)S(1)} collective-permute-done((s16[528,128]{1,0:T(8,128)(2,1)S(1)}, s16[528,128]{1,0:T(8,128)(2,1)S(1)}, u32[]{:S(2)}, u32[]{:S(2)}) %collective-permute-start.42) | collective-permute-done | bytes 135200 | tf_op jit(solution)/shard_map/ppermute | solution.py:362
  123.9 2.0 %collective-permute-done.43.refs_11_ = s16[528,128]{1,0:T(8,128)(2,1)S(1)} collective-permute-done((s16[528,128]{1,0:T(8,128)(2,1)S(1)}, s16[528,128]{1,0:T(8,128)(2,1)S(1)}, u32[]{:S(2)}, u32[]{:S(2)}) %collective-permute-start.43) | collective-permute-done | bytes 135200 | tf_op jit(solution)/shard_map/ppermute | solution.py:362
  125.9 2.3 %shard_map.71 = f32[2,256,1024]{2,1,0:T(8,128)} custom-call(s32[3]{0:T(128)S(1)} %pad_add_fusion.place, f32[64,2048]{1,0:T(8,128)S(1)} %get-tuple-element.59.refs_0_, f32[64,2048]{1,0:T(8,128)S(1)} %get-tuple-element.60.refs_1_, f32[64,2048]{1,0:T(8,128)S(1)} %get-tuple-element.61.refs_2_, f32[64,2048]{1,0:T(8,128)S(1)} %get-tuple-element.62.refs_3_, ...), custom_call_target="tpu_custom_call" | custom-call | tf_op jit(solution)/shard_map/pallas_call | solution.py:465
  (72 shorter events, 13.0 us)
Async XLA Ops:
  2.0 13.1 %collective-permute-start = (bf16[256,768]{1,0:T(8,128)(2,1)S(1)}, bf16[256,768]{1,0:T(8,128)(2,1)}, u32[]{:S(2)}, u32[]{:S(2)}) collective-permute-start(bf16[256,768]{1,0:T(8,128)(2,1)S(1)} %get-tuple-element.63.mine), channel_id=1, source_target_pairs={{0,4},{1,5},{2,6},{3,7},{4,0},{5,1},{6,2},{7,3},{8,12},{9,13},{10,... | collective-permute-start | bytes 1179656 | tf_op jit(solution)/shard_map/ppermute | solution.py:362
  5.0 17.5 %collective-permute-start.8 = (bf16[256,768]{1,0:T(8,128)(2,1)S(1)}, bf16[256,768]{1,0:T(8,128)(2,1)S(1)}, u32[]{:S(2)}, u32[]{:S(2)}) collective-permute-start(bf16[256,768]{1,0:T(8,128)(2,1)S(1)} %get-tuple-element.70.mine), channel_id=1, source_target_pairs={{0,4},{1,5},{2,6},{3,7},{4,0},{5,1},{6,2},{7,3},{8,12},{9,13},{10,... | collective-permute-start | bytes 1179656 | tf_op jit(solution)/shard_map/ppermute | solution.py:362
  5.1 22.8 %copy-start.2 = (f32[2,64,4096]{2,1,0:T(8,128)S(1)}, f32[2,64,4096]{2,1,0:T(8,128)}, u32[]{:S(2)}) copy-start(f32[2,64,4096]{2,1,0:T(8,128)} %h.1) | copy-start | bytes 6291460
  6.1 18.3 %collective-permute-start.2 = (f32[64,2048]{1,0:T(8,128)S(1)}, f32[64,2048]{1,0:T(8,128)S(1)}, u32[]{:S(2)}, u32[]{:S(2)}) collective-permute-start(f32[64,2048]{1,0:T(8,128)S(1)} %get-tuple-element.60.refs_1_), channel_id=1, source_target_pairs={{0,1},{1,0},{2,3},{3,2},{4,5},{5,4},{6,7},{7,6},{8,9},{9,8},{10,11... | collective-permute-start | bytes 1572872 | tf_op jit(solution)/shard_map/ppermute | solution.py:362
  6.2 23.3 %collective-permute-start.3 = (f32[64,2048]{1,0:T(8,128)S(1)}, f32[64,2048]{1,0:T(8,128)S(1)}, u32[]{:S(2)}, u32[]{:S(2)}) collective-permute-start(f32[64,2048]{1,0:T(8,128)S(1)} %get-tuple-element.61.refs_2_), channel_id=1, source_target_pairs={{0,2},{1,3},{2,0},{3,1},{4,6},{5,7},{6,4},{7,5},{8,10},{9,11},{10,... | collective-permute-start | bytes 1572872 | tf_op jit(solution)/shard_map/ppermute | solution.py:362
  8.2 23.4 %collective-permute-start.4 = (f32[64,2048]{1,0:T(8,128)S(1)}, f32[64,2048]{1,0:T(8,128)S(1)}, u32[]{:S(2)}, u32[]{:S(2)}) collective-permute-start(f32[64,2048]{1,0:T(8,128)S(1)} %get-tuple-element.62.refs_3_), channel_id=1, source_target_pairs={{0,3},{1,2},{2,1},{3,0},{4,7},{5,6},{6,5},{7,4},{8,11},{9,10},{10,... | collective-permute-start | bytes 1572872 | tf_op jit(solution)/shard_map/ppermute | solution.py:362
  15.1 17.7 %collective-permute-start.1 = (bf16[256,768]{1,0:T(8,128)(2,1)}, bf16[256,768]{1,0:T(8,128)(2,1)S(1)}, u32[]{:S(2)}, u32[]{:S(2)}) collective-permute-start(bf16[256,768]{1,0:T(8,128)(2,1)} %collective-permute-done.swap), channel_id=1, source_target_pairs={{0,8},{1,9},{2,10},{3,11},{4,28},{5,29},{6,30},{7,31},{8,16},{9,17... | collective-permute-start | bytes 1179656 | tf_op jit(solution)/shard_map/ppermute | solution.py:362
  22.5 14.2 %collective-permute-start.9 = (bf16[256,768]{1,0:T(8,128)(2,1)S(1)}, bf16[256,768]{1,0:T(8,128)(2,1)S(1)}, u32[]{:S(2)}, u32[]{:S(2)}) collective-permute-start(bf16[256,768]{1,0:T(8,128)(2,1)S(1)} %collective-permute-done.8.swap), channel_id=1, source_target_pairs={{0,8},{1,9},{2,10},{3,11},{4,28},{5,29},{6,30},{7,31},{8,16},{9,17... | collective-permute-start | bytes 1179656 | tf_op jit(solution)/shard_map/ppermute | solution.py:362
  24.4 4.2 %copy-start.3 = (bf16[2,4,128,128]{3,2,1,0:T(8,128)(2,1)S(1)}, bf16[2,4,128,128]{3,2,1,0:T(8,128)(2,1)}, u32[]{:S(2)}) copy-start(bf16[2,4,128,128]{3,2,1,0:T(8,128)(2,1)} %coupling.1) | copy-start | bytes 786436
  24.4 4.3 %copy-start.4 = (s32[2,4]{1,0:T(2,128)S(1)}, s32[2,4]{1,0:T(2,128)}, u32[]{:S(2)}) copy-start(s32[2,4]{1,0:T(2,128)} %donors.1) | copy-start | bytes 100
  24.4 4.3 %copy-start.5 = (s32[2]{0:T(128)S(1)}, s32[2]{0:T(128)}, u32[]{:S(2)}) copy-start(s32[2]{0:T(128)} %counts.1) | copy-start | bytes 28
  24.4 17.4 %collective-permute-start.14 = (bf16[256,512]{1,0:T(8,128)(2,1)S(1)}, bf16[256,512]{1,0:T(8,128)(2,1)S(1)}, u32[]{:S(2)}, u32[]{:S(2)}) collective-permute-start(bf16[256,512]{1,0:T(8,128)(2,1)S(1)} %get-tuple-element.76.mine), channel_id=1, source_target_pairs={{0,28},{1,29},{2,30},{3,31},{4,8},{5,9},{6,10},{7,11},{8,4},{9,5},... | collective-permute-start | bytes 786440 | tf_op jit(solution)/shard_map/ppermute | solution.py:362
  29.5 14.4 %collective-permute-start.13 = (bf16[256,512]{1,0:T(8,128)(2,1)S(1)}, bf16[256,512]{1,0:T(8,128)(2,1)S(1)}, u32[]{:S(2)}, u32[]{:S(2)}) collective-permute-start(bf16[256,512]{1,0:T(8,128)(2,1)S(1)} %get-tuple-element.76.mine), channel_id=1, source_target_pairs={{0,4},{1,5},{2,6},{3,7},{4,0},{5,1},{6,2},{7,3},{8,12},{9,13},{10,... | collective-permute-start | bytes 786440 | tf_op jit(solution)/shard_map/ppermute | solution.py:362
  34.5 7.4 %collective-permute-start.5 = (s16[400,128]{1,0:T(8,128)(2,1)S(1)}, s16[400,128]{1,0:T(8,128)(2,1)S(1)}, u32[]{:S(2)}, u32[]{:S(2)}) collective-permute-start(s16[400,128]{1,0:T(8,128)(2,1)S(1)} %get-tuple-element.67), channel_id=1, source_target_pairs={{0,1},{1,0},{2,3},{3,2},{4,5},{5,4},{6,7},{7,6},{8,9},{9,8},{10,11... | collective-permute-start | bytes 307208 | tf_op jit(solution)/shard_map/ppermute | solution.py:362
  35.0 8.5 %collective-permute-start.6 = (s16[400,128]{1,0:T(8,128)(2,1)S(1)}, s16[400,128]{1,0:T(8,128)(2,1)S(1)}, u32[]{:S(2)}, u32[]{:S(2)}) collective-permute-start(s16[400,128]{1,0:T(8,128)(2,1)S(1)} %get-tuple-element.68), channel_id=1, source_target_pairs={{0,2},{1,3},{2,0},{3,1},{4,6},{5,7},{6,4},{7,5},{8,10},{9,11},{10,... | collective-permute-start | bytes 307208 | tf_op jit(solution)/shard_map/ppermute | solution.py:362
  36.8 7.1 %collective-permute-start.7 = (s16[400,128]{1,0:T(8,128)(2,1)S(1)}, s16[400,128]{1,0:T(8,128)(2,1)S(1)}, u32[]{:S(2)}, u32[]{:S(2)}) collective-permute-start(s16[400,128]{1,0:T(8,128)(2,1)S(1)} %get-tuple-element.69), channel_id=1, source_target_pairs={{0,3},{1,2},{2,1},{3,0},{4,7},{5,6},{6,5},{7,4},{8,11},{9,10},{10,... | collective-permute-start | bytes 307208 | tf_op jit(solution)/shard_map/ppermute | solution.py:362
  41.8 5.1 %collective-permute-start.10 = (s16[400,128]{1,0:T(8,128)(2,1)S(1)}, s16[400,128]{1,0:T(8,128)(2,1)S(1)}, u32[]{:S(2)}, u32[]{:S(2)}) collective-permute-start(s16[400,128]{1,0:T(8,128)(2,1)S(1)} %get-tuple-element.73), channel_id=1, source_target_pairs={{0,1},{1,0},{2,3},{3,2},{4,5},{5,4},{6,7},{7,6},{8,9},{9,8},{10,11... | collective-permute-start | bytes 307208 | tf_op jit(solution)/shard_map/ppermute | solution.py:362
  41.9 5.7 %collective-permute-start.11 = (s16[400,128]{1,0:T(8,128)(2,1)S(1)}, s16[400,128]{1,0:T(8,128)(2,1)S(1)}, u32[]{:S(2)}, u32[]{:S(2)}) collective-permute-start(s16[400,128]{1,0:T(8,128)(2,1)S(1)} %get-tuple-element.74), channel_id=1, source_target_pairs={{0,2},{1,3},{2,0},{3,1},{4,6},{5,7},{6,4},{7,5},{8,10},{9,11},{10,... | collective-permute-start | bytes 307208 | tf_op jit(solution)/shard_map/ppermute | solution.py:362
  43.5 5.6 %collective-permute-start.12 = (s16[400,128]{1,0:T(8,128)(2,1)S(1)}, s16[400,128]{1,0:T(8,128)(2,1)S(1)}, u32[]{:S(2)}, u32[]{:S(2)}) collective-permute-start(s16[400,128]{1,0:T(8,128)(2,1)S(1)} %get-tuple-element.75), channel_id=1, source_target_pairs={{0,3},{1,2},{2,1},{3,0},{4,7},{5,6},{6,5},{7,4},{8,11},{9,10},{10,... | collective-permute-start | bytes 307208 | tf_op jit(solution)/shard_map/ppermute | solution.py:362
  45.0 4.1 %collective-permute-start.15 = (s16[272,128]{1,0:T(8,128)(2,1)S(1)}, s16[272,128]{1,0:T(8,128)(2,1)S(1)}, u32[]{:S(2)}, u32[]{:S(2)}) collective-permute-start(s16[272,128]{1,0:T(8,128)(2,1)S(1)} %get-tuple-element.79), channel_id=1, source_target_pairs={{0,1},{1,0},{2,3},{3,2},{4,5},{5,4},{6,7},{7,6},{8,9},{9,8},{10,11... | collective-permute-start | bytes 208904 | tf_op jit(solution)/shard_map/ppermute | solution.py:362
  45.4 6.0 %collective-permute-start.16 = (s16[272,128]{1,0:T(8,128)(2,1)S(1)}, s16[272,128]{1,0:T(8,128)(2,1)S(1)}, u32[]{:S(2)}, u32[]{:S(2)}) collective-permute-start(s16[272,128]{1,0:T(8,128)(2,1)S(1)} %get-tuple-element.80), channel_id=1, source_target_pairs={{0,2},{1,3},{2,0},{3,1},{4,6},{5,7},{6,4},{7,5},{8,10},{9,11},{10,... | collective-permute-start | bytes 208904 | tf_op jit(solution)/shard_map/ppermute | solution.py:362
  46.9 5.2 %collective-permute-start.17 = (s16[272,128]{1,0:T(8,128)(2,1)S(1)}, s16[272,128]{1,0:T(8,128)(2,1)S(1)}, u32[]{:S(2)}, u32[]{:S(2)}) collective-permute-start(s16[272,128]{1,0:T(8,128)(2,1)S(1)} %get-tuple-element.81), channel_id=1, source_target_pairs={{0,3},{1,2},{2,1},{3,0},{4,7},{5,6},{6,5},{7,4},{8,11},{9,10},{10,... | collective-permute-start | bytes 208904 | tf_op jit(solution)/shard_map/ppermute | solution.py:362
  54.0 5.9 %collective-permute-start.18 = (bf16[32,2048]{1,0:T(8,128)(2,1)S(1)}, bf16[32,2048]{1,0:T(8,128)(2,1)S(1)}, u32[]{:S(2)}, u32[]{:S(2)}) collective-permute-start(bf16[32,2048]{1,0:T(8,128)(2,1)S(1)} %get-tuple-element.84), channel_id=1, source_target_pairs={{0,1},{1,0},{2,3},{3,2},{4,5},{5,4},{6,7},{7,6},{8,9},{9,8},{10,11... | collective-permute-start | bytes 393224 | tf_op jit(solution)/shard_map/ppermute | solution.py:362
  54.2 6.3 %collective-permute-start.19 = (bf16[32,2048]{1,0:T(8,128)(2,1)S(1)}, bf16[32,2048]{1,0:T(8,128)(2,1)S(1)}, u32[]{:S(2)}, u32[]{:S(2)}) collective-permute-start(bf16[32,2048]{1,0:T(8,128)(2,1)S(1)} %get-tuple-element.85), channel_id=1, source_target_pairs={{0,2},{1,3},{2,0},{3,1},{4,6},{5,7},{6,4},{7,5},{8,10},{9,11},{10,... | collective-permute-start | bytes 393224 | tf_op jit(solution)/shard_map/ppermute | solution.py:362
  55.8 6.6 %collective-permute-start.20 = (bf16[32,2048]{1,0:T(8,128)(2,1)S(1)}, bf16[32,2048]{1,0:T(8,128)(2,1)S(1)}, u32[]{:S(2)}, u32[]{:S(2)}) collective-permute-start(bf16[32,2048]{1,0:T(8,128)(2,1)S(1)} %get-tuple-element.86), channel_id=1, source_target_pairs={{0,3},{1,2},{2,1},{3,0},{4,7},{5,6},{6,5},{7,4},{8,11},{9,10},{10,... | collective-permute-start | bytes 393224 | tf_op jit(solution)/shard_map/ppermute | solution.py:362
  57.8 6.8 %collective-permute-start.25 = (bf16[32,2048]{1,0:T(8,128)(2,1)S(1)}, bf16[32,2048]{1,0:T(8,128)(2,1)S(1)}, u32[]{:S(2)}, u32[]{:S(2)}) collective-permute-start(bf16[32,2048]{1,0:T(8,128)(2,1)S(1)} %get-tuple-element.90), channel_id=1, source_target_pairs={{0,1},{1,0},{2,3},{3,2},{4,5},{5,4},{6,7},{7,6},{8,9},{9,8},{10,11... | collective-permute-start | bytes 393224 | tf_op jit(solution)/shard_map/ppermute | solution.py:362
  58.3 7.8 %collective-permute-start.26 = (bf16[32,2048]{1,0:T(8,128)(2,1)S(1)}, bf16[32,2048]{1,0:T(8,128)(2,1)S(1)}, u32[]{:S(2)}, u32[]{:S(2)}) collective-permute-start(bf16[32,2048]{1,0:T(8,128)(2,1)S(1)} %get-tuple-element.91), channel_id=1, source_target_pairs={{0,2},{1,3},{2,0},{3,1},{4,6},{5,7},{6,4},{7,5},{8,10},{9,11},{10,... | collective-permute-start | bytes 393224 | tf_op jit(solution)/shard_map/ppermute | solution.py:362
  59.9 7.9 %collective-permute-start.27 = (bf16[32,2048]{1,0:T(8,128)(2,1)S(1)}, bf16[32,2048]{1,0:T(8,128)(2,1)S(1)}, u32[]{:S(2)}, u32[]{:S(2)}) collective-permute-start(bf16[32,2048]{1,0:T(8,128)(2,1)S(1)} %get-tuple-element.92), channel_id=1, source_target_pairs={{0,3},{1,2},{2,1},{3,0},{4,7},{5,6},{6,5},{7,4},{8,11},{9,10},{10,... | collective-permute-start | bytes 393224 | tf_op jit(solution)/shard_map/ppermute | solution.py:362
  62.4 9.8 %collective-permute-start.21 = (bf16[128,1024]{1,0:T(8,128)(2,1)S(1)}, bf16[128,1024]{1,0:T(8,128)(2,1)S(1)}, u32[]{:S(2)}, u32[]{:S(2)}) collective-permute-start(bf16[128,1024]{1,0:T(8,128)(2,1)S(1)} %get-tuple-element.87.refs_1_), channel_id=1, source_target_pairs={{0,4},{1,5},{2,6},{3,7},{4,0},{5,1},{6,2},{7,3},{8,12},{9,13},{10,... | collective-permute-start | bytes 786440 | tf_op jit(solution)/shard_map/ppermute | solution.py:362
  62.9 20.0 %collective-permute-start.23 = (bf16[128,1024]{1,0:T(8,128)(2,1)S(1)}, bf16[128,1024]{1,0:T(8,128)(2,1)S(1)}, u32[]{:S(2)}, u32[]{:S(2)}) collective-permute-start(bf16[128,1024]{1,0:T(8,128)(2,1)S(1)} %get-tuple-element.88.refs_4_), channel_id=1, source_target_pairs={{0,4},{1,5},{2,6},{3,7},{4,0},{5,1},{6,2},{7,3},{8,12},{9,13},{10,... | collective-permute-start | bytes 786440 | tf_op jit(solution)/shard_map/ppermute | solution.py:362
  67.8 20.8 %collective-permute-start.28 = (bf16[128,1024]{1,0:T(8,128)(2,1)S(1)}, bf16[128,1024]{1,0:T(8,128)(2,1)S(1)}, u32[]{:S(2)}, u32[]{:S(2)}) collective-permute-start(bf16[128,1024]{1,0:T(8,128)(2,1)S(1)} %get-tuple-element.93.refs_7_), channel_id=1, source_target_pairs={{0,4},{1,5},{2,6},{3,7},{4,0},{5,1},{6,2},{7,3},{8,12},{9,13},{10,... | collective-permute-start | bytes 786440 | tf_op jit(solution)/shard_map/ppermute | solution.py:362
  68.2 21.9 %collective-permute-start.31 = (bf16[128,1024]{1,0:T(8,128)(2,1)S(1)}, bf16[128,1024]{1,0:T(8,128)(2,1)S(1)}, u32[]{:S(2)}, u32[]{:S(2)}) collective-permute-start(bf16[128,1024]{1,0:T(8,128)(2,1)S(1)} %get-tuple-element.94.refs_10_), channel_id=1, source_target_pairs={{0,28},{1,29},{2,30},{3,31},{4,8},{5,9},{6,10},{7,11},{8,4},{9,5},... | collective-permute-start | bytes 786440 | tf_op jit(solution)/shard_map/ppermute | solution.py:362
  72.2 21.8 %collective-permute-start.30 = (bf16[128,1024]{1,0:T(8,128)(2,1)S(1)}, bf16[128,1024]{1,0:T(8,128)(2,1)S(1)}, u32[]{:S(2)}, u32[]{:S(2)}) collective-permute-start(bf16[128,1024]{1,0:T(8,128)(2,1)S(1)} %get-tuple-element.94.refs_10_), channel_id=1, source_target_pairs={{0,4},{1,5},{2,6},{3,7},{4,0},{5,1},{6,2},{7,3},{8,12},{9,13},{10,... | collective-permute-start | bytes 786440 | tf_op jit(solution)/shard_map/ppermute | solution.py:362
  72.2 21.7 %collective-permute-start.22 = (bf16[128,1024]{1,0:T(8,128)(2,1)S(1)}, bf16[128,1024]{1,0:T(8,128)(2,1)S(1)}, u32[]{:S(2)}, u32[]{:S(2)}) collective-permute-start(bf16[128,1024]{1,0:T(8,128)(2,1)S(1)} %collective-permute-done.21.refs_0_), channel_id=1, source_target_pairs={{0,8},{1,9},{2,10},{3,11},{4,28},{5,29},{6,30},{7,31},{8,16},{9,17... | collective-permute-start | bytes 786440 | tf_op jit(solution)/shard_map/ppermute | solution.py:362
  82.9 11.1 %collective-permute-start.24 = (bf16[128,1024]{1,0:T(8,128)(2,1)S(1)}, bf16[128,1024]{1,0:T(8,128)(2,1)S(1)}, u32[]{:S(2)}, u32[]{:S(2)}) collective-permute-start(bf16[128,1024]{1,0:T(8,128)(2,1)S(1)} %collective-permute-done.23.refs_3_), channel_id=1, source_target_pairs={{0,8},{1,9},{2,10},{3,11},{4,28},{5,29},{6,30},{7,31},{8,16},{9,17... | collective-permute-start | bytes 786440 | tf_op jit(solution)/shard_map/ppermute | solution.py:362
  88.5 9.8 %collective-permute-start.29 = (bf16[128,1024]{1,0:T(8,128)(2,1)S(1)}, bf16[128,1024]{1,0:T(8,128)(2,1)S(1)}, u32[]{:S(2)}, u32[]{:S(2)}) collective-permute-start(bf16[128,1024]{1,0:T(8,128)(2,1)S(1)} %collective-permute-done.28.refs_6_), channel_id=1, source_target_pairs={{0,8},{1,9},{2,10},{3,11},{4,28},{5,29},{6,30},{7,31},{8,16},{9,17... | collective-permute-start | bytes 786440 | tf_op jit(solution)/shard_map/ppermute | solution.py:362
  100.0 5.5 %collective-permute-start.32 = (s16[528,128]{1,0:T(8,128)(2,1)S(1)}, s16[528,128]{1,0:T(8,128)(2,1)S(1)}, u32[]{:S(2)}, u32[]{:S(2)}) collective-permute-start(s16[528,128]{1,0:T(8,128)(2,1)S(1)} %get-tuple-element.96), channel_id=1, source_target_pairs={{0,1},{1,0},{2,3},{3,2},{4,5},{5,4},{6,7},{7,6},{8,9},{9,8},{10,11... | collective-permute-start | bytes 405512 | tf_op jit(solution)/shard_map/ppermute | solution.py:362
  100.0 6.5 %collective-permute-start.33 = (s16[528,128]{1,0:T(8,128)(2,1)S(1)}, s16[528,128]{1,0:T(8,128)(2,1)S(1)}, u32[]{:S(2)}, u32[]{:S(2)}) collective-permute-start(s16[528,128]{1,0:T(8,128)(2,1)S(1)} %get-tuple-element.97), channel_id=1, source_target_pairs={{0,2},{1,3},{2,0},{3,1},{4,6},{5,7},{6,4},{7,5},{8,10},{9,11},{10,... | collective-permute-start | bytes 405512 | tf_op jit(solution)/shard_map/ppermute | solution.py:362
  101.8 6.8 %collective-permute-start.34 = (s16[528,128]{1,0:T(8,128)(2,1)S(1)}, s16[528,128]{1,0:T(8,128)(2,1)S(1)}, u32[]{:S(2)}, u32[]{:S(2)}) collective-permute-start(s16[528,128]{1,0:T(8,128)(2,1)S(1)} %get-tuple-element.98), channel_id=1, source_target_pairs={{0,3},{1,2},{2,1},{3,0},{4,7},{5,6},{6,5},{7,4},{8,11},{9,10},{10,... | collective-permute-start | bytes 405512 | tf_op jit(solution)/shard_map/ppermute | solution.py:362
  103.3 9.7 %collective-permute-start.38 = (s16[528,128]{1,0:T(8,128)(2,1)S(1)}, s16[528,128]{1,0:T(8,128)(2,1)S(1)}, u32[]{:S(2)}, u32[]{:S(2)}) collective-permute-start(s16[528,128]{1,0:T(8,128)(2,1)S(1)} %get-tuple-element.106), channel_id=1, source_target_pairs={{0,1},{1,0},{2,3},{3,2},{4,5},{5,4},{6,7},{7,6},{8,9},{9,8},{10,11... | collective-permute-start | bytes 405512 | tf_op jit(solution)/shard_map/ppermute | solution.py:362
  103.8 9.3 %collective-permute-start.39 = (s16[528,128]{1,0:T(8,128)(2,1)S(1)}, s16[528,128]{1,0:T(8,128)(2,1)S(1)}, u32[]{:S(2)}, u32[]{:S(2)}) collective-permute-start(s16[528,128]{1,0:T(8,128)(2,1)S(1)} %get-tuple-element.107), channel_id=1, source_target_pairs={{0,2},{1,3},{2,0},{3,1},{4,6},{5,7},{6,4},{7,5},{8,10},{9,11},{10,... | collective-permute-start | bytes 405512 | tf_op jit(solution)/shard_map/ppermute | solution.py:362
  105.5 8.9 %collective-permute-start.40 = (s16[528,128]{1,0:T(8,128)(2,1)S(1)}, s16[528,128]{1,0:T(8,128)(2,1)S(1)}, u32[]{:S(2)}, u32[]{:S(2)}) collective-permute-start(s16[528,128]{1,0:T(8,128)(2,1)S(1)} %get-tuple-element.108), channel_id=1, source_target_pairs={{0,3},{1,2},{2,1},{3,0},{4,7},{5,6},{6,5},{7,4},{8,11},{9,10},{10,... | collective-permute-start | bytes 405512 | tf_op jit(solution)/shard_map/ppermute | solution.py:362
  110.7 8.2 %collective-permute-start.35 = (s16[528,128]{1,0:T(8,128)(2,1)S(1)}, s16[528,128]{1,0:T(8,128)(2,1)S(1)}, u32[]{:S(2)}, u32[]{:S(2)}) collective-permute-start(s16[528,128]{1,0:T(8,128)(2,1)S(1)} %get-tuple-element.100), channel_id=1, source_target_pairs={{0,1},{1,0},{2,3},{3,2},{4,5},{5,4},{6,7},{7,6},{8,9},{9,8},{10,11... | collective-permute-start | bytes 405512 | tf_op jit(solution)/shard_map/ppermute | solution.py:362
  111.3 7.5 %collective-permute-start.36 = (s16[528,128]{1,0:T(8,128)(2,1)S(1)}, s16[528,128]{1,0:T(8,128)(2,1)S(1)}, u32[]{:S(2)}, u32[]{:S(2)}) collective-permute-start(s16[528,128]{1,0:T(8,128)(2,1)S(1)} %get-tuple-element.101), channel_id=1, source_target_pairs={{0,2},{1,3},{2,0},{3,1},{4,6},{5,7},{6,4},{7,5},{8,10},{9,11},{10,... | collective-permute-start | bytes 405512 | tf_op jit(solution)/shard_map/ppermute | solution.py:362
  113.0 7.1 %collective-permute-start.37 = (s16[528,128]{1,0:T(8,128)(2,1)S(1)}, s16[528,128]{1,0:T(8,128)(2,1)S(1)}, u32[]{:S(2)}, u32[]{:S(2)}) collective-permute-start(s16[528,128]{1,0:T(8,128)(2,1)S(1)} %get-tuple-element.102), channel_id=1, source_target_pairs={{0,3},{1,2},{2,1},{3,0},{4,7},{5,6},{6,5},{7,4},{8,11},{9,10},{10,... | collective-permute-start | bytes 405512 | tf_op jit(solution)/shard_map/ppermute | solution.py:362
  116.5 3.7 %collective-permute-start.41 = (s16[528,128]{1,0:T(8,128)(2,1)S(1)}, s16[528,128]{1,0:T(8,128)(2,1)S(1)}, u32[]{:S(2)}, u32[]{:S(2)}) collective-permute-start(s16[528,128]{1,0:T(8,128)(2,1)S(1)} %get-tuple-element.110), channel_id=1, source_target_pairs={{0,1},{1,0},{2,3},{3,2},{4,5},{5,4},{6,7},{7,6},{8,9},{9,8},{10,11... | collective-permute-start | bytes 405512 | tf_op jit(solution)/shard_map/ppermute | solution.py:362
  117.1 6.7 %collective-permute-start.42 = (s16[528,128]{1,0:T(8,128)(2,1)S(1)}, s16[528,128]{1,0:T(8,128)(2,1)S(1)}, u32[]{:S(2)}, u32[]{:S(2)}) collective-permute-start(s16[528,128]{1,0:T(8,128)(2,1)S(1)} %get-tuple-element.111), channel_id=1, source_target_pairs={{0,2},{1,3},{2,0},{3,1},{4,6},{5,7},{6,4},{7,5},{8,10},{9,11},{10,... | collective-permute-start | bytes 405512 | tf_op jit(solution)/shard_map/ppermute | solution.py:362
  118.8 7.0 %collective-permute-start.43 = (s16[528,128]{1,0:T(8,128)(2,1)S(1)}, s16[528,128]{1,0:T(8,128)(2,1)S(1)}, u32[]{:S(2)}, u32[]{:S(2)}) collective-permute-start(s16[528,128]{1,0:T(8,128)(2,1)S(1)} %get-tuple-element.112), channel_id=1, source_target_pairs={{0,3},{1,2},{2,1},{3,0},{4,7},{5,6},{6,5},{7,4},{8,11},{9,10},{10,... | collective-permute-start | bytes 405512 | tf_op jit(solution)/shard_map/ppermute | solution.py:362
  (2 other events, 5.2 us)

commit v4 on v2

--- a/solution.py
+++ b/solution.py
@@ -252,7 +252,7 @@
         back[pl.ds(m, NB, stride=step), :] = value
         return carry
 
-    lax.fori_loop(0, count, body, 0, unroll=16)
+    lax.fori_loop(0, count, body, 0, unroll=True)
     own = outs[0].shape[1] // LANE
     for k, out in enumerate(outs):
         for a in range(own):
@@ -271,7 +271,7 @@
         back[pl.ds(m, NB, stride=step), :] = rate(h[m] + rows[pl.ds(m, NB, stride=step), :], s[m])
         return carry
 
-    lax.fori_loop(0, count, body, 0, unroll=16)
+    lax.fori_loop(0, count, body, 0, unroll=True)
     own = (outs[0].shape[0] - PACK) // count
     for k, out in enumerate(outs):
         first = (j ^ k) * own

time: 129 us -> 128 us (level)
  no operation moved by 1% of the time
where the time goes in v4:
time: 128 us
  waiting for transfers between devices  63.1 us (49%)
  starting transfers between devices  42.1 us (33%)
  Pallas kernels  20.6 us (16%)
  local copies, waits for them, and re-layouts  2.04 us (2%)
    ppermute x44, waiting for transfers between devices, move(): return lax.ppermute(value, ('ka', 'ba'), pairs_of)  63.1 us
    ppermute x44, starting transfers between devices, move(): return lax.ppermute(value, ('ka', 'ba'), pairs_of)  42.1 us
    pallas_call x2, Pallas kernels, local(): call(functools.partial(second_kernel, nb), [shape((own * count + PACK, LA...  3.81 us
    pallas_call x3, Pallas kernels, local(): call(field_one_kernel, [shape((widths[q] * band + PACK, LANE), i16)] * nb...  3.75 us
    pallas_call x2, Pallas kernels, local(): call(functools.partial(first_kernel, cuts, nb * cuts, c * count, band), [...  3.59 us
  transfers between devices with their start and end apart: 44, of which 24 were waited for; matrix products, arithmetic and copies ran while one was open for 0% of the time, Pallas kernels for 11%

profile of v4, /device:TPU:0, one launch (start us, length us, event | category | flops | bytes accessed | tf_op | source)
XLA Modules:
  0.0 128.3 jit_solution(6453202380987928892)
XLA Ops:
  0.1 1.6 %copy-done = f32[2,256,1024]{2,1,0:T(8,128)S(1)} copy-done((f32[2,256,1024]{2,1,0:T(8,128)S(1)}, f32[2,256,1024]{2,1,0:T(8,128)}, u32[]{:S(2)}) %copy-start) | copy-done | bytes 2097176
  3.7 3.0 %collective-permute-start = (bf16[256,768]{1,0:T(8,128)(2,1)S(1)}, bf16[256,768]{1,0:T(8,128)(2,1)S(1)}, u32[]{:S(2)}, u32[]{:S(2)}) collective-permute-start(bf16[256,768]{1,0:T(8,128)(2,1)S(1)} %get-tuple-element.64.mine), channel_id=1, source_target_pairs={{0,4},{1,5},{2,6},{3,7},{4,0},{5,1},{6,2},{7,3},{8,12},{9,13},{10,... | collective-permute-start | bytes 1179656 | tf_op jit(solution)/shard_map/ppermute | solution.py:357
  6.8 2.0 %collective-permute-start.3 = (f32[64,2048]{1,0:T(8,128)S(1)}, f32[64,2048]{1,0:T(8,128)S(1)}, u32[]{:S(2)}, u32[]{:S(2)}) collective-permute-start(f32[64,2048]{1,0:T(8,128)S(1)} %get-tuple-element.62.refs_2_), channel_id=1, source_target_pairs={{0,2},{1,3},{2,0},{3,1},{4,6},{5,7},{6,4},{7,5},{8,10},{9,11},{10,... | collective-permute-start | bytes 1572872 | tf_op jit(solution)/shard_map/ppermute | solution.py:357
  8.7 7.9 %collective-permute-done.swap = bf16[256,768]{1,0:T(8,128)(2,1)S(1)} collective-permute-done((bf16[256,768]{1,0:T(8,128)(2,1)S(1)}, bf16[256,768]{1,0:T(8,128)(2,1)S(1)}, u32[]{:S(2)}, u32[]{:S(2)}) %collective-permute-start) | collective-permute-done | bytes 393248 | tf_op jit(solution)/shard_map/ppermute | solution.py:357
  16.6 2.1 %collective-permute-start.1 = (bf16[256,768]{1,0:T(8,128)(2,1)S(1)}, bf16[256,768]{1,0:T(8,128)(2,1)S(1)}, u32[]{:S(2)}, u32[]{:S(2)}) collective-permute-start(bf16[256,768]{1,0:T(8,128)(2,1)S(1)} %collective-permute-done.swap), channel_id=1, source_target_pairs={{0,8},{1,9},{2,10},{3,11},{4,28},{5,29},{6,30},{7,31},{8,16},{9,17... | collective-permute-start | bytes 1179656 | tf_op jit(solution)/shard_map/ppermute | solution.py:357
  18.8 5.5 %collective-permute-done.8.swap = bf16[256,768]{1,0:T(8,128)(2,1)S(1)} collective-permute-done((bf16[256,768]{1,0:T(8,128)(2,1)S(1)}, bf16[256,768]{1,0:T(8,128)(2,1)S(1)}, u32[]{:S(2)}, u32[]{:S(2)}) %collective-permute-start.8) | collective-permute-done | bytes 393248 | tf_op jit(solution)/shard_map/ppermute | solution.py:357
  24.3 1.8 %collective-permute-start.9 = (bf16[256,768]{1,0:T(8,128)(2,1)S(1)}, bf16[256,768]{1,0:T(8,128)(2,1)S(1)}, u32[]{:S(2)}, u32[]{:S(2)}) collective-permute-start(bf16[256,768]{1,0:T(8,128)(2,1)S(1)} %collective-permute-done.8.swap), channel_id=1, source_target_pairs={{0,8},{1,9},{2,10},{3,11},{4,28},{5,29},{6,30},{7,31},{8,16},{9,17... | collective-permute-start | bytes 1179656 | tf_op jit(solution)/shard_map/ppermute | solution.py:357
  26.1 3.6 %collective-permute-start.13 = (bf16[256,512]{1,0:T(8,128)(2,1)S(1)}, bf16[256,512]{1,0:T(8,128)(2,1)S(1)}, u32[]{:S(2)}, u32[]{:S(2)}) collective-permute-start(bf16[256,512]{1,0:T(8,128)(2,1)S(1)} %get-tuple-element.77.mine), channel_id=1, source_target_pairs={{0,4},{1,5},{2,6},{3,7},{4,0},{5,1},{6,2},{7,3},{8,12},{9,13},{10,... | collective-permute-start | bytes 786440 | tf_op jit(solution)/shard_map/ppermute | solution.py:357
  31.3 1.1 shard_map.58
  32.4 2.5 %collective-permute-done.13.swap = bf16[256,512]{1,0:T(8,128)(2,1)S(1)} collective-permute-done((bf16[256,512]{1,0:T(8,128)(2,1)S(1)}, bf16[256,512]{1,0:T(8,128)(2,1)S(1)}, u32[]{:S(2)}, u32[]{:S(2)}) %collective-permute-start.13) | collective-permute-done | bytes 262176 | tf_op jit(solution)/shard_map/ppermute | solution.py:357
  34.9 1.3 %shard_map.60 = (s16[400,128]{1,0:T(8,128)(2,1)S(1)}, s16[400,128]{1,0:T(8,128)(2,1)S(1)}, s16[400,128]{1,0:T(8,128)(2,1)S(1)}, s16[400,128]{1,0:T(8,128)(2,1)S(1)}) custom-call(s32[3]{0:T(128)S(1)} %pad_add_fusion.place, bf16[256,768]{1,0:T(8,128)(2,1)S(1)} %shard_map.59.dense, bf16[256,768]{1,0:T(8,128)(2,1)S(1)} %get-tuple-element.64.mine, ...), custom_call_target="tpu_custom_call" | custom-call | bytes 3600000 | tf_op jit(solution)/shard_map/pallas_call | solution.py:397
  36.3 1.6 %collective-permute-start.6 = (s16[400,128]{1,0:T(8,128)(2,1)S(1)}, s16[400,128]{1,0:T(8,128)(2,1)S(1)}, u32[]{:S(2)}, u32[]{:S(2)}) collective-permute-start(s16[400,128]{1,0:T(8,128)(2,1)S(1)} %get-tuple-element.69), channel_id=1, source_target_pairs={{0,2},{1,3},{2,0},{3,1},{4,6},{5,7},{6,4},{7,5},{8,10},{9,11},{10,... | collective-permute-start | bytes 307208 | tf_op jit(solution)/shard_map/ppermute | solution.py:357
  38.2 1.3 %shard_map.61 = (s16[400,128]{1,0:T(8,128)(2,1)S(1)}, s16[400,128]{1,0:T(8,128)(2,1)S(1)}, s16[400,128]{1,0:T(8,128)(2,1)S(1)}, s16[400,128]{1,0:T(8,128)(2,1)S(1)}) custom-call(s32[3]{0:T(128)S(1)} %pad_add_fusion.place, bf16[256,768]{1,0:T(8,128)(2,1)S(1)} %shard_map.59.dense, bf16[256,768]{1,0:T(8,128)(2,1)S(1)} %get-tuple-element.71.mine, ...), custom_call_target="tpu_custom_call" | custom-call | bytes 3600000 | tf_op jit(solution)/shard_map/pallas_call | solution.py:397
  40.1 1.6 %collective-permute-start.11 = (s16[400,128]{1,0:T(8,128)(2,1)S(1)}, s16[400,128]{1,0:T(8,128)(2,1)S(1)}, u32[]{:S(2)}, u32[]{:S(2)}) collective-permute-start(s16[400,128]{1,0:T(8,128)(2,1)S(1)} %get-tuple-element.75), channel_id=1, source_target_pairs={{0,2},{1,3},{2,0},{3,1},{4,6},{5,7},{6,4},{7,5},{8,10},{9,11},{10,... | collective-permute-start | bytes 307208 | tf_op jit(solution)/shard_map/ppermute | solution.py:357
  43.4 1.1 shard_map.62
  45.3 1.5 %collective-permute-start.16 = (s16[272,128]{1,0:T(8,128)(2,1)S(1)}, s16[272,128]{1,0:T(8,128)(2,1)S(1)}, u32[]{:S(2)}, u32[]{:S(2)}) collective-permute-start(s16[272,128]{1,0:T(8,128)(2,1)S(1)} %get-tuple-element.82), channel_id=1, source_target_pairs={{0,2},{1,3},{2,0},{3,1},{4,6},{5,7},{6,4},{7,5},{8,10},{9,11},{10,... | collective-permute-start | bytes 208904 | tf_op jit(solution)/shard_map/ppermute | solution.py:357
  47.8 1.9 %collective-permute-done.16.refs_10_ = s16[272,128]{1,0:T(8,128)(2,1)S(1)} collective-permute-done((s16[272,128]{1,0:T(8,128)(2,1)S(1)}, s16[272,128]{1,0:T(8,128)(2,1)S(1)}, u32[]{:S(2)}, u32[]{:S(2)}) %collective-permute-start.16) | collective-permute-done | bytes 69664 | tf_op jit(solution)/shard_map/ppermute | solution.py:357
  49.7 1.6 %collective-permute-done.17.refs_11_ = s16[272,128]{1,0:T(8,128)(2,1)S(1)} collective-permute-done((s16[272,128]{1,0:T(8,128)(2,1)S(1)}, s16[272,128]{1,0:T(8,128)(2,1)S(1)}, u32[]{:S(2)}, u32[]{:S(2)}) %collective-permute-start.17) | collective-permute-done | bytes 69664 | tf_op jit(solution)/shard_map/ppermute | solution.py:357
  51.3 1.8 %shard_map.63 = (f32[32,64,128]{2,1,0:T(8,128)S(1)}, bf16[32,2048]{1,0:T(8,128)(2,1)S(1)}, bf16[32,2048]{1,0:T(8,128)(2,1)S(1)}, bf16[32,2048]{1,0:T(8,128)(2,1)S(1)}, bf16[32,2048]{1,0:T(8,128)(2,1)S(1)}) custom-call(s32[3]{0:T(128)S(1)} %pad_add_fusion.place, f32[32,64,128]{2,1,0:T(8,128)S(1)} %get-tuple-element.118.h, ...), custom_call_target="tpu_custom_call" | custom-call | bytes 3600000 | tf_op jit(solution)/shard_map/pallas_call | solution.py:412
  53.2 1.2 collective-permute-start.19
  55.0 1.8 %shard_map.65 = (f32[32,64,128]{2,1,0:T(8,128)S(1)}, bf16[32,2048]{1,0:T(8,128)(2,1)S(1)}, bf16[32,2048]{1,0:T(8,128)(2,1)S(1)}, bf16[32,2048]{1,0:T(8,128)(2,1)S(1)}, bf16[32,2048]{1,0:T(8,128)(2,1)S(1)}) custom-call(s32[3]{0:T(128)S(1)} %pad_add_fusion.place, f32[32,64,128]{2,1,0:T(8,128)S(1)} %get-tuple-element.117.h, ...), custom_call_target="tpu_custom_call" | custom-call | bytes 3600000 | tf_op jit(solution)/shard_map/pallas_call | solution.py:412
  57.3 1.2 collective-permute-start.26
  59.6 1.9 %collective-permute-done.20.refs_3_ = bf16[32,2048]{1,0:T(8,128)(2,1)S(1)} collective-permute-done((bf16[32,2048]{1,0:T(8,128)(2,1)S(1)}, bf16[32,2048]{1,0:T(8,128)(2,1)S(1)}, u32[]{:S(2)}, u32[]{:S(2)}) %collective-permute-start.20) | collective-permute-done | bytes 131104 | tf_op jit(solution)/shard_map/ppermute | solution.py:357
  61.5 2.6 %collective-permute-start.21 = (bf16[128,1024]{1,0:T(8,128)(2,1)S(1)}, bf16[128,1024]{1,0:T(8,128)(2,1)S(1)}, u32[]{:S(2)}, u32[]{:S(2)}) collective-permute-start(bf16[128,1024]{1,0:T(8,128)(2,1)S(1)} %get-tuple-element.89.refs_1_), channel_id=1, source_target_pairs={{0,4},{1,5},{2,6},{3,7},{4,0},{5,1},{6,2},{7,3},{8,12},{9,13},{10,... | collective-permute-start | bytes 786440 | tf_op jit(solution)/shard_map/ppermute | solution.py:357
  65.2 1.9 %collective-permute-done.27.refs_3_ = bf16[32,2048]{1,0:T(8,128)(2,1)S(1)} collective-permute-done((bf16[32,2048]{1,0:T(8,128)(2,1)S(1)}, bf16[32,2048]{1,0:T(8,128)(2,1)S(1)}, u32[]{:S(2)}, u32[]{:S(2)}) %collective-permute-start.27) | collective-permute-done | bytes 131104 | tf_op jit(solution)/shard_map/ppermute | solution.py:357
  67.1 2.6 %collective-permute-start.28 = (bf16[128,1024]{1,0:T(8,128)(2,1)S(1)}, bf16[128,1024]{1,0:T(8,128)(2,1)S(1)}, u32[]{:S(2)}, u32[]{:S(2)}) collective-permute-start(bf16[128,1024]{1,0:T(8,128)(2,1)S(1)} %get-tuple-element.95.refs_7_), channel_id=1, source_target_pairs={{0,4},{1,5},{2,6},{3,7},{4,0},{5,1},{6,2},{7,3},{8,12},{9,13},{10,... | collective-permute-start | bytes 786440 | tf_op jit(solution)/shard_map/ppermute | solution.py:357
  69.8 1.4 %collective-permute-done.21.refs_0_ = bf16[128,1024]{1,0:T(8,128)(2,1)S(1)} collective-permute-done((bf16[128,1024]{1,0:T(8,128)(2,1)S(1)}, bf16[128,1024]{1,0:T(8,128)(2,1)S(1)}, u32[]{:S(2)}, u32[]{:S(2)}) %collective-permute-start.21) | collective-permute-done | bytes 262176 | tf_op jit(solution)/shard_map/ppermute | solution.py:357
  71.2 1.2 collective-permute-start.22
  72.4 4.4 %collective-permute-done.23.refs_3_ = bf16[128,1024]{1,0:T(8,128)(2,1)S(1)} collective-permute-done((bf16[128,1024]{1,0:T(8,128)(2,1)S(1)}, bf16[128,1024]{1,0:T(8,128)(2,1)S(1)}, u32[]{:S(2)}, u32[]{:S(2)}) %collective-permute-start.23) | collective-permute-done | bytes 262176 | tf_op jit(solution)/shard_map/ppermute | solution.py:357
  76.8 1.2 collective-permute-start.24
  78.0 4.4 %collective-permute-done.28.refs_6_ = bf16[128,1024]{1,0:T(8,128)(2,1)S(1)} collective-permute-done((bf16[128,1024]{1,0:T(8,128)(2,1)S(1)}, bf16[128,1024]{1,0:T(8,128)(2,1)S(1)}, u32[]{:S(2)}, u32[]{:S(2)}) %collective-permute-start.28) | collective-permute-done | bytes 262176 | tf_op jit(solution)/shard_map/ppermute | solution.py:357
  82.4 1.2 collective-permute-start.29
  83.6 4.4 %collective-permute-done.30.refs_9_ = bf16[128,1024]{1,0:T(8,128)(2,1)S(1)} collective-permute-done((bf16[128,1024]{1,0:T(8,128)(2,1)S(1)}, bf16[128,1024]{1,0:T(8,128)(2,1)S(1)}, u32[]{:S(2)}, u32[]{:S(2)}) %collective-permute-start.30) | collective-permute-done | bytes 262176 | tf_op jit(solution)/shard_map/ppermute | solution.py:357
  88.0 1.2 collective-permute-start.31
  89.2 3.4 %collective-permute-done.29.refs_8_ = bf16[128,1024]{1,0:T(8,128)(2,1)S(1)} collective-permute-done((bf16[128,1024]{1,0:T(8,128)(2,1)S(1)}, bf16[128,1024]{1,0:T(8,128)(2,1)S(1)}, u32[]{:S(2)}, u32[]{:S(2)}) %collective-permute-start.29) | collective-permute-done | bytes 262176 | tf_op jit(solution)/shard_map/ppermute | solution.py:357
  92.6 5.6 %collective-permute-done.31.refs_11_ = bf16[128,1024]{1,0:T(8,128)(2,1)S(1)} collective-permute-done((bf16[128,1024]{1,0:T(8,128)(2,1)S(1)}, bf16[128,1024]{1,0:T(8,128)(2,1)S(1)}, u32[]{:S(2)}, u32[]{:S(2)}) %collective-permute-start.31) | collective-permute-done | bytes 262176 | tf_op jit(solution)/shard_map/ppermute | solution.py:357
  98.2 1.6 %shard_map.67 = (s16[528,128]{1,0:T(8,128)(2,1)S(1)}, s16[528,128]{1,0:T(8,128)(2,1)S(1)}, s16[528,128]{1,0:T(8,128)(2,1)S(1)}, s16[528,128]{1,0:T(8,128)(2,1)S(1)}, bf16[768,2048]{1,0:T(8,128)(2,1)S(1)}) custom-call(s32[3]{0:T(128)S(1)} %pad_add_fusion.place, bf16[256,768]{1,0:T(8,128)(2,1)S(1)} %shard_map.59.dense, ...), custom_call_target="tpu_custom_call" | custom-call | bytes 3600000 | tf_op jit(solution)/shard_map/pallas_call | solution.py:430
  100.8 1.1 collective-permute-start.34
  101.8 1.4 %shard_map.69 = (s16[528,128]{1,0:T(8,128)(2,1)S(1)}, s16[528,128]{1,0:T(8,128)(2,1)S(1)}, s16[528,128]{1,0:T(8,128)(2,1)S(1)}, s16[528,128]{1,0:T(8,128)(2,1)S(1)}) custom-call(s32[3]{0:T(128)S(1)} %pad_add_fusion.place, bf16[256,768]{1,0:T(8,128)(2,1)S(1)} %shard_map.59.dense, bf16[768,2048]{1,0:T(8,128)(2,1)S(1)} %get-tuple-element.106.window), custom_call_target="tpu_custom_call" | custom-call | bytes 3600000 | tf_op jit(solution)/shard_map/pallas_call | solution.py:437
  105.2 1.2 collective-permute-done.33.refs_2_
  106.4 2.0 %collective-permute-done.34.refs_3_ = s16[528,128]{1,0:T(8,128)(2,1)S(1)} collective-permute-done((s16[528,128]{1,0:T(8,128)(2,1)S(1)}, s16[528,128]{1,0:T(8,128)(2,1)S(1)}, u32[]{:S(2)}, u32[]{:S(2)}) %collective-permute-start.34) | collective-permute-done | bytes 135200 | tf_op jit(solution)/shard_map/ppermute | solution.py:357
  108.4 1.9 %shard_map.68 = (s16[528,128]{1,0:T(8,128)(2,1)S(1)}, s16[528,128]{1,0:T(8,128)(2,1)S(1)}, s16[528,128]{1,0:T(8,128)(2,1)S(1)}, s16[528,128]{1,0:T(8,128)(2,1)S(1)}) custom-call(s32[3]{0:T(128)S(1)} %pad_add_fusion.place, f32[32,64,128]{2,1,0:T(8,128)S(1)} %get-tuple-element.118.h, f32[32,64,128]{2,1,0:T(8,128)S(1)} %get-tuple-element.84.s, ...), custom_call_target="tpu_custom_call" | custom-call | bytes 3600000 | tf_op jit(solution)/shard_map/pallas_call | solution.py:442
  112.6 1.7 %collective-permute-done.40.refs_3_ = s16[528,128]{1,0:T(8,128)(2,1)S(1)} collective-permute-done((s16[528,128]{1,0:T(8,128)(2,1)S(1)}, s16[528,128]{1,0:T(8,128)(2,1)S(1)}, u32[]{:S(2)}, u32[]{:S(2)}) %collective-permute-start.40) | collective-permute-done | bytes 135200 | tf_op jit(solution)/shard_map/ppermute | solution.py:357
  114.2 1.9 %shard_map.70 = (s16[528,128]{1,0:T(8,128)(2,1)S(1)}, s16[528,128]{1,0:T(8,128)(2,1)S(1)}, s16[528,128]{1,0:T(8,128)(2,1)S(1)}, s16[528,128]{1,0:T(8,128)(2,1)S(1)}) custom-call(s32[3]{0:T(128)S(1)} %pad_add_fusion.place, f32[32,64,128]{2,1,0:T(8,128)S(1)} %get-tuple-element.117.h, f32[32,64,128]{2,1,0:T(8,128)S(1)} %get-tuple-element.105.s, ...), custom_call_target="tpu_custom_call" | custom-call | bytes 3600000 | tf_op jit(solution)/shard_map/pallas_call | solution.py:442
  118.4 1.7 %collective-permute-done.37.refs_7_ = s16[528,128]{1,0:T(8,128)(2,1)S(1)} collective-permute-done((s16[528,128]{1,0:T(8,128)(2,1)S(1)}, s16[528,128]{1,0:T(8,128)(2,1)S(1)}, u32[]{:S(2)}, u32[]{:S(2)}) %collective-permute-start.37) | collective-permute-done | bytes 135200 | tf_op jit(solution)/shard_map/ppermute | solution.py:357
  120.0 3.8 %collective-permute-done.42.refs_10_ = s16[528,128]{1,0:T(8,128)(2,1)S(1)} collective-permute-done((s16[528,128]{1,0:T(8,128)(2,1)S(1)}, s16[528,128]{1,0:T(8,128)(2,1)S(1)}, u32[]{:S(2)}, u32[]{:S(2)}) %collective-permute-start.42) | collective-permute-done | bytes 135200 | tf_op jit(solution)/shard_map/ppermute | solution.py:357
  123.8 2.0 %collective-permute-done.43.refs_11_ = s16[528,128]{1,0:T(8,128)(2,1)S(1)} collective-permute-done((s16[528,128]{1,0:T(8,128)(2,1)S(1)}, s16[528,128]{1,0:T(8,128)(2,1)S(1)}, u32[]{:S(2)}, u32[]{:S(2)}) %collective-permute-start.43) | collective-permute-done | bytes 135200 | tf_op jit(solution)/shard_map/ppermute | solution.py:357
  125.8 2.3 %shard_map.71 = f32[2,256,1024]{2,1,0:T(8,128)} custom-call(s32[3]{0:T(128)S(1)} %pad_add_fusion.place, f32[64,2048]{1,0:T(8,128)S(1)} %get-tuple-element.60.refs_0_, f32[64,2048]{1,0:T(8,128)S(1)} %get-tuple-element.61.refs_1_, f32[64,2048]{1,0:T(8,128)S(1)} %get-tuple-element.62.refs_2_, f32[64,2048]{1,0:T(8,128)S(1)} %get-tuple-element.63.refs_3_, ...), custom_call_target="tpu_custom_call" | custom-call | tf_op jit(solution)/shard_map/pallas_call | solution.py:449
  (72 shorter events, 18.9 us)
Async XLA Ops:
  1.7 28.0 %copy-start.2 = (f32[2,64,4096]{2,1,0:T(8,128)S(1)}, f32[2,64,4096]{2,1,0:T(8,128)}, u32[]{:S(2)}) copy-start(f32[2,64,4096]{2,1,0:T(8,128)} %h.1) | copy-start | bytes 6291460
  2.6 23.5 %collective-permute-start.2 = (f32[64,2048]{1,0:T(8,128)S(1)}, f32[64,2048]{1,0:T(8,128)S(1)}, u32[]{:S(2)}, u32[]{:S(2)}) collective-permute-start(f32[64,2048]{1,0:T(8,128)S(1)} %get-tuple-element.61.refs_1_), channel_id=1, source_target_pairs={{0,1},{1,0},{2,3},{3,2},{4,5},{5,4},{6,7},{7,6},{8,9},{9,8},{10,11... | collective-permute-start | bytes 1572872 | tf_op jit(solution)/shard_map/ppermute | solution.py:357
  3.7 12.9 %collective-permute-start = (bf16[256,768]{1,0:T(8,128)(2,1)S(1)}, bf16[256,768]{1,0:T(8,128)(2,1)S(1)}, u32[]{:S(2)}, u32[]{:S(2)}) collective-permute-start(bf16[256,768]{1,0:T(8,128)(2,1)S(1)} %get-tuple-element.64.mine), channel_id=1, source_target_pairs={{0,4},{1,5},{2,6},{3,7},{4,0},{5,1},{6,2},{7,3},{8,12},{9,13},{10,... | collective-permute-start | bytes 1179656 | tf_op jit(solution)/shard_map/ppermute | solution.py:357
  6.7 17.6 %collective-permute-start.8 = (bf16[256,768]{1,0:T(8,128)(2,1)S(1)}, bf16[256,768]{1,0:T(8,128)(2,1)S(1)}, u32[]{:S(2)}, u32[]{:S(2)}) collective-permute-start(bf16[256,768]{1,0:T(8,128)(2,1)S(1)} %get-tuple-element.71.mine), channel_id=1, source_target_pairs={{0,4},{1,5},{2,6},{3,7},{4,0},{5,1},{6,2},{7,3},{8,12},{9,13},{10,... | collective-permute-start | bytes 1179656 | tf_op jit(solution)/shard_map/ppermute | solution.py:357
  6.8 24.6 %collective-permute-start.3 = (f32[64,2048]{1,0:T(8,128)S(1)}, f32[64,2048]{1,0:T(8,128)S(1)}, u32[]{:S(2)}, u32[]{:S(2)}) collective-permute-start(f32[64,2048]{1,0:T(8,128)S(1)} %get-tuple-element.62.refs_2_), channel_id=1, source_target_pairs={{0,2},{1,3},{2,0},{3,1},{4,6},{5,7},{6,4},{7,5},{8,10},{9,11},{10,... | collective-permute-start | bytes 1572872 | tf_op jit(solution)/shard_map/ppermute | solution.py:357
  8.7 22.6 %collective-permute-start.4 = (f32[64,2048]{1,0:T(8,128)S(1)}, f32[64,2048]{1,0:T(8,128)S(1)}, u32[]{:S(2)}, u32[]{:S(2)}) collective-permute-start(f32[64,2048]{1,0:T(8,128)S(1)} %get-tuple-element.63.refs_3_), channel_id=1, source_target_pairs={{0,3},{1,2},{2,1},{3,0},{4,7},{5,6},{6,5},{7,4},{8,11},{9,10},{10,... | collective-permute-start | bytes 1572872 | tf_op jit(solution)/shard_map/ppermute | solution.py:357
  16.6 18.3 %collective-permute-start.1 = (bf16[256,768]{1,0:T(8,128)(2,1)S(1)}, bf16[256,768]{1,0:T(8,128)(2,1)S(1)}, u32[]{:S(2)}, u32[]{:S(2)}) collective-permute-start(bf16[256,768]{1,0:T(8,128)(2,1)S(1)} %collective-permute-done.swap), channel_id=1, source_target_pairs={{0,8},{1,9},{2,10},{3,11},{4,28},{5,29},{6,30},{7,31},{8,16},{9,17... | collective-permute-start | bytes 1179656 | tf_op jit(solution)/shard_map/ppermute | solution.py:357
  24.3 13.9 %collective-permute-start.9 = (bf16[256,768]{1,0:T(8,128)(2,1)S(1)}, bf16[256,768]{1,0:T(8,128)(2,1)S(1)}, u32[]{:S(2)}, u32[]{:S(2)}) collective-permute-start(bf16[256,768]{1,0:T(8,128)(2,1)S(1)} %collective-permute-done.8.swap), channel_id=1, source_target_pairs={{0,8},{1,9},{2,10},{3,11},{4,28},{5,29},{6,30},{7,31},{8,16},{9,17... | collective-permute-start | bytes 1179656 | tf_op jit(solution)/shard_map/ppermute | solution.py:357
  26.1 4.4 %copy-start.3 = (bf16[2,4,128,128]{3,2,1,0:T(8,128)(2,1)S(1)}, bf16[2,4,128,128]{3,2,1,0:T(8,128)(2,1)}, u32[]{:S(2)}) copy-start(bf16[2,4,128,128]{3,2,1,0:T(8,128)(2,1)} %coupling.1) | copy-start | bytes 786436
  26.1 4.4 %copy-start.4 = (s32[2,4]{1,0:T(2,128)S(1)}, s32[2,4]{1,0:T(2,128)}, u32[]{:S(2)}) copy-start(s32[2,4]{1,0:T(2,128)} %donors.1) | copy-start | bytes 100
  26.1 4.4 %copy-start.5 = (s32[2]{0:T(128)S(1)}, s32[2]{0:T(128)}, u32[]{:S(2)}) copy-start(s32[2]{0:T(128)} %counts.1) | copy-start | bytes 28
  26.1 8.8 %collective-permute-start.13 = (bf16[256,512]{1,0:T(8,128)(2,1)S(1)}, bf16[256,512]{1,0:T(8,128)(2,1)S(1)}, u32[]{:S(2)}, u32[]{:S(2)}) collective-permute-start(bf16[256,512]{1,0:T(8,128)(2,1)S(1)} %get-tuple-element.77.mine), channel_id=1, source_target_pairs={{0,4},{1,5},{2,6},{3,7},{4,0},{5,1},{6,2},{7,3},{8,12},{9,13},{10,... | collective-permute-start | bytes 786440 | tf_op jit(solution)/shard_map/ppermute | solution.py:357
  34.9 8.4 %collective-permute-start.14 = (bf16[256,512]{1,0:T(8,128)(2,1)S(1)}, bf16[256,512]{1,0:T(8,128)(2,1)S(1)}, u32[]{:S(2)}, u32[]{:S(2)}) collective-permute-start(bf16[256,512]{1,0:T(8,128)(2,1)S(1)} %collective-permute-done.13.swap), channel_id=1, source_target_pairs={{0,8},{1,9},{2,10},{3,11},{4,28},{5,29},{6,30},{7,31},{8,16},{9,17... | collective-permute-start | bytes 786440 | tf_op jit(solution)/shard_map/ppermute | solution.py:357
  36.2 3.8 %collective-permute-start.5 = (s16[400,128]{1,0:T(8,128)(2,1)S(1)}, s16[400,128]{1,0:T(8,128)(2,1)S(1)}, u32[]{:S(2)}, u32[]{:S(2)}) collective-permute-start(s16[400,128]{1,0:T(8,128)(2,1)S(1)} %get-tuple-element.68), channel_id=1, source_target_pairs={{0,1},{1,0},{2,3},{3,2},{4,5},{5,4},{6,7},{7,6},{8,9},{9,8},{10,11... | collective-permute-start | bytes 307208 | tf_op jit(solution)/shard_map/ppermute | solution.py:357
  36.3 5.7 %collective-permute-start.6 = (s16[400,128]{1,0:T(8,128)(2,1)S(1)}, s16[400,128]{1,0:T(8,128)(2,1)S(1)}, u32[]{:S(2)}, u32[]{:S(2)}) collective-permute-start(s16[400,128]{1,0:T(8,128)(2,1)S(1)} %get-tuple-element.69), channel_id=1, source_target_pairs={{0,2},{1,3},{2,0},{3,1},{4,6},{5,7},{6,4},{7,5},{8,10},{9,11},{10,... | collective-permute-start | bytes 307208 | tf_op jit(solution)/shard_map/ppermute | solution.py:357
  37.9 5.5 %collective-permute-start.7 = (s16[400,128]{1,0:T(8,128)(2,1)S(1)}, s16[400,128]{1,0:T(8,128)(2,1)S(1)}, u32[]{:S(2)}, u32[]{:S(2)}) collective-permute-start(s16[400,128]{1,0:T(8,128)(2,1)S(1)} %get-tuple-element.70), channel_id=1, source_target_pairs={{0,3},{1,2},{2,1},{3,0},{4,7},{5,6},{6,5},{7,4},{8,11},{9,10},{10,... | collective-permute-start | bytes 307208 | tf_op jit(solution)/shard_map/ppermute | solution.py:357
  39.5 7.3 %collective-permute-start.10 = (s16[400,128]{1,0:T(8,128)(2,1)S(1)}, s16[400,128]{1,0:T(8,128)(2,1)S(1)}, u32[]{:S(2)}, u32[]{:S(2)}) collective-permute-start(s16[400,128]{1,0:T(8,128)(2,1)S(1)} %get-tuple-element.74), channel_id=1, source_target_pairs={{0,1},{1,0},{2,3},{3,2},{4,5},{5,4},{6,7},{7,6},{8,9},{9,8},{10,11... | collective-permute-start | bytes 307208 | tf_op jit(solution)/shard_map/ppermute | solution.py:357
  40.1 6.9 %collective-permute-start.11 = (s16[400,128]{1,0:T(8,128)(2,1)S(1)}, s16[400,128]{1,0:T(8,128)(2,1)S(1)}, u32[]{:S(2)}, u32[]{:S(2)}) collective-permute-start(s16[400,128]{1,0:T(8,128)(2,1)S(1)} %get-tuple-element.75), channel_id=1, source_target_pairs={{0,2},{1,3},{2,0},{3,1},{4,6},{5,7},{6,4},{7,5},{8,10},{9,11},{10,... | collective-permute-start | bytes 307208 | tf_op jit(solution)/shard_map/ppermute | solution.py:357
  42.1 5.7 %collective-permute-start.12 = (s16[400,128]{1,0:T(8,128)(2,1)S(1)}, s16[400,128]{1,0:T(8,128)(2,1)S(1)}, u32[]{:S(2)}, u32[]{:S(2)}) collective-permute-start(s16[400,128]{1,0:T(8,128)(2,1)S(1)} %get-tuple-element.76), channel_id=1, source_target_pairs={{0,3},{1,2},{2,1},{3,0},{4,7},{5,6},{6,5},{7,4},{8,11},{9,10},{10,... | collective-permute-start | bytes 307208 | tf_op jit(solution)/shard_map/ppermute | solution.py:357
  44.5 3.2 %collective-permute-start.15 = (s16[272,128]{1,0:T(8,128)(2,1)S(1)}, s16[272,128]{1,0:T(8,128)(2,1)S(1)}, u32[]{:S(2)}, u32[]{:S(2)}) collective-permute-start(s16[272,128]{1,0:T(8,128)(2,1)S(1)} %get-tuple-element.81), channel_id=1, source_target_pairs={{0,1},{1,0},{2,3},{3,2},{4,5},{5,4},{6,7},{7,6},{8,9},{9,8},{10,11... | collective-permute-start | bytes 208904 | tf_op jit(solution)/shard_map/ppermute | solution.py:357
  45.3 4.4 %collective-permute-start.16 = (s16[272,128]{1,0:T(8,128)(2,1)S(1)}, s16[272,128]{1,0:T(8,128)(2,1)S(1)}, u32[]{:S(2)}, u32[]{:S(2)}) collective-permute-start(s16[272,128]{1,0:T(8,128)(2,1)S(1)} %get-tuple-element.82), channel_id=1, source_target_pairs={{0,2},{1,3},{2,0},{3,1},{4,6},{5,7},{6,4},{7,5},{8,10},{9,11},{10,... | collective-permute-start | bytes 208904 | tf_op jit(solution)/shard_map/ppermute | solution.py:357
  46.8 4.5 %collective-permute-start.17 = (s16[272,128]{1,0:T(8,128)(2,1)S(1)}, s16[272,128]{1,0:T(8,128)(2,1)S(1)}, u32[]{:S(2)}, u32[]{:S(2)}) collective-permute-start(s16[272,128]{1,0:T(8,128)(2,1)S(1)} %get-tuple-element.83), channel_id=1, source_target_pairs={{0,3},{1,2},{2,1},{3,0},{4,7},{5,6},{6,5},{7,4},{8,11},{9,10},{10,... | collective-permute-start | bytes 208904 | tf_op jit(solution)/shard_map/ppermute | solution.py:357
  53.1 5.3 %collective-permute-start.18 = (bf16[32,2048]{1,0:T(8,128)(2,1)S(1)}, bf16[32,2048]{1,0:T(8,128)(2,1)S(1)}, u32[]{:S(2)}, u32[]{:S(2)}) collective-permute-start(bf16[32,2048]{1,0:T(8,128)(2,1)S(1)} %get-tuple-element.86), channel_id=1, source_target_pairs={{0,1},{1,0},{2,3},{3,2},{4,5},{5,4},{6,7},{7,6},{8,9},{9,8},{10,11... | collective-permute-start | bytes 393224 | tf_op jit(solution)/shard_map/ppermute | solution.py:357
  53.2 6.3 %collective-permute-start.19 = (bf16[32,2048]{1,0:T(8,128)(2,1)S(1)}, bf16[32,2048]{1,0:T(8,128)(2,1)S(1)}, u32[]{:S(2)}, u32[]{:S(2)}) collective-permute-start(bf16[32,2048]{1,0:T(8,128)(2,1)S(1)} %get-tuple-element.87), channel_id=1, source_target_pairs={{0,2},{1,3},{2,0},{3,1},{4,6},{5,7},{6,4},{7,5},{8,10},{9,11},{10,... | collective-permute-start | bytes 393224 | tf_op jit(solution)/shard_map/ppermute | solution.py:357
  54.4 7.0 %collective-permute-start.20 = (bf16[32,2048]{1,0:T(8,128)(2,1)S(1)}, bf16[32,2048]{1,0:T(8,128)(2,1)S(1)}, u32[]{:S(2)}, u32[]{:S(2)}) collective-permute-start(bf16[32,2048]{1,0:T(8,128)(2,1)S(1)} %get-tuple-element.88), channel_id=1, source_target_pairs={{0,3},{1,2},{2,1},{3,0},{4,7},{5,6},{6,5},{7,4},{8,11},{9,10},{10,... | collective-permute-start | bytes 393224 | tf_op jit(solution)/shard_map/ppermute | solution.py:357
  56.8 7.3 %collective-permute-start.25 = (bf16[32,2048]{1,0:T(8,128)(2,1)S(1)}, bf16[32,2048]{1,0:T(8,128)(2,1)S(1)}, u32[]{:S(2)}, u32[]{:S(2)}) collective-permute-start(bf16[32,2048]{1,0:T(8,128)(2,1)S(1)} %get-tuple-element.92), channel_id=1, source_target_pairs={{0,1},{1,0},{2,3},{3,2},{4,5},{5,4},{6,7},{7,6},{8,9},{9,8},{10,11... | collective-permute-start | bytes 393224 | tf_op jit(solution)/shard_map/ppermute | solution.py:357
  57.3 7.9 %collective-permute-start.26 = (bf16[32,2048]{1,0:T(8,128)(2,1)S(1)}, bf16[32,2048]{1,0:T(8,128)(2,1)S(1)}, u32[]{:S(2)}, u32[]{:S(2)}) collective-permute-start(bf16[32,2048]{1,0:T(8,128)(2,1)S(1)} %get-tuple-element.93), channel_id=1, source_target_pairs={{0,2},{1,3},{2,0},{3,1},{4,6},{5,7},{6,4},{7,5},{8,10},{9,11},{10,... | collective-permute-start | bytes 393224 | tf_op jit(solution)/shard_map/ppermute | solution.py:357
  58.4 8.6 %collective-permute-start.27 = (bf16[32,2048]{1,0:T(8,128)(2,1)S(1)}, bf16[32,2048]{1,0:T(8,128)(2,1)S(1)}, u32[]{:S(2)}, u32[]{:S(2)}) collective-permute-start(bf16[32,2048]{1,0:T(8,128)(2,1)S(1)} %get-tuple-element.94), channel_id=1, source_target_pairs={{0,3},{1,2},{2,1},{3,0},{4,7},{5,6},{6,5},{7,4},{8,11},{9,10},{10,... | collective-permute-start | bytes 393224 | tf_op jit(solution)/shard_map/ppermute | solution.py:357
  61.5 9.7 %collective-permute-start.21 = (bf16[128,1024]{1,0:T(8,128)(2,1)S(1)}, bf16[128,1024]{1,0:T(8,128)(2,1)S(1)}, u32[]{:S(2)}, u32[]{:S(2)}) collective-permute-start(bf16[128,1024]{1,0:T(8,128)(2,1)S(1)} %get-tuple-element.89.refs_1_), channel_id=1, source_target_pairs={{0,4},{1,5},{2,6},{3,7},{4,0},{5,1},{6,2},{7,3},{8,12},{9,13},{10,... | collective-permute-start | bytes 786440 | tf_op jit(solution)/shard_map/ppermute | solution.py:357
  64.1 12.7 %collective-permute-start.23 = (bf16[128,1024]{1,0:T(8,128)(2,1)S(1)}, bf16[128,1024]{1,0:T(8,128)(2,1)S(1)}, u32[]{:S(2)}, u32[]{:S(2)}) collective-permute-start(bf16[128,1024]{1,0:T(8,128)(2,1)S(1)} %get-tuple-element.90.refs_4_), channel_id=1, source_target_pairs={{0,4},{1,5},{2,6},{3,7},{4,0},{5,1},{6,2},{7,3},{8,12},{9,13},{10,... | collective-permute-start | bytes 786440 | tf_op jit(solution)/shard_map/ppermute | solution.py:357
  67.1 15.3 %collective-permute-start.28 = (bf16[128,1024]{1,0:T(8,128)(2,1)S(1)}, bf16[128,1024]{1,0:T(8,128)(2,1)S(1)}, u32[]{:S(2)}, u32[]{:S(2)}) collective-permute-start(bf16[128,1024]{1,0:T(8,128)(2,1)S(1)} %get-tuple-element.95.refs_7_), channel_id=1, source_target_pairs={{0,4},{1,5},{2,6},{3,7},{4,0},{5,1},{6,2},{7,3},{8,12},{9,13},{10,... | collective-permute-start | bytes 786440 | tf_op jit(solution)/shard_map/ppermute | solution.py:357
  69.7 18.3 %collective-permute-start.30 = (bf16[128,1024]{1,0:T(8,128)(2,1)S(1)}, bf16[128,1024]{1,0:T(8,128)(2,1)S(1)}, u32[]{:S(2)}, u32[]{:S(2)}) collective-permute-start(bf16[128,1024]{1,0:T(8,128)(2,1)S(1)} %get-tuple-element.96.refs_10_), channel_id=1, source_target_pairs={{0,4},{1,5},{2,6},{3,7},{4,0},{5,1},{6,2},{7,3},{8,12},{9,13},{10,... | collective-permute-start | bytes 786440 | tf_op jit(solution)/shard_map/ppermute | solution.py:357
  71.2 18.1 %collective-permute-start.22 = (bf16[128,1024]{1,0:T(8,128)(2,1)S(1)}, bf16[128,1024]{1,0:T(8,128)(2,1)S(1)}, u32[]{:S(2)}, u32[]{:S(2)}) collective-permute-start(bf16[128,1024]{1,0:T(8,128)(2,1)S(1)} %collective-permute-done.21.refs_0_), channel_id=1, source_target_pairs={{0,8},{1,9},{2,10},{3,11},{4,28},{5,29},{6,30},{7,31},{8,16},{9,17... | collective-permute-start | bytes 786440 | tf_op jit(solution)/shard_map/ppermute | solution.py:357
  76.8 12.5 %collective-permute-start.24 = (bf16[128,1024]{1,0:T(8,128)(2,1)S(1)}, bf16[128,1024]{1,0:T(8,128)(2,1)S(1)}, u32[]{:S(2)}, u32[]{:S(2)}) collective-permute-start(bf16[128,1024]{1,0:T(8,128)(2,1)S(1)} %collective-permute-done.23.refs_3_), channel_id=1, source_target_pairs={{0,8},{1,9},{2,10},{3,11},{4,28},{5,29},{6,30},{7,31},{8,16},{9,17... | collective-permute-start | bytes 786440 | tf_op jit(solution)/shard_map/ppermute | solution.py:357
  82.4 10.2 %collective-permute-start.29 = (bf16[128,1024]{1,0:T(8,128)(2,1)S(1)}, bf16[128,1024]{1,0:T(8,128)(2,1)S(1)}, u32[]{:S(2)}, u32[]{:S(2)}) collective-permute-start(bf16[128,1024]{1,0:T(8,128)(2,1)S(1)} %collective-permute-done.28.refs_6_), channel_id=1, source_target_pairs={{0,8},{1,9},{2,10},{3,11},{4,28},{5,29},{6,30},{7,31},{8,16},{9,17... | collective-permute-start | bytes 786440 | tf_op jit(solution)/shard_map/ppermute | solution.py:357
  88.0 10.2 %collective-permute-start.31 = (bf16[128,1024]{1,0:T(8,128)(2,1)S(1)}, bf16[128,1024]{1,0:T(8,128)(2,1)S(1)}, u32[]{:S(2)}, u32[]{:S(2)}) collective-permute-start(bf16[128,1024]{1,0:T(8,128)(2,1)S(1)} %collective-permute-done.30.refs_9_), channel_id=1, source_target_pairs={{0,8},{1,9},{2,10},{3,11},{4,28},{5,29},{6,30},{7,31},{8,16},{9,17... | collective-permute-start | bytes 786440 | tf_op jit(solution)/shard_map/ppermute | solution.py:357
  99.9 4.5 %collective-permute-start.32 = (s16[528,128]{1,0:T(8,128)(2,1)S(1)}, s16[528,128]{1,0:T(8,128)(2,1)S(1)}, u32[]{:S(2)}, u32[]{:S(2)}) collective-permute-start(s16[528,128]{1,0:T(8,128)(2,1)S(1)} %get-tuple-element.98), channel_id=1, source_target_pairs={{0,1},{1,0},{2,3},{3,2},{4,5},{5,4},{6,7},{7,6},{8,9},{9,8},{10,11... | collective-permute-start | bytes 405512 | tf_op jit(solution)/shard_map/ppermute | solution.py:357
  100.0 6.5 %collective-permute-start.33 = (s16[528,128]{1,0:T(8,128)(2,1)S(1)}, s16[528,128]{1,0:T(8,128)(2,1)S(1)}, u32[]{:S(2)}, u32[]{:S(2)}) collective-permute-start(s16[528,128]{1,0:T(8,128)(2,1)S(1)} %get-tuple-element.99), channel_id=1, source_target_pairs={{0,2},{1,3},{2,0},{3,1},{4,6},{5,7},{6,4},{7,5},{8,10},{9,11},{10,... | collective-permute-start | bytes 405512 | tf_op jit(solution)/shard_map/ppermute | solution.py:357
  100.8 7.6 %collective-permute-start.34 = (s16[528,128]{1,0:T(8,128)(2,1)S(1)}, s16[528,128]{1,0:T(8,128)(2,1)S(1)}, u32[]{:S(2)}, u32[]{:S(2)}) collective-permute-start(s16[528,128]{1,0:T(8,128)(2,1)S(1)} %get-tuple-element.100), channel_id=1, source_target_pairs={{0,3},{1,2},{2,1},{3,0},{4,7},{5,6},{6,5},{7,4},{8,11},{9,10},{10,... | collective-permute-start | bytes 405512 | tf_op jit(solution)/shard_map/ppermute | solution.py:357
  103.3 8.6 %collective-permute-start.38 = (s16[528,128]{1,0:T(8,128)(2,1)S(1)}, s16[528,128]{1,0:T(8,128)(2,1)S(1)}, u32[]{:S(2)}, u32[]{:S(2)}) collective-permute-start(s16[528,128]{1,0:T(8,128)(2,1)S(1)} %get-tuple-element.108), channel_id=1, source_target_pairs={{0,1},{1,0},{2,3},{3,2},{4,5},{5,4},{6,7},{7,6},{8,9},{9,8},{10,11... | collective-permute-start | bytes 405512 | tf_op jit(solution)/shard_map/ppermute | solution.py:357
  103.7 8.9 %collective-permute-start.39 = (s16[528,128]{1,0:T(8,128)(2,1)S(1)}, s16[528,128]{1,0:T(8,128)(2,1)S(1)}, u32[]{:S(2)}, u32[]{:S(2)}) collective-permute-start(s16[528,128]{1,0:T(8,128)(2,1)S(1)} %get-tuple-element.109), channel_id=1, source_target_pairs={{0,2},{1,3},{2,0},{3,1},{4,6},{5,7},{6,4},{7,5},{8,10},{9,11},{10,... | collective-permute-start | bytes 405512 | tf_op jit(solution)/shard_map/ppermute | solution.py:357
  104.4 9.8 %collective-permute-start.40 = (s16[528,128]{1,0:T(8,128)(2,1)S(1)}, s16[528,128]{1,0:T(8,128)(2,1)S(1)}, u32[]{:S(2)}, u32[]{:S(2)}) collective-permute-start(s16[528,128]{1,0:T(8,128)(2,1)S(1)} %get-tuple-element.110), channel_id=1, source_target_pairs={{0,3},{1,2},{2,1},{3,0},{4,7},{5,6},{6,5},{7,4},{8,11},{9,10},{10,... | collective-permute-start | bytes 405512 | tf_op jit(solution)/shard_map/ppermute | solution.py:357
  110.3 7.3 %collective-permute-start.35 = (s16[528,128]{1,0:T(8,128)(2,1)S(1)}, s16[528,128]{1,0:T(8,128)(2,1)S(1)}, u32[]{:S(2)}, u32[]{:S(2)}) collective-permute-start(s16[528,128]{1,0:T(8,128)(2,1)S(1)} %get-tuple-element.102), channel_id=1, source_target_pairs={{0,1},{1,0},{2,3},{3,2},{4,5},{5,4},{6,7},{7,6},{8,9},{9,8},{10,11... | collective-permute-start | bytes 405512 | tf_op jit(solution)/shard_map/ppermute | solution.py:357
  111.1 7.2 %collective-permute-start.36 = (s16[528,128]{1,0:T(8,128)(2,1)S(1)}, s16[528,128]{1,0:T(8,128)(2,1)S(1)}, u32[]{:S(2)}, u32[]{:S(2)}) collective-permute-start(s16[528,128]{1,0:T(8,128)(2,1)S(1)} %get-tuple-element.103), channel_id=1, source_target_pairs={{0,2},{1,3},{2,0},{3,1},{4,6},{5,7},{6,4},{7,5},{8,10},{9,11},{10,... | collective-permute-start | bytes 405512 | tf_op jit(solution)/shard_map/ppermute | solution.py:357
  111.9 8.1 %collective-permute-start.37 = (s16[528,128]{1,0:T(8,128)(2,1)S(1)}, s16[528,128]{1,0:T(8,128)(2,1)S(1)}, u32[]{:S(2)}, u32[]{:S(2)}) collective-permute-start(s16[528,128]{1,0:T(8,128)(2,1)S(1)} %get-tuple-element.104), channel_id=1, source_target_pairs={{0,3},{1,2},{2,1},{3,0},{4,7},{5,6},{6,5},{7,4},{8,11},{9,10},{10,... | collective-permute-start | bytes 405512 | tf_op jit(solution)/shard_map/ppermute | solution.py:357
  116.1 3.9 %collective-permute-start.41 = (s16[528,128]{1,0:T(8,128)(2,1)S(1)}, s16[528,128]{1,0:T(8,128)(2,1)S(1)}, u32[]{:S(2)}, u32[]{:S(2)}) collective-permute-start(s16[528,128]{1,0:T(8,128)(2,1)S(1)} %get-tuple-element.112), channel_id=1, source_target_pairs={{0,1},{1,0},{2,3},{3,2},{4,5},{5,4},{6,7},{7,6},{8,9},{9,8},{10,11... | collective-permute-start | bytes 405512 | tf_op jit(solution)/shard_map/ppermute | solution.py:357
  116.9 6.9 %collective-permute-start.42 = (s16[528,128]{1,0:T(8,128)(2,1)S(1)}, s16[528,128]{1,0:T(8,128)(2,1)S(1)}, u32[]{:S(2)}, u32[]{:S(2)}) collective-permute-start(s16[528,128]{1,0:T(8,128)(2,1)S(1)} %get-tuple-element.113), channel_id=1, source_target_pairs={{0,2},{1,3},{2,0},{3,1},{4,6},{5,7},{6,4},{7,5},{8,10},{9,11},{10,... | collective-permute-start | bytes 405512 | tf_op jit(solution)/shard_map/ppermute | solution.py:357
  117.7 8.1 %collective-permute-start.43 = (s16[528,128]{1,0:T(8,128)(2,1)S(1)}, s16[528,128]{1,0:T(8,128)(2,1)S(1)}, u32[]{:S(2)}, u32[]{:S(2)}) collective-permute-start(s16[528,128]{1,0:T(8,128)(2,1)S(1)} %get-tuple-element.114), channel_id=1, source_target_pairs={{0,3},{1,2},{2,1},{3,0},{4,7},{5,6},{6,5},{7,4},{8,11},{9,10},{10,... | collective-permute-start | bytes 405512 | tf_op jit(solution)/shard_map/ppermute | solution.py:357
  (2 other events, 3.2 us)
